TPU v7x, 32 devices: a whole 2x2x4 slice. The times are simulated.
32 devices in a mesh: pipe: 4 (over y, x), dp: 8 (over z, core).
Axes of the slice: x: 2, y: 2, z: 4, core: 2. Of those that a mesh axis runs over, the one named last changes fastest.
Arguments:
- block_input: bfloat16 [4, 784, 2048], P(None, 'dp'), may hold values from -20 to 20
- proj_weight: bfloat16 [4, 2048, 512], P('pipe'), may hold values from -0.125 to 0.125
- spatial_weight: bfloat16 [4, 4608, 256], P('pipe'), may hold values from -0.09375 to 0.09375
- norm_gain: float32 [2, 3072], replicated, may hold values from 0.1 to 1.9
- norm_shift: float32 [2, 3072], replicated, may hold values from -1.5 to 1.5
- output_grad: bfloat16 [4, 784, 2048], P(None, 'dp'), may hold values from -6 to 6
- image_ids: int32 [4, 16], P(None, 'dp'), may hold values from 0 to 63
Outputs:
- block_output: bfloat16 [4, 784, 2048], P(None, 'dp', 'pipe')
- input_grad: bfloat16 [4, 784, 2048], P(None, 'dp', 'pipe')
- proj_grad: float32 [4, 2048, 512], P('pipe')
- spatial_grad: float32 [4, 4608, 256], P('pipe')
- gain_grad: float32 [2, 3072], P(None, 'pipe')
- shift_grad: float32 [2, 3072], P(None, 'pipe')
- memory_bank: float32 [64, 2048], P('dp', 'pipe')
All inputs are finite; a program needn't handle non-finite values.
Results may differ from a plain program's by a relative error of at most 0.019.
Values may be sent and summed in bfloat16 or wider, within the bound.
A program may use at most 256 MiB of HBM per device.

v0:
```python
import jax
import jax.numpy as jnp
from jax import lax
from jax.sharding import PartitionSpec as P

SIDE = 7
BANK_DEV = 8


EPS = 1e-05


def passed_along(x, axis, by):
    count = lax.axis_size(axis)
    pairs = [(i, i + by) for i in range(count) if 0 <= i + by < count]
    return lax.ppermute(x, axis, pairs)


def smooth(values):
    return jax.nn.gelu(values, approximate=True)


def smooth_back(values, upstream):
    return jax.vjp(smooth, values)[1](upstream)[0]


def unfold_taps(hidden):
    row_count, channels = hidden.shape
    images = row_count // (SIDE * SIDE)
    image_grid = hidden.reshape(images, SIDE, SIDE, channels)
    padded = jnp.pad(image_grid, ((0, 0), (1, 1), (1, 1), (0, 0)))
    tap_list = [
        padded[:, row_off : row_off + SIDE, col_off : col_off + SIDE, :]
        for row_off in range(3)
        for col_off in range(3)
    ]
    return jnp.stack(tap_list, axis=3).reshape(row_count, 9 * channels)


def fold_taps(columns, channels):
    row_count = columns.shape[0]
    images = row_count // (SIDE * SIDE)
    split_taps = columns.reshape(images, SIDE, SIDE, 9, channels)
    summed = jnp.zeros((images, SIDE + 2, SIDE + 2, channels), jnp.float32)
    for position in range(9):
        row_off = position // 3
        col_off = position % 3
        summed = summed + jnp.pad(
            split_taps[:, :, :, position, :],
            ((0, 0), (row_off, 2 - row_off), (col_off, 2 - col_off), (0, 0)),
        )
    return summed[:, 1 : SIDE + 1, 1 : SIDE + 1, :].reshape(row_count, channels)


def norm_stats(values):
    row_total = values.shape[0] * lax.axis_size("dp")
    totals = lax.psum((jnp.sum(values, axis=0), jnp.sum(values * values, axis=0)), "dp")
    average = totals[0] / row_total
    return (average, lax.rsqrt(totals[1] / row_total - average * average + EPS))


def norm_back(upstream, normed, inverse, scale_part):
    row_total = upstream.shape[0] * lax.axis_size("dp")
    totals = lax.psum((jnp.sum(upstream, axis=0), jnp.sum(upstream * normed, axis=0)), "dp")
    grad_in = (
        scale_part * inverse * (upstream - totals[0] / row_total - normed * (totals[1] / row_total))
    )
    return (grad_in, totals[1], totals[0])


def contract_rows(left, right):
    return lax.dot_general(
        left, right, (((0,), (0,)), ((), ())), preferred_element_type=jnp.float32
    )


def contract_cols(left, right):
    return lax.dot_general(
        left, right, (((1,), (1,)), ((), ())), preferred_element_type=jnp.float32
    )


def front_pass(block_in, w_reduce, w_spatial, scale_seg, offset_seg, stored):
    middle = w_reduce.shape[1]
    half_width = w_spatial.shape[1]
    pre_one = jnp.dot(block_in, w_reduce, preferred_element_type=jnp.float32)
    if stored is None:
        avg_one, inv_one = norm_stats(pre_one)
    else:
        avg_one, inv_one = (stored[0, :middle], stored[1, :middle])
    normed_one = (pre_one - avg_one) * inv_one
    act_one = normed_one * scale_seg[:middle] + offset_seg[:middle]
    hidden_one = smooth(act_one).astype(jnp.bfloat16)
    columns = unfold_taps(hidden_one)
    pre_two = jnp.dot(columns, w_spatial, preferred_element_type=jnp.float32)
    if stored is None:
        avg_two, inv_two = norm_stats(pre_two)
    else:
        avg_two, inv_two = (
            stored[0, middle : middle + half_width],
            stored[1, middle : middle + half_width],
        )
    normed_two = (pre_two - avg_two) * inv_two
    act_two = (
        normed_two * scale_seg[middle : middle + half_width]
        + offset_seg[middle : middle + half_width]
    )
    hidden_two = smooth(act_two).astype(jnp.bfloat16)
    return (
        hidden_one,
        columns,
        normed_one,
        act_one,
        inv_one,
        avg_one,
        normed_two,
        act_two,
        inv_two,
        avg_two,
        hidden_two,
    )


def back_pass(block_in, mid_in, w_expand, w_spatial, scale_seg, offset_seg, stored):
    middle = w_expand.shape[1]
    half_width = w_spatial.shape[1]
    hidden_one = mid_in[:, :middle]
    hidden_front = mid_in[:, middle:]
    columns = unfold_taps(hidden_one)
    pre_two = jnp.dot(columns, w_spatial, preferred_element_type=jnp.float32)
    if stored is None:
        avg_two, inv_two = norm_stats(pre_two)
    else:
        avg_two, inv_two = (stored[0, :half_width], stored[1, :half_width])
    normed_two = (pre_two - avg_two) * inv_two
    act_two = normed_two * scale_seg[:half_width] + offset_seg[:half_width]
    hidden_back = smooth(act_two).astype(jnp.bfloat16)
    hidden_two = jnp.concatenate([hidden_front, hidden_back], axis=1)
    pre_three = contract_cols(hidden_two, w_expand)
    if stored is None:
        avg_three, inv_three = norm_stats(pre_three)
    else:
        avg_three, inv_three = (stored[0, half_width:], stored[1, half_width:])
    normed_three = (pre_three - avg_three) * inv_three
    act_three = normed_three * scale_seg[half_width:] + offset_seg[half_width:]
    pre_out = act_three + block_in.astype(jnp.float32)
    return (
        columns,
        normed_two,
        act_two,
        inv_two,
        avg_two,
        hidden_two,
        normed_three,
        inv_three,
        avg_three,
        pre_out,
    )


def store(stacked, value, slot_index, active):
    previous = lax.dynamic_index_in_dim(stacked, slot_index, 0, keepdims=False)
    return lax.dynamic_update_index_in_dim(
        stacked, jnp.where(active, value, previous), slot_index, 0
    )


def on_device(
    block_input, proj_weight, spatial_weight, norm_gain, norm_shift, output_grad, image_ids
):
    phases = lax.axis_size("pipe")
    phase_index = lax.axis_index("pipe")
    is_back = phase_index % 2 == 1
    block_id = phase_index // 2
    w_local = proj_weight[0]
    w_spatial = spatial_weight[0]
    channels, middle = w_local.shape
    half_width = w_spatial.shape[1]
    seg_width = half_width + channels
    mid_width = middle + half_width
    norm_width = norm_gain.shape[1]
    seg_start = jnp.where(is_back, middle + half_width, 0).astype(jnp.int32)
    scale_row = lax.dynamic_index_in_dim(norm_gain, block_id, 0, keepdims=False)
    offset_row = lax.dynamic_index_in_dim(norm_shift, block_id, 0, keepdims=False)
    scale_seg = lax.dynamic_slice_in_dim(scale_row, seg_start, seg_width)
    offset_seg = lax.dynamic_slice_in_dim(offset_row, seg_start, seg_width)
    micro_count = block_input.shape[0]
    row_count = block_input.shape[1]
    filler = jnp.zeros((seg_width - mid_width,), jnp.float32)

    def front_forward(block_in):
        pieces = front_pass(block_in, w_local, w_spatial, scale_seg, offset_seg, None)
        stored = jnp.stack(
            [
                jnp.concatenate([pieces[5], pieces[9], filler]),
                jnp.concatenate([pieces[4], pieces[8], filler]),
            ]
        )
        send_mid = jnp.concatenate([pieces[0], pieces[10]], axis=1)
        return (block_in, send_mid, stored, jnp.zeros((row_count, channels), jnp.float32))

    def back_forward(block_in, mid_in):
        pieces = back_pass(block_in, mid_in, w_local, w_spatial, scale_seg, offset_seg, None)
        stored = jnp.stack(
            [jnp.concatenate([pieces[4], pieces[8]]), jnp.concatenate([pieces[3], pieces[7]])]
        )
        result = smooth(pieces[9])
        return (
            result.astype(jnp.bfloat16),
            jnp.zeros((row_count, mid_width), jnp.bfloat16),
            stored,
            result,
        )

    def front_backward(block_in, stored, resid_grad, mid_grad):
        pieces = front_pass(block_in, w_local, w_spatial, scale_seg, offset_seg, stored)
        (
            hidden_one,
            columns,
            normed_one,
            act_one,
            inv_one,
            avg_one,
            normed_two,
            act_two,
            inv_two,
            avg_two,
            hidden_two,
        ) = pieces
        grad_two = smooth_back(act_two, mid_grad[:, middle:])
        pre_grad_two, scale_two, offset_two = norm_back(
            grad_two, normed_two, inv_two, scale_seg[middle : middle + half_width]
        )
        low_two = pre_grad_two.astype(jnp.bfloat16)
        term_spatial = contract_rows(columns, low_two)
        hidden_grad = fold_taps(contract_cols(low_two, w_spatial), middle) + mid_grad[:, :middle]
        grad_one = smooth_back(act_one, hidden_grad)
        pre_grad_one, scale_one, offset_one = norm_back(
            grad_one, normed_one, inv_one, scale_seg[:middle]
        )
        low_one = pre_grad_one.astype(jnp.bfloat16)
        term_reduce = contract_rows(block_in, low_one)
        input_part = contract_cols(low_one, w_local) + resid_grad
        return (
            input_part,
            jnp.zeros((row_count, mid_width), jnp.float32),
            term_reduce,
            term_spatial,
            jnp.concatenate([scale_one, scale_two, filler]),
            jnp.concatenate([offset_one, offset_two, filler]),
        )

    def back_backward(block_in, mid_in, stored, out_grad):
        pieces = back_pass(block_in, mid_in, w_local, w_spatial, scale_seg, offset_seg, stored)
        (
            columns,
            normed_two,
            act_two,
            inv_two,
            avg_two,
            hidden_two,
            normed_three,
            inv_three,
            avg_three,
            pre_out,
        ) = pieces
        grad_out = smooth_back(pre_out, out_grad)
        pre_grad_three, scale_three, offset_three = norm_back(
            grad_out, normed_three, inv_three, scale_seg[half_width:]
        )
        low_three = pre_grad_three.astype(jnp.bfloat16)
        term_reduce = contract_rows(low_three, hidden_two)
        hidden_grad = jnp.dot(low_three, w_local, preferred_element_type=jnp.float32)
        grad_back = smooth_back(act_two, hidden_grad[:, half_width:])
        pre_grad_two, scale_two, offset_two = norm_back(
            grad_back, normed_two, inv_two, scale_seg[:half_width]
        )
        low_two = pre_grad_two.astype(jnp.bfloat16)
        term_spatial = contract_rows(columns, low_two)
        front_hidden = fold_taps(contract_cols(low_two, w_spatial), middle)
        send_mid = jnp.concatenate([front_hidden, hidden_grad[:, :half_width]], axis=1)
        return (
            grad_out,
            send_mid,
            term_reduce,
            term_spatial,
            jnp.concatenate([scale_two, scale_three]),
            jnp.concatenate([offset_two, offset_three]),
        )

    saved_act = jnp.zeros((micro_count, row_count, channels), jnp.bfloat16)
    saved_mid = jnp.zeros((micro_count, row_count, mid_width), jnp.bfloat16)
    saved_stats = jnp.zeros((micro_count, 2, seg_width), jnp.float32)
    final_out = jnp.zeros((micro_count, row_count, channels), jnp.float32)
    incoming_act = jnp.zeros((row_count, channels), jnp.bfloat16)
    incoming_mid = jnp.zeros((row_count, mid_width), jnp.bfloat16)
    tick_count = micro_count + phases - 1
    for tick_index in range(tick_count):
        micro_index = tick_index - phase_index
        active = (micro_index >= 0) & (micro_index < micro_count)
        slot_index = jnp.clip(micro_index, 0, micro_count - 1)
        from_input = lax.dynamic_index_in_dim(block_input, slot_index, 0, keepdims=False)
        block_in = jnp.where(phase_index == 0, from_input, incoming_act)
        mid_in = incoming_mid
        send_act, send_mid, stats_now, result = lax.cond(
            is_back, lambda: back_forward(block_in, mid_in), lambda: front_forward(block_in)
        )
        saved_act = store(saved_act, block_in, slot_index, active)
        saved_mid = store(saved_mid, mid_in, slot_index, active)
        saved_stats = store(saved_stats, stats_now, slot_index, active)
        final_out = store(final_out, result, slot_index, active)
        if tick_index + 1 < tick_count:
            incoming_act, incoming_mid = passed_along((send_act, send_mid), "pipe", 1)
    pending_reduce = jnp.zeros((channels, middle), jnp.float32)
    pending_spatial = jnp.zeros((9 * middle, half_width), jnp.float32)
    grad_scale = jnp.zeros((seg_width,), jnp.float32)
    grad_offset = jnp.zeros((seg_width,), jnp.float32)
    input_grads = jnp.zeros((micro_count, row_count, channels), jnp.float32)
    back_act = jnp.zeros((row_count, channels), jnp.float32)
    back_mid = jnp.zeros((row_count, mid_width), jnp.float32)
    for tick_index in range(tick_count):
        micro_index = tick_index - (phases - 1 - phase_index)
        active = (micro_index >= 0) & (micro_index < micro_count)
        slot_index = jnp.clip(micro_index, 0, micro_count - 1)
        from_output = lax.dynamic_index_in_dim(output_grad, slot_index, 0, keepdims=False).astype(
            jnp.float32
        )
        upstream = jnp.where(phase_index == phases - 1, from_output, back_act)
        mid_grad = back_mid
        block_in = lax.dynamic_index_in_dim(saved_act, slot_index, 0, keepdims=False)
        mid_in = lax.dynamic_index_in_dim(saved_mid, slot_index, 0, keepdims=False)
        stored = lax.dynamic_index_in_dim(saved_stats, slot_index, 0, keepdims=False)
        section_out = lax.cond(
            is_back,
            lambda: back_backward(block_in, mid_in, stored, upstream),
            lambda: front_backward(block_in, stored, upstream, mid_grad),
        )
        send_act, send_mid, term_reduce, term_spatial, term_scale, term_offset = section_out
        pending_reduce = pending_reduce + jnp.where(active, term_reduce, 0.0)
        pending_spatial = pending_spatial + jnp.where(active, term_spatial, 0.0)
        grad_scale = grad_scale + jnp.where(active, term_scale, 0.0)
        grad_offset = grad_offset + jnp.where(active, term_offset, 0.0)
        input_grads = store(input_grads, send_act, slot_index, active)
        if tick_index + 1 < tick_count:
            back_act, back_mid = (
                passed_along(send_act.astype(jnp.bfloat16), "pipe", -1).astype(send_act.dtype),
                passed_along(send_mid.astype(jnp.bfloat16), "pipe", -1).astype(send_mid.dtype),
            )
    summed_grads = lax.psum((pending_reduce, pending_spatial), "dp")
    total_reduce = summed_grads[0]
    total_spatial = summed_grads[1]
    zero_index = jnp.int32(0)
    scale_term = lax.dynamic_update_slice(
        jnp.zeros((1, 2, norm_width), jnp.float32),
        grad_scale[None, None, :],
        (zero_index, block_id, seg_start),
    )
    offset_term = lax.dynamic_update_slice(
        jnp.zeros((1, 2, norm_width), jnp.float32),
        grad_offset[None, None, :],
        (zero_index, block_id, seg_start),
    )
    out_term = jnp.where(phase_index == phases - 1, final_out, 0.0)
    input_term = jnp.where(phase_index == 0, input_grads, 0.0)
    results = (
        lax.psum_scatter(
            out_term.astype(jnp.bfloat16), "pipe", scatter_dimension=2, tiled=True
        ).astype(jnp.float32),
        lax.psum_scatter(
            input_term.astype(jnp.bfloat16), "pipe", scatter_dimension=2, tiled=True
        ).astype(jnp.float32),
        lax.psum_scatter(
            scale_term.astype(jnp.bfloat16), "pipe", scatter_dimension=2, tiled=True
        ).astype(jnp.float32),
        lax.psum_scatter(
            offset_term.astype(jnp.bfloat16), "pipe", scatter_dimension=2, tiled=True
        ).astype(jnp.float32),
    )
    out_quarter = results[0].astype(jnp.bfloat16)
    input_quarter = results[1].astype(jnp.bfloat16)
    gain_part = results[2][0]
    shift_part = results[3][0]
    images_here = row_count // (SIDE * SIDE)
    pooled = jnp.mean(
        out_quarter.astype(jnp.float32).reshape(
            micro_count, images_here, SIDE * SIDE, out_quarter.shape[2]
        ),
        axis=2,
    )
    bank_total = BANK_DEV * lax.axis_size("dp")
    selector = (
        image_ids[:, :, None] == jnp.arange(bank_total, dtype=jnp.int32)[None, None, :]
    ).astype(jnp.float32)
    bank_term = jnp.einsum("mib,mic->bc", selector, pooled, precision=lax.Precision.HIGHEST)
    memory_bank = lax.psum_scatter(bank_term, "dp", scatter_dimension=0, tiled=True)
    return (
        out_quarter,
        input_quarter,
        total_reduce[None],
        total_spatial[None],
        gain_part,
        shift_part,
        memory_bank,
    )


def solution(mesh):
    return jax.shard_map(
        on_device,
        mesh=mesh,
        in_specs=(
            P(None, "dp", None),
            P("pipe", None, None),
            P("pipe", None, None),
            P(),
            P(),
            P(None, "dp", None),
            P(None, "dp"),
        ),
        out_specs=(
            P(None, "dp", "pipe"),
            P(None, "dp", "pipe"),
            P("pipe", None, None),
            P("pipe", None, None),
            P(None, "pipe"),
            P(None, "pipe"),
            P("dp", "pipe"),
        ),
        check_vma=False,
    )
```

profile of v0, /device:TPU:0, one launch (start us, length us, event | category | flops | bytes accessed | tf_op | source)
XLA Modules:
  0.0 1728.0 jit_solution(14917273324480996407)
XLA Ops:
  7.3 12.6 constant_dynamic-slice_fusion.39
  22.5 45.8 %conditional.14 = (bf16[98,2048]{1,0:T(8,128)(2,1)S(1)}, bf16[98,768]{1,0:T(8,128)(2,1)}, f32[2,2304]{1,0:T(2,128)S(1)}, bf16[98,2048]{1,0:T(8,128)(2,1)S(1)}) conditional(s32[]{:T(128)} %convert_element_type.549, (bf16[98,2048]{1,0:T(8,128)(2,1)S(1)}, bf16[2048,512]{1,0:T(8,128)(2,1)}, f32[2304]{0:T(1024)}, f32[2304]{0:T(1024)S(1)}, ...), branch_computations={%region_0.9_spmd, %region_9.18_spmd} | conditional | flops 440766720 | bytes 15788812 | solution.py:305
  25.2 18.0 %all-reduce.147 = (f32[512]{0:T(512)S(1)}, f32[512]{0:T(512)S(1)}) all-reduce(f32[512]{0:T(512)S(1)} %get-tuple-element.1315, f32[512]{0:T(512)S(1)} %get-tuple-element.1314), channel_id=1, replica_groups=mesh['pipe'=4,'dp'=8] {'dp'}, use_global_device_ids=true, to_apply=%region_4.4 | all-reduce | flops 1024 | bytes 8192 | tf_op jit(solution)/shard_map/cond/branch_0_fun/psum | solution.py:57
  53.6 13.6 all-reduce.146
  68.3 27.9 %collective-permute-start = (bf16[98,2048]{1,0:T(8,128)(2,1)S(1)}, bf16[98,2048]{1,0:T(8,128)(2,1)}, u32[]{:S(2)}, u32[]{:S(2)}) collective-permute-start(bf16[98,2048]{1,0:T(8,128)(2,1)S(1)} %get-tuple-element.678), channel_id=1, source_target_pairs={{0,8},{8,16},{16,24},{1,9},{9,17},{17,25},{2,10},{10,18},{18,26},{... | collective-permute-start | bytes 1204232 | tf_op jit(solution)/shard_map/ppermute | solution.py:16
  102.3 12.9 constant_dynamic-slice_fusion.1
  123.1 52.2 %conditional.15 = (bf16[98,2048]{1,0:T(8,128)(2,1)S(1)}, bf16[98,768]{1,0:T(8,128)(2,1)}, f32[2,2304]{1,0:T(2,128)S(1)}, bf16[98,2048]{1,0:T(8,128)(2,1)S(1)}) conditional(s32[]{:T(128)} %convert_element_type.549, (bf16[98,2048]{1,0:T(8,128)(2,1)S(1)}, bf16[2048,512]{1,0:T(8,128)(2,1)}, f32[2304]{0:T(1024)}, f32[2304]{0:T(1024)S(1)}, ...), branch_computations={%region_18.27_spmd, %region_27.36_spmd} | conditional | flops 440967424 | bytes 17586212 | solution.py:305
  126.5 13.6 all-reduce.151
  158.3 14.3 all-reduce.150
  175.3 16.9 collective-permute-start.2
  205.0 54.2 %conditional.16 = (bf16[98,2048]{1,0:T(8,128)(2,1)S(1)}, bf16[98,768]{1,0:T(8,128)(2,1)}, f32[2,2304]{1,0:T(2,128)S(1)}, bf16[98,2048]{1,0:T(8,128)(2,1)S(1)}) conditional(s32[]{:T(128)} %convert_element_type.549, (bf16[98,2048]{1,0:T(8,128)(2,1)S(1)}, bf16[2048,512]{1,0:T(8,128)(2,1)}, f32[2304]{0:T(1024)}, f32[2304]{0:T(1024)S(1)}, ...), branch_computations={%region_36.45_spmd, %region_45.54_spmd} | conditional | flops 440967424 | bytes 17586212 | solution.py:305
  208.5 15.8 all-reduce.155
  242.5 14.3 all-reduce.154
  259.3 16.6 collective-permute-start.4
  288.7 54.7 %conditional.17 = (bf16[98,2048]{1,0:T(8,128)(2,1)S(1)}, bf16[98,768]{1,0:T(8,128)(2,1)}, f32[2,2304]{1,0:T(2,128)S(1)}, bf16[98,2048]{1,0:T(8,128)(2,1)S(1)}) conditional(s32[]{:T(128)} %convert_element_type.549, (bf16[98,2048]{1,0:T(8,128)(2,1)S(1)}, bf16[2048,512]{1,0:T(8,128)(2,1)}, f32[2304]{0:T(1024)}, f32[2304]{0:T(1024)S(1)}, ...), branch_computations={%region_54.63_spmd, %region_63.72_spmd} | conditional | flops 440967424 | bytes 17586212 | solution.py:305
  292.2 16.3 all-reduce.159
  326.6 14.3 all-reduce.158
  343.5 25.1 %collective-permute-start.6 = (bf16[98,2048]{1,0:T(8,128)(2,1)S(1)}, bf16[98,2048]{1,0:T(8,128)(2,1)S(1)}, u32[]{:S(2)}, u32[]{:S(2)}) collective-permute-start(bf16[98,2048]{1,0:T(8,128)(2,1)S(1)} %get-tuple-element.687), channel_id=1, source_target_pairs={{0,8},{8,16},{16,24},{1,9},{9,17},{17,25},{2,10},{10,18},{18,26},{... | collective-permute-start | bytes 1204232 | tf_op jit(solution)/shard_map/ppermute | solution.py:16
  381.5 54.3 %conditional.18 = (bf16[98,2048]{1,0:T(8,128)(2,1)S(1)}, bf16[98,768]{1,0:T(8,128)(2,1)}, f32[2,2304]{1,0:T(2,128)S(1)}, bf16[98,2048]{1,0:T(8,128)(2,1)S(1)}) conditional(s32[]{:T(128)} %convert_element_type.549, (bf16[98,2048]{1,0:T(8,128)(2,1)S(1)}, bf16[2048,512]{1,0:T(8,128)(2,1)}, f32[2304]{0:T(1024)}, f32[2304]{0:T(1024)S(1)}, ...), branch_computations={%region_72.81_spmd, %region_81.90_spmd} | conditional | flops 440967424 | bytes 17586212 | solution.py:305
  384.9 15.9 all-reduce.163
  418.9 14.3 all-reduce.162
  435.9 16.7 collective-permute-start.8
  465.5 54.2 %conditional.19 = (bf16[98,2048]{1,0:T(8,128)(2,1)S(1)}, bf16[98,768]{1,0:T(8,128)(2,1)}, f32[2,2304]{1,0:T(2,128)S(1)}, bf16[98,2048]{1,0:T(8,128)(2,1)S(1)}) conditional(s32[]{:T(128)} %convert_element_type.549, (bf16[98,2048]{1,0:T(8,128)(2,1)S(1)}, bf16[2048,512]{1,0:T(8,128)(2,1)}, f32[2304]{0:T(1024)}, f32[2304]{0:T(1024)S(1)}, ...), branch_computations={%region_90.99_spmd, %region_99.108_spmd} | conditional | flops 440967424 | bytes 17586212 | solution.py:305
  468.9 15.8 all-reduce.167
  502.9 14.3 all-reduce.166
  519.7 16.5 collective-permute-start.10
  547.3 45.6 %conditional.20 = (f32[2,2304]{1,0:T(2,128)}, bf16[98,2048]{1,0:T(8,128)(2,1)}) conditional(s32[]{:T(128)} %convert_element_type.549, (bf16[98,2048]{1,0:T(8,128)(2,1)S(1)}, bf16[2048,512]{1,0:T(8,128)(2,1)}, f32[2304]{0:T(1024)}, f32[2304]{0:T(1024)S(1)}, bf16[4608,256]{1,0:T(8,128)(2,1)S(1)}) %tuple.708, (bf16[98,768]{1,0:T(8,128)(2,1)}, ...), branch_computations={%region_108.117_spmd, %region_117.126_spmd} | conditional | flops 440967424 | bytes 16632850 | solution.py:305
  550.7 16.1 all-reduce.171
  577.4 13.6 all-reduce.170
  600.6 85.4 %conditional.21 = (f32[98,2048]{1,0:T(8,128)}, bf16[98,768]{1,0:T(8,128)(2,1)}, f32[2048,512]{1,0:T(8,128)}, f32[4608,256]{1,0:T(8,128)}, f32[2304]{0:T(1024)S(1)}, /*index=5*/f32[2304]{0:T(1024)S(1)}) conditional(s32[]{:T(128)} %convert_element_type.549, (f32[2304]{0:T(1024)}, f32[2,2304]{1,0:T(2,128)S(1)}, bf16[98,2048]{1,0:T(8,128)(2,1)S(1)}, ...), branch_computations={%region_127.136_spmd, %region_136.145_spmd} | conditional | flops 1319103744 | bytes 61417260 | solution.py:333
  616.8 14.4 all-reduce.175
  653.7 14.3 all-reduce.174
  691.3 42.4 %collective-permute-done.12 = bf16[98,768]{1,0:T(8,128)(2,1)S(1)} collective-permute-done((bf16[98,768]{1,0:T(8,128)(2,1)}, bf16[98,768]{1,0:T(8,128)(2,1)S(1)}, u32[]{:S(2)}, u32[]{:S(2)}) %collective-permute-start.12) | collective-permute-done | bytes 150560 | tf_op jit(solution)/shard_map/ppermute | solution.py:16
  743.8 84.9 %conditional.22 = (f32[98,2048]{1,0:T(8,128)}, bf16[98,768]{1,0:T(8,128)(2,1)}, f32[2048,512]{1,0:T(8,128)}, f32[4608,256]{1,0:T(8,128)S(1)}, f32[2304]{0:T(1024)S(1)}, /*index=5*/f32[2304]{0:T(1024)S(1)}) conditional(s32[]{:T(128)} %convert_element_type.549, (f32[2304]{0:T(1024)}, f32[2,2304]{1,0:T(2,128)S(1)}, f32[98,768]{1,0:T(8,128)}, ...), branch_computations={%region_145.154_spmd, %region_154.163_spmd} | conditional | flops 1319103744 | bytes 59811596 | solution.py:333
  762.0 14.3 all-reduce.179
  798.8 14.3 all-reduce.178
  836.7 11.5 collective-permute-done.14
  858.2 87.1 %conditional.23 = (f32[98,2048]{1,0:T(8,128)}, bf16[98,768]{1,0:T(8,128)(2,1)}, f32[2048,512]{1,0:T(8,128)}, f32[4608,256]{1,0:T(8,128)}, f32[2304]{0:T(1024)S(1)}, /*index=5*/f32[2304]{0:T(1024)S(1)}) conditional(s32[]{:T(128)} %convert_element_type.549, (f32[2304]{0:T(1024)}, f32[2,2304]{1,0:T(2,128)S(1)}, f32[98,768]{1,0:T(8,128)}, ...), branch_computations={%region_163.172_spmd, %region_172.181_spmd} | conditional | flops 1319103744 | bytes 59811596 | solution.py:333
  876.2 14.3 all-reduce.183
  913.2 14.3 all-reduce.182
  953.0 11.8 collective-permute-done.16
  974.8 87.1 %conditional.24 = (f32[98,2048]{1,0:T(8,128)}, bf16[98,768]{1,0:T(8,128)(2,1)}, f32[2048,512]{1,0:T(8,128)}, f32[4608,256]{1,0:T(8,128)}, f32[2304]{0:T(1024)S(1)}, /*index=5*/f32[2304]{0:T(1024)S(1)}) conditional(s32[]{:T(128)} %convert_element_type.549, (f32[2304]{0:T(1024)}, f32[2,2304]{1,0:T(2,128)S(1)}, f32[98,768]{1,0:T(8,128)}, ...), branch_computations={%region_181.190_spmd, %region_190.199_spmd} | conditional | flops 1319103744 | bytes 59811596 | solution.py:333
  992.8 14.2 all-reduce.187
  1029.7 14.3 all-reduce.186
  1069.8 11.5 collective-permute-done.18
  1091.3 85.3 %conditional.25 = (f32[98,2048]{1,0:T(8,128)}, bf16[98,768]{1,0:T(8,128)(2,1)}, f32[2048,512]{1,0:T(8,128)}, f32[4608,256]{1,0:T(8,128)S(1)}, f32[2304]{0:T(1024)S(1)}, /*index=5*/f32[2304]{0:T(1024)S(1)}) conditional(s32[]{:T(128)} %convert_element_type.549, (f32[2304]{0:T(1024)}, f32[2,2304]{1,0:T(2,128)S(1)}, f32[98,768]{1,0:T(8,128)}, ...), branch_computations={%region_199.208_spmd, %region_208.217_spmd} | conditional | flops 1319103744 | bytes 59811596 | solution.py:333
  1109.5 14.2 all-reduce.191
  1131.3 8.7 fusion.1049
  1146.5 14.3 all-reduce.190
  1184.7 11.4 collective-permute-done.20
  1206.1 85.1 %conditional.26 = (f32[98,2048]{1,0:T(8,128)}, bf16[98,768]{1,0:T(8,128)(2,1)}, f32[2048,512]{1,0:T(8,128)}, f32[4608,256]{1,0:T(8,128)S(1)}, f32[2304]{0:T(1024)S(1)}, /*index=5*/f32[2304]{0:T(1024)S(1)}) conditional(s32[]{:T(128)} %convert_element_type.549, (f32[2304]{0:T(1024)}, f32[2,2304]{1,0:T(2,128)S(1)}, f32[98,768]{1,0:T(8,128)}, ...), branch_computations={%region_217.226_spmd, %region_226.235_spmd} | conditional | flops 1319103744 | bytes 59811596 | solution.py:333
  1224.1 14.3 all-reduce.195
  1261.1 14.3 all-reduce.194
  1299.3 11.3 collective-permute-done.22
  1320.7 78.2 %conditional.27 = (f32[98,2048]{1,0:T(8,128)}, f32[4608,256]{1,0:T(8,128)}, f32[2304]{0:T(1024)S(1)}, f32[2304]{0:T(1024)S(1)}, f32[2048,512]{1,0:T(8,128)}) conditional(s32[]{:T(128)} %convert_element_type.549, (f32[2304]{0:T(1024)}, f32[2,2304]{1,0:T(2,128)S(1)}, f32[98,768]{1,0:T(8,128)}, bf16[98,2048]{1,0:T(8,128)(2,1)}, ...), branch_computations={%region_235.244_spmd, %region_244.253_spmd} | conditional | flops 1313810176 | bytes 63363396 | solution.py:333
  1338.0 14.3 all-reduce.199
  1359.8 8.7 fusion.1061
  1370.6 13.6 all-reduce.198
  1414.5 10.0 add_bitcast_fusion
  1427.3 9.2 add_bitcast_fusion.1
  1438.0 21.4 %reduce-scatter.18.cloned.1.call-done = bf16[768,2]{1,0:T(8,128)(2,1)} async-done(((bf16[3072,2]{1,0:T(8,128)(2,1)}), bf16[768,2]{1,0:T(8,128)(2,1)}) %reduce-scatter.18.cloned.1.call-update) | async-done | bytes 3088
  1462.9 31.2 %reduce-scatter.12.cloned.1.call-done = bf16[4,98,512]{2,1,0:T(8,128)(2,1)} async-done(((bf16[4,98,2048]{2,1,0:T(8,128)(2,1)}), bf16[4,98,512]{2,1,0:T(8,128)(2,1)}) %reduce-scatter.12.cloned.1.call-update) | async-done | bytes 401424 | tf_op jit(solution)/shard_map/reduce_scatter | solution.py:369
  1496.1 30.8 %reduce-scatter.14.cloned.1.call-done = f32[8,512]{1,0:T(8,128)} async-done(((f32[64,512]{1,0:T(8,128)}), f32[8,512]{1,0:T(8,128)}) %reduce-scatter.14.cloned.1.call-update) | async-done | bytes 16400 | tf_op jit(solution)/shard_map/reduce_scatter | solution.py:395
  1526.9 187.0 %all-reduce.205.cloned.1.call-done = (f32[1,2048,512]{2,1,0:T(8,128)}, f32[1,4608,256]{2,1,0:T(8,128)}) async-done(((f32[1,2048,512]{2,1,0:T(8,128)}, f32[1,4608,256]{2,1,0:T(8,128)}), (f32[1,2048,512]{2,1,0:T(8,128)}, f32[1,4608,256]{2,1,0:T(8,128)})) %all-reduce.205.cloned.1.call-update) | async-done | bytes 8912912 | tf_op jit(solution)/shard_map/psum | solution.py:349
  (1077 shorter events, 743.8 us)
Async XLA Ops:
  7.2 1417.4 %reduce-scatter.10.cloned.1.call-start = ((), (), s32[]{:S(2)}) async-start(), calls=%async_computation.5 | async-start | bytes 2129920 | tf_op jit(solution)/shard_map/reduce_scatter | solution.py:366
  68.3 50.6 %collective-permute-start = (bf16[98,2048]{1,0:T(8,128)(2,1)S(1)}, bf16[98,2048]{1,0:T(8,128)(2,1)}, u32[]{:S(2)}, u32[]{:S(2)}) collective-permute-start(bf16[98,2048]{1,0:T(8,128)(2,1)S(1)} %get-tuple-element.678), channel_id=1, source_target_pairs={{0,8},{8,16},{16,24},{1,9},{9,17},{17,25},{2,10},{10,18},{18,26},{... | collective-permute-start | bytes 1204232 | tf_op jit(solution)/shard_map/ppermute | solution.py:16
  96.2 21.0 %collective-permute-start.1 = (bf16[98,768]{1,0:T(8,128)(2,1)}, bf16[98,768]{1,0:T(8,128)(2,1)}, u32[]{:S(2)}, u32[]{:S(2)}) collective-permute-start(bf16[98,768]{1,0:T(8,128)(2,1)} %get-tuple-element.679), channel_id=1, source_target_pairs={{0,8},{8,16},{16,24},{1,9},{9,17},{17,25},{2,10},{10,18},{18,26},{... | collective-permute-start | bytes 451592 | tf_op jit(solution)/shard_map/ppermute | solution.py:16
  175.3 26.0 %copy-start.87 = (bf16[1,98,768]{2,1,0:T(8,128)(2,1)S(1)}, bf16[1,98,768]{2,1,0:T(8,128)(2,1)}, u32[]{:S(2)}) copy-start(bf16[1,98,768]{2,1,0:T(8,128)(2,1)} %constant_dynamic-slice_fusion.22) | copy-start | bytes 451588
  175.3 26.8 %copy-start.45 = (bf16[1,98,2048]{2,0,1:T(2,128)(2,1)S(1)}, bf16[1,98,2048]{2,0,1:T(2,128)(2,1)}, u32[]{:S(2)}) copy-start(bf16[1,98,2048]{2,0,1:T(2,128)(2,1)} %get-tuple-element.2043) | copy-start | bytes 1204228
  175.3 26.7 %copy-start.52 = (bf16[1,98,2048]{2,1,0:T(8,128)(2,1)S(1)}, bf16[1,98,2048]{2,1,0:T(8,128)(2,1)}, u32[]{:S(2)}) copy-start(bf16[1,98,2048]{2,1,0:T(8,128)(2,1)} %constant_dynamic-slice_fusion.29) | copy-start | bytes 1204228
  175.3 26.7 %collective-permute-start.2 = (bf16[98,2048]{1,0:T(8,128)(2,1)S(1)}, bf16[98,2048]{1,0:T(8,128)(2,1)S(1)}, u32[]{:S(2)}, u32[]{:S(2)}) collective-permute-start(bf16[98,2048]{1,0:T(8,128)(2,1)S(1)} %get-tuple-element.681), channel_id=1, source_target_pairs={{0,8},{8,16},{16,24},{1,9},{9,17},{17,25},{2,10},{10,18},{18,26},{... | collective-permute-start | bytes 1204232 | tf_op jit(solution)/shard_map/ppermute | solution.py:16
  192.2 9.1 collective-permute-start.3
  259.3 25.8 %copy-start.88 = (bf16[1,98,768]{2,1,0:T(8,128)(2,1)S(1)}, bf16[1,98,768]{2,1,0:T(8,128)(2,1)}, u32[]{:S(2)}) copy-start(bf16[1,98,768]{2,1,0:T(8,128)(2,1)} %constant_dynamic-slice_fusion.21) | copy-start | bytes 451588
  259.3 26.5 %copy-start.44 = (bf16[1,98,2048]{2,0,1:T(2,128)(2,1)S(1)}, bf16[1,98,2048]{2,0,1:T(2,128)(2,1)}, u32[]{:S(2)}) copy-start(bf16[1,98,2048]{2,0,1:T(2,128)(2,1)} %get-tuple-element.2042) | copy-start | bytes 1204228
  259.3 26.5 %copy-start.53 = (bf16[1,98,2048]{2,1,0:T(8,128)(2,1)S(1)}, bf16[1,98,2048]{2,1,0:T(8,128)(2,1)}, u32[]{:S(2)}) copy-start(bf16[1,98,2048]{2,1,0:T(8,128)(2,1)} %constant_dynamic-slice_fusion.28) | copy-start | bytes 1204228
  259.3 26.5 %collective-permute-start.4 = (bf16[98,2048]{1,0:T(8,128)(2,1)S(1)}, bf16[98,2048]{1,0:T(8,128)(2,1)S(1)}, u32[]{:S(2)}, u32[]{:S(2)}) collective-permute-start(bf16[98,2048]{1,0:T(8,128)(2,1)S(1)} %get-tuple-element.684), channel_id=1, source_target_pairs={{0,8},{8,16},{16,24},{1,9},{9,17},{17,25},{2,10},{10,18},{18,26},{... | collective-permute-start | bytes 1204232 | tf_op jit(solution)/shard_map/ppermute | solution.py:16
  275.9 9.1 collective-permute-start.5
  343.5 25.1 %copy-start.66 = (bf16[98,2048]{1,0:T(8,128)(2,1)}, bf16[98,2048]{1,0:T(8,128)(2,1)S(1)}, u32[]{:S(2)}) copy-start(bf16[98,2048]{1,0:T(8,128)(2,1)S(1)} %get-tuple-element.686) | copy-start | bytes 1204228
  343.5 34.2 %copy-start.89 = (bf16[1,98,768]{2,1,0:T(8,128)(2,1)S(1)}, bf16[1,98,768]{2,1,0:T(8,128)(2,1)}, u32[]{:S(2)}) copy-start(bf16[1,98,768]{2,1,0:T(8,128)(2,1)} %constant_dynamic-slice_fusion.20) | copy-start | bytes 451588
  343.5 35.0 %copy-start.43 = (bf16[1,98,2048]{2,0,1:T(2,128)(2,1)S(1)}, bf16[1,98,2048]{2,0,1:T(2,128)(2,1)}, u32[]{:S(2)}) copy-start(bf16[1,98,2048]{2,0,1:T(2,128)(2,1)} %get-tuple-element.2041) | copy-start | bytes 1204228
  343.5 35.0 %copy-start.54 = (bf16[1,98,2048]{2,1,0:T(8,128)(2,1)S(1)}, bf16[1,98,2048]{2,1,0:T(8,128)(2,1)}, u32[]{:S(2)}) copy-start(bf16[1,98,2048]{2,1,0:T(8,128)(2,1)} %constant_dynamic-slice_fusion.27) | copy-start | bytes 1204228
  343.5 35.0 %collective-permute-start.6 = (bf16[98,2048]{1,0:T(8,128)(2,1)S(1)}, bf16[98,2048]{1,0:T(8,128)(2,1)S(1)}, u32[]{:S(2)}, u32[]{:S(2)}) collective-permute-start(bf16[98,2048]{1,0:T(8,128)(2,1)S(1)} %get-tuple-element.687), channel_id=1, source_target_pairs={{0,8},{8,16},{16,24},{1,9},{9,17},{17,25},{2,10},{10,18},{18,26},{... | collective-permute-start | bytes 1204232 | tf_op jit(solution)/shard_map/ppermute | solution.py:16
  368.6 9.1 collective-permute-start.7
  435.9 25.8 %copy-start.90 = (bf16[1,98,768]{2,1,0:T(8,128)(2,1)S(1)}, bf16[1,98,768]{2,1,0:T(8,128)(2,1)}, u32[]{:S(2)}) copy-start(bf16[1,98,768]{2,1,0:T(8,128)(2,1)} %constant_dynamic-slice_fusion.19) | copy-start | bytes 451588
  435.9 26.6 %copy-start.42 = (bf16[1,98,2048]{2,0,1:T(2,128)(2,1)S(1)}, bf16[1,98,2048]{2,0,1:T(2,128)(2,1)}, u32[]{:S(2)}) copy-start(bf16[1,98,2048]{2,0,1:T(2,128)(2,1)} %get-tuple-element.2040) | copy-start | bytes 1204228
  435.9 26.6 %copy-start.55 = (bf16[1,98,2048]{2,1,0:T(8,128)(2,1)S(1)}, bf16[1,98,2048]{2,1,0:T(8,128)(2,1)}, u32[]{:S(2)}) copy-start(bf16[1,98,2048]{2,1,0:T(8,128)(2,1)} %constant_dynamic-slice_fusion.26) | copy-start | bytes 1204228
  435.9 26.5 %collective-permute-start.8 = (bf16[98,2048]{1,0:T(8,128)(2,1)S(1)}, bf16[98,2048]{1,0:T(8,128)(2,1)S(1)}, u32[]{:S(2)}, u32[]{:S(2)}) collective-permute-start(bf16[98,2048]{1,0:T(8,128)(2,1)S(1)} %get-tuple-element.690), channel_id=1, source_target_pairs={{0,8},{8,16},{16,24},{1,9},{9,17},{17,25},{2,10},{10,18},{18,26},{... | collective-permute-start | bytes 1204232 | tf_op jit(solution)/shard_map/ppermute | solution.py:16
  452.6 9.1 collective-permute-start.9
  519.7 25.7 %copy-start.91 = (bf16[1,98,768]{2,1,0:T(8,128)(2,1)S(1)}, bf16[1,98,768]{2,1,0:T(8,128)(2,1)}, u32[]{:S(2)}) copy-start(bf16[1,98,768]{2,1,0:T(8,128)(2,1)} %constant_dynamic-slice_fusion.18) | copy-start | bytes 451588
  519.7 26.4 %copy-start.41 = (bf16[1,98,2048]{2,0,1:T(2,128)(2,1)S(1)}, bf16[1,98,2048]{2,0,1:T(2,128)(2,1)}, u32[]{:S(2)}) copy-start(bf16[1,98,2048]{2,0,1:T(2,128)(2,1)} %get-tuple-element.2039) | copy-start | bytes 1204228
  519.7 26.4 %copy-start.56 = (bf16[1,98,2048]{2,1,0:T(8,128)(2,1)S(1)}, bf16[1,98,2048]{2,1,0:T(8,128)(2,1)}, u32[]{:S(2)}) copy-start(bf16[1,98,2048]{2,1,0:T(8,128)(2,1)} %constant_dynamic-slice_fusion.25) | copy-start | bytes 1204228
  519.7 25.7 %collective-permute-start.10 = (bf16[98,2048]{1,0:T(8,128)(2,1)S(1)}, bf16[98,2048]{1,0:T(8,128)(2,1)S(1)}, u32[]{:S(2)}, u32[]{:S(2)}) collective-permute-start(bf16[98,2048]{1,0:T(8,128)(2,1)S(1)} %get-tuple-element.693), channel_id=1, source_target_pairs={{0,8},{8,16},{16,24},{1,9},{9,17},{17,25},{2,10},{10,18},{18,26},{... | collective-permute-start | bytes 1204232 | tf_op jit(solution)/shard_map/ppermute | solution.py:16
  536.3 9.1 collective-permute-start.11
  545.5 55.1 %copy-start.9 = (bf16[4,98,768]{2,1,0:T(8,128)(2,1)}, bf16[4,98,768]{2,1,0:T(8,128)(2,1)S(1)}, u32[]{:S(2)}) copy-start(bf16[4,98,768]{2,1,0:T(8,128)(2,1)S(1)} %bitcast_dynamic-update-slice_fusion.20) | copy-start | bytes 1806340
  596.4 840.1 %reduce-scatter.16.cloned.1.call-start = ((), (), s32[]{:S(2)}) async-start(), calls=%async_computation.8 | async-start | bytes 983040
  686.0 47.7 %collective-permute-start.12 = (bf16[98,768]{1,0:T(8,128)(2,1)}, bf16[98,768]{1,0:T(8,128)(2,1)S(1)}, u32[]{:S(2)}, u32[]{:S(2)}) collective-permute-start(bf16[98,768]{1,0:T(8,128)(2,1)} %get-tuple-element.704), channel_id=1, source_target_pairs={{8,0},{16,8},{24,16},{9,1},{17,9},{25,17},{10,2},{18,10},{26,18},{... | collective-permute-start | bytes 451592 | tf_op jit(solution)/shard_map/ppermute | solution.py:16
  688.7 53.9 %copy-start.51 = (bf16[1,98,2048]{2,0,1:T(2,128)(2,1)S(1)}, bf16[1,98,2048]{2,0,1:T(2,128)(2,1)}, u32[]{:S(2)}) copy-start(bf16[1,98,2048]{2,0,1:T(2,128)(2,1)} %get-tuple-element.2037) | copy-start | bytes 1204228
  688.7 53.9 %collective-permute-start.13 = (bf16[98,2048]{1,0:T(8,128)(2,1)S(1)}, bf16[98,2048]{1,0:T(8,128)(2,1)S(1)}, u32[]{:S(2)}, u32[]{:S(2)}) collective-permute-start(bf16[98,2048]{1,0:T(8,128)(2,1)S(1)} %convert_element_type.556), channel_id=1, source_target_pairs={{8,0},{16,8},{24,16},{9,1},{17,9},{25,17},{10,2},{18,10},{26,18},{... | collective-permute-start | bytes 1204232 | tf_op jit(solution)/shard_map/ppermute | solution.py:16
  690.3 53.5 %copy-start.138 = (f32[2,2304]{1,0:T(2,128)S(1)}, f32[2,2304]{1,0:T(2,128)}, u32[]{:S(2)}) copy-start(f32[2,2304]{1,0:T(2,128)} %get-tuple-element.2053) | copy-start | bytes 55300
  690.4 53.4 %copy-start.5 = (bf16[4,98,2048]{2,1,0:T(8,128)(2,1)}, bf16[4,98,2048]{2,1,0:T(8,128)(2,1)S(1)}, u32[]{:S(2)}) copy-start(bf16[4,98,2048]{2,1,0:T(8,128)(2,1)S(1)} %bitcast_dynamic-update-slice_fusion.6) | copy-start | bytes 4816900
  828.8 29.4 %copy-start.1 = (f32[4608,256]{1,0:T(8,128)}, f32[4608,256]{1,0:T(8,128)S(1)}, u32[]{:S(2)}) copy-start(f32[4608,256]{1,0:T(8,128)S(1)} %get-tuple-element.724) | copy-start | bytes 14155780
  828.8 19.3 %collective-permute-start.14 = (bf16[98,768]{1,0:T(8,128)(2,1)}, bf16[98,768]{1,0:T(8,128)(2,1)S(1)}, u32[]{:S(2)}, u32[]{:S(2)}) collective-permute-start(bf16[98,768]{1,0:T(8,128)(2,1)} %get-tuple-element.706), channel_id=1, source_target_pairs={{8,0},{16,8},{24,16},{9,1},{17,9},{25,17},{10,2},{18,10},{26,18},{... | collective-permute-start | bytes 451592 | tf_op jit(solution)/shard_map/ppermute | solution.py:16
  830.1 26.8 %copy-start.50 = (bf16[1,98,2048]{2,0,1:T(2,128)(2,1)S(1)}, bf16[1,98,2048]{2,0,1:T(2,128)(2,1)}, u32[]{:S(2)}) copy-start(bf16[1,98,2048]{2,0,1:T(2,128)(2,1)} %get-tuple-element.2036) | copy-start | bytes 1204228
  831.6 25.3 %collective-permute-start.15 = (bf16[98,2048]{1,0:T(8,128)(2,1)S(1)}, bf16[98,2048]{1,0:T(8,128)(2,1)S(1)}, u32[]{:S(2)}, u32[]{:S(2)}) collective-permute-start(bf16[98,2048]{1,0:T(8,128)(2,1)S(1)} %convert_element_type.562), channel_id=1, source_target_pairs={{8,0},{16,8},{24,16},{9,1},{17,9},{25,17},{10,2},{18,10},{26,18},{... | collective-permute-start | bytes 1204232 | tf_op jit(solution)/shard_map/ppermute | solution.py:16
  834.8 23.4 %copy-start.137 = (f32[2,2304]{1,0:T(2,128)S(1)}, f32[2,2304]{1,0:T(2,128)}, u32[]{:S(2)}) copy-start(f32[2,2304]{1,0:T(2,128)} %get-tuple-element.2052) | copy-start | bytes 55300
  945.4 19.4 %collective-permute-start.16 = (bf16[98,768]{1,0:T(8,128)(2,1)}, bf16[98,768]{1,0:T(8,128)(2,1)S(1)}, u32[]{:S(2)}, u32[]{:S(2)}) collective-permute-start(bf16[98,768]{1,0:T(8,128)(2,1)} %get-tuple-element.708), channel_id=1, source_target_pairs={{8,0},{16,8},{24,16},{9,1},{17,9},{25,17},{10,2},{18,10},{26,18},{... | collective-permute-start | bytes 451592 | tf_op jit(solution)/shard_map/ppermute | solution.py:16
  946.7 26.9 %copy-start.49 = (bf16[1,98,2048]{2,0,1:T(2,128)(2,1)S(1)}, bf16[1,98,2048]{2,0,1:T(2,128)(2,1)}, u32[]{:S(2)}) copy-start(bf16[1,98,2048]{2,0,1:T(2,128)(2,1)} %get-tuple-element.2035) | copy-start | bytes 1204228
  948.0 25.6 %collective-permute-start.17 = (bf16[98,2048]{1,0:T(8,128)(2,1)S(1)}, bf16[98,2048]{1,0:T(8,128)(2,1)S(1)}, u32[]{:S(2)}, u32[]{:S(2)}) collective-permute-start(bf16[98,2048]{1,0:T(8,128)(2,1)S(1)} %convert_element_type.568), channel_id=1, source_target_pairs={{8,0},{16,8},{24,16},{9,1},{17,9},{25,17},{10,2},{18,10},{26,18},{... | collective-permute-start | bytes 1204232 | tf_op jit(solution)/shard_map/ppermute | solution.py:16
  951.2 23.7 %copy-start.136 = (f32[2,2304]{1,0:T(2,128)S(1)}, f32[2,2304]{1,0:T(2,128)}, u32[]{:S(2)}) copy-start(f32[2,2304]{1,0:T(2,128)} %get-tuple-element.2051) | copy-start | bytes 55300
  1061.9 19.3 %collective-permute-start.18 = (bf16[98,768]{1,0:T(8,128)(2,1)}, bf16[98,768]{1,0:T(8,128)(2,1)S(1)}, u32[]{:S(2)}, u32[]{:S(2)}) collective-permute-start(bf16[98,768]{1,0:T(8,128)(2,1)} %get-tuple-element.710), channel_id=1, source_target_pairs={{8,0},{16,8},{24,16},{9,1},{17,9},{25,17},{10,2},{18,10},{26,18},{... | collective-permute-start | bytes 451592 | tf_op jit(solution)/shard_map/ppermute | solution.py:16
  1063.3 26.8 %copy-start.48 = (bf16[1,98,2048]{2,0,1:T(2,128)(2,1)S(1)}, bf16[1,98,2048]{2,0,1:T(2,128)(2,1)}, u32[]{:S(2)}) copy-start(bf16[1,98,2048]{2,0,1:T(2,128)(2,1)} %get-tuple-element.2034) | copy-start | bytes 1204228
  1064.6 25.5 %collective-permute-start.19 = (bf16[98,2048]{1,0:T(8,128)(2,1)S(1)}, bf16[98,2048]{1,0:T(8,128)(2,1)S(1)}, u32[]{:S(2)}, u32[]{:S(2)}) collective-permute-start(bf16[98,2048]{1,0:T(8,128)(2,1)S(1)} %convert_element_type.574), channel_id=1, source_target_pairs={{8,0},{16,8},{24,16},{9,1},{17,9},{25,17},{10,2},{18,10},{26,18},{... | collective-permute-start | bytes 1204232 | tf_op jit(solution)/shard_map/ppermute | solution.py:16
  1068.0 23.3 %copy-start.135 = (f32[2,2304]{1,0:T(2,128)S(1)}, f32[2,2304]{1,0:T(2,128)}, u32[]{:S(2)}) copy-start(f32[2,2304]{1,0:T(2,128)} %get-tuple-element.2050) | copy-start | bytes 55300
  1176.6 29.5 %copy-start.2 = (f32[4608,256]{1,0:T(8,128)}, f32[4608,256]{1,0:T(8,128)S(1)}, u32[]{:S(2)}) copy-start(f32[4608,256]{1,0:T(8,128)S(1)} %get-tuple-element.727) | copy-start | bytes 14155780
  1176.6 19.5 %collective-permute-start.20 = (bf16[98,768]{1,0:T(8,128)(2,1)}, bf16[98,768]{1,0:T(8,128)(2,1)S(1)}, u32[]{:S(2)}, u32[]{:S(2)}) collective-permute-start(bf16[98,768]{1,0:T(8,128)(2,1)} %get-tuple-element.712), channel_id=1, source_target_pairs={{8,0},{16,8},{24,16},{9,1},{17,9},{25,17},{10,2},{18,10},{26,18},{... | collective-permute-start | bytes 451592 | tf_op jit(solution)/shard_map/ppermute | solution.py:16
  1177.9 27.0 %copy-start.47 = (bf16[1,98,2048]{2,0,1:T(2,128)(2,1)S(1)}, bf16[1,98,2048]{2,0,1:T(2,128)(2,1)}, u32[]{:S(2)}) copy-start(bf16[1,98,2048]{2,0,1:T(2,128)(2,1)} %get-tuple-element.2033) | copy-start | bytes 1204228
  1179.4 25.5 %collective-permute-start.21 = (bf16[98,2048]{1,0:T(8,128)(2,1)S(1)}, bf16[98,2048]{1,0:T(8,128)(2,1)S(1)}, u32[]{:S(2)}, u32[]{:S(2)}) collective-permute-start(bf16[98,2048]{1,0:T(8,128)(2,1)S(1)} %convert_element_type.580), channel_id=1, source_target_pairs={{8,0},{16,8},{24,16},{9,1},{17,9},{25,17},{10,2},{18,10},{26,18},{... | collective-permute-start | bytes 1204232 | tf_op jit(solution)/shard_map/ppermute | solution.py:16
  1182.8 23.3 %copy-start.134 = (f32[2,2304]{1,0:T(2,128)S(1)}, f32[2,2304]{1,0:T(2,128)}, u32[]{:S(2)}) copy-start(f32[2,2304]{1,0:T(2,128)} %get-tuple-element.2049) | copy-start | bytes 55300
  1291.2 29.5 %copy-start.3 = (f32[4608,256]{1,0:T(8,128)}, f32[4608,256]{1,0:T(8,128)S(1)}, u32[]{:S(2)}) copy-start(f32[4608,256]{1,0:T(8,128)S(1)} %get-tuple-element.728) | copy-start | bytes 14155780
  1291.3 19.4 %collective-permute-start.22 = (bf16[98,768]{1,0:T(8,128)(2,1)}, bf16[98,768]{1,0:T(8,128)(2,1)S(1)}, u32[]{:S(2)}, u32[]{:S(2)}) collective-permute-start(bf16[98,768]{1,0:T(8,128)(2,1)} %get-tuple-element.714), channel_id=1, source_target_pairs={{8,0},{16,8},{24,16},{9,1},{17,9},{25,17},{10,2},{18,10},{26,18},{... | collective-permute-start | bytes 451592 | tf_op jit(solution)/shard_map/ppermute | solution.py:16
  1292.6 26.9 %copy-start.46 = (bf16[1,98,2048]{2,0,1:T(2,128)(2,1)S(1)}, bf16[1,98,2048]{2,0,1:T(2,128)(2,1)}, u32[]{:S(2)}) copy-start(bf16[1,98,2048]{2,0,1:T(2,128)(2,1)} %get-tuple-element.2032) | copy-start | bytes 1204228
  1294.1 25.4 %collective-permute-start.23 = (bf16[98,2048]{1,0:T(8,128)(2,1)S(1)}, bf16[98,2048]{1,0:T(8,128)(2,1)S(1)}, u32[]{:S(2)}, u32[]{:S(2)}) collective-permute-start(bf16[98,2048]{1,0:T(8,128)(2,1)S(1)} %convert_element_type.586), channel_id=1, source_target_pairs={{8,0},{16,8},{24,16},{9,1},{17,9},{25,17},{10,2},{18,10},{26,18},{... | collective-permute-start | bytes 1204232 | tf_op jit(solution)/shard_map/ppermute | solution.py:16
  1297.5 23.2 %copy-start.133 = (f32[2,2304]{1,0:T(2,128)S(1)}, f32[2,2304]{1,0:T(2,128)}, u32[]{:S(2)}) copy-start(f32[2,2304]{1,0:T(2,128)} %get-tuple-element.2048) | copy-start | bytes 55300
  1406.9 52.4 %reduce-scatter.18.cloned.1.call-start = ((), (), s32[]{:S(2)}) async-start(), calls=%async_computation.9 | async-start | bytes 983040
  1412.8 81.4 %reduce-scatter.12.cloned.1.call-start = ((), (), s32[]{:S(2)}) async-start(), calls=%async_computation.6 | async-start | bytes 2129920 | tf_op jit(solution)/shard_map/reduce_scatter | solution.py:369
  1414.5 112.5 %reduce-scatter.14.cloned.1.call-start = ((), (), s32[]{:S(2)}) async-start(), calls=%async_computation.7 | async-start | bytes 147456 | tf_op jit(solution)/shard_map/reduce_scatter | solution.py:395
  1427.0 287.0 %all-reduce.205.cloned.1.call-start = ((), (), s32[]{:S(2)}) async-start(), calls=%async_computation.10 | async-start | bytes 17825792 | tf_op jit(solution)/shard_map/psum | solution.py:349
  1436.5 25.5 %copy-start.62 = (bf16[4,98,512]{2,1,0:T(8,128)(2,1)S(1)}, bf16[4,98,512]{2,1,0:T(8,128)(2,1)}, u32[]{:S(2)}) copy-start(bf16[4,98,512]{2,1,0:T(8,128)(2,1)} %reduce-scatter.10.cloned.1.call-done) | copy-start | bytes 1204228
  (140 other events, 582.0 us)
Sparse Core Ops, SparseCore 0:
  596.5 57.5 reduce-scatter.9
  1407.0 23.2 reduce-scatter.15
  1433.2 26.0 reduce-scatter.17
  1462.2 31.9 reduce-scatter.11
  1496.8 30.0 reduce-scatter.13
  1529.9 183.9 all-reduce.204
where the time goes:
time: 1750 us; the launch traced here: 1730 us
  waiting for transfers between devices  429 us (25%)
  local copies, waits for them, and re-layouts  416 us (24%)
  blocking collectives  409 us (23%)
  other arithmetic  166 us (9%)
  starting transfers between devices  147 us (8%)
  matrix products  137 us (8%)
    psum x14, blocking collectives, norm_stats(): lax.psum((jnp.sum(values, axis=0), jnp.sum(values * values, axis=0)), 'dp')  210 us
    psum x14, blocking collectives, norm_back(): lax.psum((jnp.sum(upstream, axis=0), jnp.sum(upstream * normed, axis=0)),...  199 us
    psum x1, waiting for transfers between devices, on_device(): summed_grads = lax.psum((pending_reduce, pending_spatial), 'dp')  187 us
    ppermute x24, waiting for transfers between devices, passed_along(): return lax.ppermute(x, axis, pairs)  159 us
    ppermute x24, starting transfers between devices, passed_along(): return lax.ppermute(x, axis, pairs)  147 us
    cond x346, local copies, waits for them, and re-layouts  104 us
    slice x70, local copies, waits for them, and re-layouts, fold_taps(): split_taps[:, :, :, position, :]  67 us
    another operation x42, local copies, waits for them, and re-layouts, unfold_taps(): return jnp.stack(tap_list, axis=3).reshape(row_count, 9 * channels)  43.8 us
  transfers between devices with their start and end apart: 30, of which 21 were waited for; matrix products, arithmetic and copies ran while one was open for 30% of the time, Pallas kernels for 0%

commit v1 on v0

v1 whole, which is shorter than its diff:
```python
import functools
import math
import types

import jax
import jax.numpy as jnp
from jax import lax
from jax.experimental import pallas as pl
from jax.experimental.pallas import tpu as pltpu
from jax.sharding import PartitionSpec as P

SIDE = 7
TAPS = 9
EPS = 1e-05
LANES = 128
GROUPS = 2
MESH = pl.DeviceIdType.MESH
F32 = jnp.float32
BF16 = jnp.bfloat16


def gelu_pair(v):
    c0 = math.sqrt(2.0 / math.pi)
    c1 = 0.044715
    sq = v * v
    t = jnp.tanh(c0 * v * (1.0 + c1 * sq))
    half = 0.5 + 0.5 * t
    slope = half + (0.5 * c0) * v * (1.0 - t * t) * (1.0 + (3.0 * c1) * sq)
    return v * half, slope


def dot(a, b):
    return jnp.dot(a, b, preferred_element_type=F32)


def dot_nt(a, b):
    return lax.dot_general(a, b, (((1,), (1,)), ((), ())), preferred_element_type=F32)


def dot_tn(a, b):
    return lax.dot_general(a, b, (((0,), (0,)), ((), ())), preferred_element_type=F32)


class Sizes:
    def __init__(self, mesh, block_input, proj, spatial, bank_rows):
        self.pipes = mesh.shape["pipe"]
        self.dps = mesh.shape["dp"]
        self.micro = block_input.shape[0]
        self.rows = block_input.shape[1]
        self.pad = -(-self.rows // 16) * 16
        self.ch = block_input.shape[2]
        self.mid = proj.shape[2]
        self.images = self.rows // (SIDE * SIDE)
        self.cs = self.ch // self.pipes
        self.msd = self.mid // self.pipes
        self.groups = GROUPS
        self.gm = self.micro // self.groups
        self.zs = self.dps // 2
        self.total = self.rows * self.dps
        self.bank = bank_rows
        self.deep = (self.cs // 2) % (16 * self.zs) == 0 and (TAPS * self.mid // 2) % (16 * self.zs) == 0


def scratch_list(c):
    full = (c.micro, c.pad)
    seg = (c.pipes, c.micro, c.pad, LANES)
    items = [
        ("u_all", pltpu.VMEM(full + (c.ch,), BF16)),
        ("u_seg", pltpu.VMEM((2,) + full + (c.cs,), BF16)),
        ("g_seg", pltpu.VMEM(full + (c.cs,), BF16)),
        ("p_own", pltpu.VMEM((c.ch, c.mid), BF16)),
        ("pq", pltpu.VMEM((c.pipes, c.cs, c.mid), BF16)),
        ("wf", pltpu.VMEM((2, TAPS, c.mid, LANES), BF16)),
        ("wb", pltpu.VMEM((2, TAPS, LANES, c.mid), BF16)),
        ("mask", pltpu.VMEM((TAPS, c.pad, LANES), F32)),
        ("z1", pltpu.VMEM((2,) + full + (LANES,), F32)),
        ("d1", pltpu.VMEM((2,) + full + (LANES,), F32)),
        ("z2", pltpu.VMEM((2,) + full + (LANES,), F32)),
        ("d2", pltpu.VMEM((2,) + full + (LANES,), F32)),
        ("z3", pltpu.VMEM((2,) + full + (c.cs,), F32)),
        ("d3", pltpu.VMEM((2,) + full + (c.cs,), F32)),
        ("e3", pltpu.VMEM(full + (c.cs,), F32)),
        ("t1", pltpu.VMEM(full + (LANES,), F32)),
        ("gr1", pltpu.VMEM((2, c.micro, 1, LANES), F32)),
        ("gr2", pltpu.VMEM((2, c.micro, 1, LANES), F32)),
        ("gr3", pltpu.VMEM((2, c.micro, 1, c.cs), F32)),
        ("h1", pltpu.VMEM((2,) + seg, BF16)),
        ("h2", pltpu.VMEM((2,) + seg, BF16)),
        ("da3", pltpu.VMEM((2,) + full + (c.cs,), BF16)),
        ("da2", pltpu.VMEM((2,) + seg, BF16)),
        ("da1", pltpu.VMEM((2,) + seg, BF16)),
        ("first", pltpu.VMEM(full + (LANES,), BF16)),
        ("put", pltpu.VMEM((4,) + seg, BF16)),
        ("got", pltpu.VMEM((4,) + seg, BF16)),
        ("out_seg", pltpu.VMEM(full + (c.cs,), BF16)),
        ("in_seg", pltpu.VMEM(full + (c.cs,), BF16)),
        ("ar_small", pltpu.VMEM((8, c.dps, c.micro, 2, LANES), F32)),
        ("ar_wide", pltpu.VMEM((4, c.dps, c.micro, 2, c.cs), F32)),
        ("pool", pltpu.VMEM((c.micro * c.images, 1, c.cs), F32)),
        ("bank_put", pltpu.VMEM((c.dps, c.bank, c.cs), F32)),
        ("bank_got", pltpu.VMEM((c.dps, c.bank, c.cs), F32)),
        ("norm_sum", pltpu.VMEM((c.pipes, 6, 8, LANES), F32)),
        ("gp", pltpu.VMEM((c.pipes, c.cs, c.mid), BF16)),
        ("gw", pltpu.VMEM((2, TAPS * c.mid, LANES), BF16)),
        ("ar_s", pltpu.SemaphoreType.DMA((12, c.groups))),
        ("ar_r", pltpu.SemaphoreType.DMA((12, c.groups))),
        ("ag_s", pltpu.SemaphoreType.DMA((8, c.groups))),
        ("ag_r", pltpu.SemaphoreType.DMA((8, c.groups))),
        ("rs_s", pltpu.SemaphoreType.DMA((4, c.groups))),
        ("rs_r", pltpu.SemaphoreType.DMA((4, c.groups))),
        ("w_s", pltpu.SemaphoreType.DMA((3, c.pipes))),
        ("pq_r", pltpu.SemaphoreType.DMA((c.pipes,))),
        ("wf_r", pltpu.SemaphoreType.DMA((2,))),
        ("wb_r", pltpu.SemaphoreType.DMA((2, 2))),
        ("bank_s", pltpu.SemaphoreType.DMA((1,))),
        ("bank_r", pltpu.SemaphoreType.DMA((1,))),
        ("ns_s", pltpu.SemaphoreType.DMA((1,))),
        ("ns_r", pltpu.SemaphoreType.DMA((1,))),
        ("in_r", pltpu.SemaphoreType.DMA((4,))),
        ("out_r", pltpu.SemaphoreType.DMA((6,))),
    ]
    if c.deep:
        prow, wrow = c.cs // 2, TAPS * c.mid // 2
        items += [
            ("p_sib", pltpu.VMEM((c.pipes, prow, c.mid), BF16)),
            ("w_sib", pltpu.VMEM((2, wrow, LANES), BF16)),
            ("p_z", pltpu.VMEM((c.pipes, c.zs, prow // c.zs, c.mid), BF16)),
            ("w_z", pltpu.VMEM((2, c.zs, wrow // c.zs, LANES), BF16)),
            ("p_fin", pltpu.VMEM((c.pipes, prow, c.mid), BF16)),
            ("w_fin", pltpu.VMEM((2, wrow, LANES), BF16)),
            ("p_out", pltpu.VMEM((c.ch, c.mid), BF16)),
            ("w_out", pltpu.VMEM((TAPS * c.mid, 2 * LANES), BF16)),
            ("gs", pltpu.SemaphoreType.DMA((6, 5))),
            ("gr", pltpu.SemaphoreType.DMA((6, 5))),
            ("own_s", pltpu.SemaphoreType.DMA((6,))),
            ("fin_s", pltpu.SemaphoreType.DMA((6,))),
            ("fin_r", pltpu.SemaphoreType.DMA((6,))),
        ]
    return items


def body(c, names, *refs):
    (u_hbm, go_hbm, pw_hbm, sw_hbm, gain_ref, shift_ref, ids_ref) = refs[:7]
    (bo_out, ig_out, gp_out, gw_out, ns_out, mb_out) = refs[7:13]
    s = types.SimpleNamespace(**dict(zip(names, refs[13:])))
    me_p = lax.axis_index("pipe")
    me_d = lax.axis_index("dp")
    me_x = lax.rem(me_p, 2)
    me_y = lax.div(me_p, 2)
    NP, ND, M, GM, G, R = c.pipes, c.dps, c.micro, c.gm, c.groups, c.pad
    flat = GM * R
    count = float(c.total)

    def shard(k, p):
        half = lax.div(p, 2)
        return 2 * lax.rem(p, 2) + (half if k == 0 else 1 - half)

    def pipe_peer(i):
        return lax.rem(me_p + i, NP)

    def dp_peer(i):
        return lax.rem(me_d + i, ND)

    def remote(src, dst, ss, rs, p, d):
        return pltpu.make_async_remote_copy(
            src_ref=src, dst_ref=dst, send_sem=ss, recv_sem=rs, device_id=(p, d), device_id_type=MESH
        )

    def take_recv(view, ss, rs):
        remote(view, view, ss, rs, me_p, me_d).wait_recv()

    def take_send(view, ss, rs):
        remote(view, view, ss, rs, me_p, me_d).wait_send()

    def group(g):
        return pl.ds(g * GM, GM)

    lane0 = pl.multiple_of(me_p * c.cs, LANES)
    seg_cols = pl.ds(lane0, c.cs)
    load_u = pltpu.make_async_copy(u_hbm.at[:, :, seg_cols], s.u_seg.at[0], s.in_r.at[0])
    load_g = pltpu.make_async_copy(go_hbm.at[:, :, seg_cols], s.g_seg, s.in_r.at[1])
    load_all = pltpu.make_async_copy(u_hbm, s.u_all, s.in_r.at[2])
    load_p = pltpu.make_async_copy(pw_hbm, s.p_own, s.in_r.at[3])

    @pl.when(me_p == 0)
    def _():
        load_all.start()
        load_p.start()

    load_u.start()
    load_g.start()

    barrier = pltpu.get_barrier_semaphore()
    for i in range(1, NP):
        pl.semaphore_signal(barrier, inc=1, device_id=(pipe_peer(i), me_d), device_id_type=MESH)

    @pl.loop(1, ND)
    def _(i):
        pl.semaphore_signal(barrier, inc=1, device_id=(me_p, dp_peer(i)), device_id_type=MESH)

    row = lax.broadcasted_iota(jnp.int32, (R, LANES), 0)
    image = jnp.zeros_like(row)
    for n in range(1, c.images):
        image = image + (row >= n * SIDE * SIDE).astype(jnp.int32)
    pixel = row - image * (SIDE * SIDE)
    up = jnp.zeros_like(row)
    for n in range(1, SIDE):
        up = up + (pixel >= n * SIDE).astype(jnp.int32)
    across = pixel - up * SIDE
    for t in range(TAPS):
        i, j = t // 3 - 1, t % 3 - 1
        ok = (up + i >= 0) & (up + i < SIDE) & (across + j >= 0) & (across + j < SIDE) & (row < c.rows)
        s.mask[t] = ok.astype(F32)
    s.norm_sum[...] = jnp.zeros_like(s.norm_sum)

    pl.semaphore_wait(barrier, NP - 1 + ND - 1)

    def rows_of(p):
        return pl.ds(pl.multiple_of(p * c.cs, 16), c.cs)

    def proj_send(i):
        p = pipe_peer(i)
        return remote(pw_hbm.at[rows_of(p)], s.pq.at[me_p], s.w_s.at[0, i], s.pq_r.at[me_p], p, me_d)

    def front_send():
        return remote(
            sw_hbm.at[:, :, pl.ds(LANES, LANES)], s.wf.at[me_y], s.w_s.at[1, 0], s.wf_r.at[me_y], lax.rem(me_p + 2, NP), me_d
        )

    def back_rows(p):
        sh = 2 * lax.rem(p, 2) + lax.rem(lax.div(p, 2) + me_y, 2)
        return pl.ds(pl.multiple_of(sh * LANES, LANES), LANES)

    def back_cols():
        return pl.ds(pl.multiple_of(me_x * 2 * LANES, LANES), 2 * LANES)

    def back_send(i):
        p = pipe_peer(i)
        return remote(
            sw_hbm.at[:, back_rows(p), :], s.wb.at[me_y, :, :, back_cols()], s.w_s.at[2, i], s.wb_r.at[me_y, me_x], p, me_d
        )

    pltpu.make_async_copy(pw_hbm.at[rows_of(me_p)], s.pq.at[me_p], s.pq_r.at[me_p]).start()
    pltpu.make_async_copy(sw_hbm.at[:, :, pl.ds(0, LANES)], s.wf.at[me_y], s.wf_r.at[me_y]).start()
    pltpu.make_async_copy(
        sw_hbm.at[:, back_rows(me_p), :], s.wb.at[me_y, :, :, back_cols()], s.wb_r.at[me_y, me_x]
    ).start()
    front_send().start()

    def need_proj(i):
        pltpu.make_async_copy(s.pq.at[i], s.pq.at[i], s.pq_r.at[i]).wait()

    def need_front(k):
        pltpu.make_async_copy(s.wf.at[k], s.wf.at[k], s.wf_r.at[k]).wait()

    def need_back(k):
        for e in range(2):
            view = s.wb.at[k, :, :, pl.ds(e * 2 * LANES, 2 * LANES)]
            pltpu.make_async_copy(view, view, s.wb_r.at[k, e]).wait()

    def ar_ref(idx):
        return s.ar_small.at[idx] if idx < 8 else s.ar_wide.at[idx - 8]

    def ar_send(idx, g, first, second):
        buf = ar_ref(idx)
        buf[me_d, group(g), 0:1, :] = first
        buf[me_d, group(g), 1:2, :] = second

        @pl.loop(1, ND)
        def _(i):
            view = buf.at[me_d, group(g)]
            remote(view, view, s.ar_s.at[idx, g], s.ar_r.at[idx, g], me_p, dp_peer(i)).start()

    def ar_take(idx, g):
        buf = ar_ref(idx)
        take_recv(buf.at[pl.ds(0, ND - 1), group(g)], s.ar_s.at[idx, g], s.ar_r.at[idx, g])
        tot = buf[0, group(g)]
        for d in range(1, ND):
            tot = tot + buf[d, group(g)]
        return tot[:, 0:1, :], tot[:, 1:2, :]

    def ag_send(idx, g, buf, slot):
        view = buf.at[slot, group(g)]
        for i in range(1, NP):
            remote(view, view, s.ag_s.at[idx, g], s.ag_r.at[idx, g], pipe_peer(i), me_d).start()

    def ag_take(idx, g, buf):
        take_recv(buf.at[pl.ds(0, NP - 1), group(g)], s.ag_s.at[idx, g], s.ag_r.at[idx, g])
        return jnp.concatenate([buf[j, group(g)].reshape(flat, LANES) for j in range(NP)], axis=1)

    def rs_send(idx, g, k, partial):
        for j in range(NP):
            s.put[idx, j, group(g)] = partial[:, j * LANES : (j + 1) * LANES].reshape(GM, R, LANES).astype(BF16)
        for i in range(1, NP):
            p = pipe_peer(i)
            remote(
                s.put.at[idx, shard(k, p), group(g)],
                s.got.at[idx, me_p, group(g)],
                s.rs_s.at[idx, g],
                s.rs_r.at[idx, g],
                p,
                me_d,
            ).start()

    def rs_take(idx, g, k):
        take_recv(s.got.at[idx, pl.ds(0, NP - 1), group(g)], s.rs_s.at[idx, g], s.rs_r.at[idx, g])
        tot = s.put[idx, shard(k, me_p), group(g)].astype(F32)
        for i in range(1, NP):
            tot = tot + s.got[idx, pipe_peer(i), group(g)].astype(F32)
        return tot

    def shard_cols(base, k):
        return pl.ds(pl.multiple_of(base + shard(k, me_p) * LANES, LANES), LANES)

    def norm_cols(which, k):
        if which == 1:
            return shard_cols(0, k)
        if which == 2:
            return shard_cols(c.mid, k)
        return pl.ds(pl.multiple_of(2 * c.mid + me_p * c.cs, LANES), c.cs)

    def real_rows(width):
        return lax.broadcasted_iota(jnp.int32, (GM, R, width), 1) < c.rows

    ZD = {1: (s.z1, s.d1, s.gr1), 2: (s.z2, s.d2, s.gr2), 3: (s.z3, s.d3, s.gr3)}
    FWD = {(0, 1): 0, (0, 2): 1, (1, 1): 2, (1, 2): 3, (0, 3): 8, (1, 3): 9}
    BWD = {(1, 2): 4, (1, 1): 5, (0, 2): 6, (0, 1): 7, (1, 3): 10, (0, 3): 11}

    def stats_out(k, which, g, a):
        ZD[which][0][k, group(g)] = a
        ar_send(FWD[(k, which)], g, jnp.sum(a, axis=1, keepdims=True), jnp.sum(a * a, axis=1, keepdims=True))

    def normed(k, which, g):
        z_ref, _, gr_ref = ZD[which]
        one, two = ar_take(FWD[(k, which)], g)
        mean = one / count
        inv = lax.rsqrt(two / count - mean * mean + EPS)
        z = (z_ref[k, group(g)] - mean) * inv
        z_ref[k, group(g)] = z
        gain = gain_ref[k : k + 1, norm_cols(which, k)][None]
        gr_ref[k, group(g)] = gain * inv
        return z * gain + shift_ref[k : k + 1, norm_cols(which, k)][None]

    def hidden_out(k, which, g, idx, buf):
        act, slope = gelu_pair(normed(k, which, g))
        ZD[which][1][k, group(g)] = slope
        mine = shard(k, me_p)
        buf[k, mine, group(g)] = jnp.where(real_rows(LANES), act, 0.0).astype(BF16)
        ag_send(idx, g, buf.at[k], mine)

    def back_out(k, which, g, up):
        ar_send(
            BWD[(k, which)],
            g,
            jnp.sum(up, axis=1, keepdims=True),
            jnp.sum(up * ZD[which][0][k, group(g)], axis=1, keepdims=True),
        )

    def back_in(k, which, g, up):
        z_ref, _, gr_ref = ZD[which]
        one, two = ar_take(BWD[(k, which)], g)
        chunk0 = {1: 0, 2: 1, 3: 2}[which]
        for n in range(one.shape[-1] // LANES):
            lanes = slice(n * LANES, (n + 1) * LANES)
            s.norm_sum[me_p, chunk0 + n, 2 * k : 2 * k + 1, :] += jnp.sum(two[:, :, lanes], axis=0)
            s.norm_sum[me_p, chunk0 + n, 2 * k + 1 : 2 * k + 2, :] += jnp.sum(one[:, :, lanes], axis=0)
        grad = gr_ref[k, group(g)] * (up - one / count - z_ref[k, group(g)] * (two / count))
        return jnp.where(real_rows(grad.shape[-1]), grad, 0.0).astype(BF16)

    def shifted(v, by):
        by = by % flat
        return v if by == 0 else pltpu.roll(v, by, 0)

    def tap_shift(t):
        return SIDE * (t // 3 - 1) + (t % 3 - 1)

    def masked(v, t):
        return v.reshape(GM, R, LANES) * s.mask[t][None]

    def conv(k, h):
        acc = None
        for t0 in range(0, TAPS, 2):
            taps = [t for t in (t0, t0 + 1) if t < TAPS]
            w = s.wf[k, taps[0]] if len(taps) == 1 else jnp.concatenate([s.wf[k, t] for t in taps], axis=1)
            y = dot(h, w)
            for n, t in enumerate(taps):
                part = masked(shifted(y[:, n * LANES : (n + 1) * LANES], -tap_shift(t)), t)
                acc = part if acc is None else acc + part
        return acc

    def conv_back(k, d):
        acc = None
        for t0 in range(0, TAPS, 2):
            taps = [t for t in (t0, t0 + 1) if t < TAPS]
            w = s.wb[k, taps[0]] if len(taps) == 1 else jnp.concatenate([s.wb[k, t] for t in taps], axis=0)
            y = dot_nt(d, w)
            for n, t in enumerate(taps):
                part = masked(y[:, n * LANES : (n + 1) * LANES], t).reshape(flat, LANES)
                part = shifted(part, tap_shift(t))
                acc = part if acc is None else acc + part
        return acc.reshape(GM, R, LANES)

    @pl.when(me_p == 0)
    def _():
        load_all.wait()
        load_p.wait()

        @pl.loop(0, G)
        def _(g):
            a = dot(s.u_all[group(g)].reshape(flat, c.ch), s.p_own[...])
            for j in range(NP):
                s.put[0, j, group(g)] = a[:, j * LANES : (j + 1) * LANES].reshape(GM, R, LANES).astype(BF16)
            s.first[group(g)] = s.put[0, 0, group(g)]
            for p in range(1, NP):
                remote(
                    s.put.at[0, shard(0, jnp.int32(p)), group(g)], s.first.at[group(g)], s.rs_s.at[0, g], s.rs_r.at[0, g], p, me_d
                ).start()

    for i in range(1, NP):
        proj_send(i).start()

    for k in range(2):

        @pl.loop(0, G)
        def _(g):
            if k == 0:

                @pl.when(me_p != 0)
                def _():
                    take_recv(s.first.at[group(g)], s.rs_s.at[0, g], s.rs_r.at[0, g])

                a = s.first[group(g)].astype(F32)
            else:
                a = rs_take(1, g, 1)
            stats_out(k, 1, g, a)

        @pl.loop(0, G)
        def _(g):
            hidden_out(k, 1, g, 2 * k, s.h1)

        need_front(k)

        @pl.loop(0, G)
        def _(g):
            stats_out(k, 2, g, conv(k, ag_take(2 * k, g, s.h1.at[k])))

        @pl.loop(0, G)
        def _(g):
            hidden_out(k, 2, g, 2 * k + 1, s.h2)

        need_proj(2 * k + 1)
        if k == 0:
            load_u.wait()
            for i in range(1, NP):
                back_send(i).start()

        @pl.loop(0, G)
        def _(g):
            a = dot_nt(ag_take(2 * k + 1, g, s.h2.at[k]), s.pq[2 * k + 1])
            stats_out(k, 3, g, a.reshape(GM, R, c.cs))

        if k == 0:
            need_proj(2)

            @pl.loop(0, G)
            def _(g):
                v = normed(0, 3, g) + s.u_seg[0, group(g)].astype(F32)
                act, slope = gelu_pair(v)
                s.d3[0, group(g)] = slope
                o = jnp.where(real_rows(c.cs), act, 0.0).astype(BF16)
                s.u_seg[1, group(g)] = o
                rs_send(1, g, 1, dot(o.reshape(flat, c.cs), s.pq[2]))

    load_g.wait()

    @pl.loop(0, G)
    def _(g):
        v = normed(1, 3, g) + s.u_seg[1, group(g)].astype(F32)
        act, slope = gelu_pair(v)
        o = jnp.where(real_rows(c.cs), act, 0.0).astype(BF16)
        s.out_seg[group(g)] = o
        e = s.g_seg[group(g)].astype(F32) * slope
        s.e3[group(g)] = e
        back_out(1, 3, g, e)
        o32 = o.astype(F32)
        place = lax.broadcasted_iota(jnp.int32, (GM, R, c.cs), 1)
        for n in range(c.images):
            here = (place >= n * SIDE * SIDE) & (place < (n + 1) * SIDE * SIDE)
            mean = jnp.sum(jnp.where(here, o32, 0.0), axis=1, keepdims=True) / float(SIDE * SIDE)
            for m in range(GM):
                s.pool[(g * GM + m) * c.images + n] = mean[m]

    out_copy = pltpu.make_async_copy(s.out_seg, bo_out, s.out_r.at[0])
    out_copy.start()

    banks = ND * c.bank
    which = lax.broadcasted_iota(jnp.int32, (banks, c.cs), 0)
    term = jnp.zeros((banks, c.cs), F32)
    for n in range(M * c.images):
        ids = jnp.concatenate([ids_ref[n : n + 1, :]] * (c.cs // LANES), axis=1)
        term = term + jnp.where(which == ids, s.pool[n], 0.0)
    s.bank_put[...] = term.reshape(ND, c.bank, c.cs)

    @pl.loop(1, ND)
    def _(i):
        d = dp_peer(i)
        remote(s.bank_put.at[d], s.bank_got.at[me_d], s.bank_s.at[0], s.bank_r.at[0], me_p, d).start()

    s.bank_got[me_d] = s.bank_put[me_d]

    def all_rows(ref):
        return ref[...].reshape(M * R, ref.shape[-1])

    def all_seg(ref):
        return jnp.concatenate([ref[j].reshape(M * R, LANES) for j in range(NP)], axis=1)

    def grad_q(k):
        h = all_seg(s.h2.at[k])
        s.gp[2 * k + 1] = dot_tn(all_rows(s.da3.at[k]), h).astype(BF16)

    def grad_p(k):
        d = all_seg(s.da1.at[k])
        s.gp[2 * k] = dot_tn(all_rows(s.u_seg.at[k]), d).astype(BF16)

    def grad_w(k):
        h = all_seg(s.h1.at[k])
        d = s.da2[k, shard(k, me_p)].astype(F32)
        for t0 in range(0, TAPS, 2):
            taps = [t for t in (t0, t0 + 1) if t < TAPS]
            cols = []
            for t in taps:
                part = (d * s.mask[t][None]).reshape(M * R, LANES)
                by = tap_shift(t) % (M * R)
                cols.append((part if by == 0 else pltpu.roll(part, by, 0)).astype(BF16))
            v = dot_tn(h, cols[0] if len(cols) == 1 else jnp.concatenate(cols, axis=1))
            for n, t in enumerate(taps):
                s.gw[k, t * c.mid : (t + 1) * c.mid, :] = v[:, n * LANES : (n + 1) * LANES].astype(BF16)

    me_c = lax.rem(me_d, 2)
    me_z = lax.div(me_d, 2)
    sib = me_d + 1 - 2 * me_c

    def half_rows(n, which):
        return pl.ds(pl.multiple_of(which * n, 16), n)

    def job_refs(job):
        if job < NP:
            return s.gp.at[job], s.p_sib.at[job], s.p_z.at[job], s.p_fin.at[job], c.cs // 2
        k = job - NP
        return s.gw.at[k], s.w_sib.at[k], s.w_z.at[k], s.w_fin.at[k], TAPS * c.mid // 2

    def z_dev(z):
        return 2 * z + me_c

    def z_peer(i):
        return lax.rem(me_z + i, c.zs)

    def job_core(job):
        own, got, _, _, n = job_refs(job)
        remote(own.at[half_rows(n, 1 - me_c)], got, s.gs.at[job, 0], s.gr.at[job, 0], me_p, sib).start()

    def job_spread(job):
        own, got, zbuf, fin, n = job_refs(job)
        q = n // c.zs
        take_recv(got, s.gs.at[job, 0], s.gr.at[job, 0])
        got[...] = (got[...].astype(F32) + own[half_rows(n, me_c), :].astype(F32)).astype(BF16)
        for i in range(1, c.zs):
            z = z_peer(i)
            remote(got.at[half_rows(q, z)], zbuf.at[me_z], s.gs.at[job, 1], s.gr.at[job, 1], me_p, z_dev(z)).start()
        zbuf[me_z] = got[half_rows(q, me_z), :]

    def job_sum(job):
        _, got, zbuf, fin, n = job_refs(job)
        q = n // c.zs
        if c.zs > 1:
            take_recv(zbuf.at[pl.ds(0, c.zs - 1)], s.gs.at[job, 1], s.gr.at[job, 1])
        tot = zbuf[0].astype(F32)
        for z in range(1, c.zs):
            tot = tot + zbuf[z].astype(F32)
        fin[half_rows(q, me_z), :] = tot.astype(BF16)
        view = fin.at[half_rows(q, me_z)]
        for i in range(1, c.zs):
            remote(view, view, s.gs.at[job, 2], s.gr.at[job, 2], me_p, z_dev(z_peer(i))).start()

    def job_place(job, p, core):
        n = job_refs(job)[4]
        if job < NP:
            return s.p_out.at[pl.ds(pl.multiple_of(p * 2 * n + core * n, 16), n)]
        k = job - NP
        side = lax.div(p, 2) if k == 0 else 1 - lax.div(p, 2)
        return s.w_out.at[half_rows(n, core), pl.ds(pl.multiple_of(side * LANES, LANES), LANES)]

    def job_home(job, p):
        return job if job < NP else 2 * (job - NP) + lax.rem(p, 2)

    def job_holds(job):
        return me_p == job if job < NP else me_y == job - NP

    def job_plane(job):
        _, _, _, fin, n = job_refs(job)
        if c.zs > 1:
            take_recv(fin.at[pl.ds(0, n // c.zs * (c.zs - 1))], s.gs.at[job, 2], s.gr.at[job, 2])
        home = job_home(job, me_p)

        @pl.when(me_p != home)
        def _():
            remote(fin, job_place(job, me_p, me_c), s.gs.at[job, 3], s.gr.at[job, 3], home, me_d).start()

        @pl.when(me_p == home)
        def _():
            pltpu.make_async_copy(fin, job_place(job, me_p, me_c), s.own_s.at[job]).start()

    def job_sources(job):
        if job < NP:
            return [lax.rem(me_p + i, NP) for i in range(1, NP)]
        return [lax.rem(me_p + 2, NP)]

    def job_share(job):
        _, _, _, fin, n = job_refs(job)

        @pl.when(job_holds(job))
        def _():
            pltpu.make_async_copy(fin, job_place(job, me_p, me_c), s.own_s.at[job]).wait()
            src = job_sources(job)
            if job < NP:
                view = s.p_out.at[pl.ds(0, n * len(src))]
            else:
                view = fin
            take_recv(view, s.gs.at[job, 3], s.gr.at[job, 3])
            for p in [me_p] + src:
                view = job_place(job, p, me_c)
                remote(view, view, s.fin_s.at[job], s.fin_r.at[job], me_p, sib).start()

    def job_end(job):
        _, _, _, fin, n = job_refs(job)
        half, q = fin, n // c.zs
        take_send(half, s.gs.at[job, 0], s.gr.at[job, 0])
        if c.zs > 1:
            take_send(fin.at[pl.ds(0, q * (c.zs - 1))], s.gs.at[job, 1], s.gr.at[job, 1])
            take_send(fin.at[pl.ds(0, q * (c.zs - 1))], s.gs.at[job, 2], s.gr.at[job, 2])

        @pl.when(me_p != job_home(job, me_p))
        def _():
            take_send(half, s.gs.at[job, 3], s.gr.at[job, 3])

        @pl.when(job_holds(job))
        def _():
            parts = NP if job < NP else 2
            view = s.p_out.at[pl.ds(0, n * parts)] if job < NP else s.w_out.at[pl.ds(0, n)]
            take_recv(view, s.fin_s.at[job], s.fin_r.at[job])
            take_send(view, s.fin_s.at[job], s.fin_r.at[job])

    for k in (1, 0):
        side = 2 * (1 - k)

        @pl.loop(0, G)
        def _(g):
            grad = back_in(k, 3, g, s.e3[group(g)])
            s.da3[k, group(g)] = grad
            rs_send(2 + (1 - k), g, k, dot(grad.reshape(flat, c.cs), s.pq[2 * k + 1]))

        grad_q(k)

        @pl.loop(0, G)
        def _(g):
            up = rs_take(2 + (1 - k), g, k) * s.d2[k, group(g)]
            s.t1[group(g)] = up
            back_out(k, 2, g, up)

        @pl.loop(0, G)
        def _(g):
            mine = shard(k, me_p)
            s.da2[k, mine, group(g)] = back_in(k, 2, g, s.t1[group(g)])
            ag_send(4 + side, g, s.da2.at[k], mine)

        need_back(k)
        grad_w(k)

        @pl.loop(0, G)
        def _(g):
            up = conv_back(k, ag_take(4 + side, g, s.da2.at[k])) * s.d1[k, group(g)]
            s.t1[group(g)] = up
            back_out(k, 1, g, up)

        @pl.loop(0, G)
        def _(g):
            mine = shard(k, me_p)
            s.da1[k, mine, group(g)] = back_in(k, 1, g, s.t1[group(g)])
            ag_send(5 + side, g, s.da1.at[k], mine)

        if k == 0:
            need_proj(0)
        if k == 1:
            need_proj(3) if False else None

        @pl.loop(0, G)
        def _(g):
            d = dot_nt(ag_take(5 + side, g, s.da1.at[k]), s.pq[2 * k])
            d = d.reshape(GM, R, c.cs) + s.e3[group(g)]
            if k == 1:
                e = d * s.d3[0, group(g)]
                s.e3[group(g)] = e
                back_out(0, 3, g, e)
            else:
                s.in_seg[group(g)] = d.astype(BF16)

        grad_p(k)

    in_copy = pltpu.make_async_copy(s.in_seg, ig_out, s.out_r.at[1])
    in_copy.start()
    view = s.norm_sum.at[me_p]
    for i in range(1, NP):
        remote(view, view, s.ns_s.at[0], s.ns_r.at[0], pipe_peer(i), me_d).start()

    if c.deep:
        order = (3, 5, 2, 1, 4, 0)
        for step in (job_core, job_spread, job_sum, job_plane, job_share):
            for job in order:
                step(job)

    take_recv(s.bank_got.at[pl.ds(0, ND - 1)], s.bank_s.at[0], s.bank_r.at[0])
    tot = s.bank_got[0]
    for d in range(1, ND):
        tot = tot + s.bank_got[d]
    mb_out[...] = tot
    take_recv(s.norm_sum.at[pl.ds(0, NP - 1)], s.ns_s.at[0], s.ns_r.at[0])
    per = c.mid // LANES
    wide = c.cs // LANES
    each = (2 * per + c.ch // LANES) // NP
    for k in range(2):
        for n in range(each):
            q = me_p * each + n
            in_one = q < per
            in_two = (q >= per) & (q < 2 * per)
            sh = jnp.where(in_one, q, q - per)
            half = lax.rem(sh + k, 2)
            small = 2 * half + lax.div(sh, 2)
            far = q - 2 * per
            p = jnp.where(q < 2 * per, small, lax.div(far, wide))
            chunk = jnp.where(in_one, 0, jnp.where(in_two, 1, 2 + lax.rem(far, wide)))
            ns_out[n, 2 * k : 2 * k + 2, :] = s.norm_sum[p, chunk, 2 * k : 2 * k + 2, :]

    if c.deep:
        for job in range(6):
            job_end(job)
        p_copy = pltpu.make_async_copy(s.p_out, gp_out, s.out_r.at[2])
        w_copy = pltpu.make_async_copy(s.w_out, gw_out, s.out_r.at[3])
    else:
        p_copy = pltpu.make_async_copy(s.gp, gp_out, s.out_r.at[2])
        w_copy = pltpu.make_async_copy(s.gw, gw_out, s.out_r.at[3])
    p_copy.start()
    w_copy.start()
    take_send(s.norm_sum.at[pl.ds(0, NP - 1)], s.ns_s.at[0], s.ns_r.at[0])
    take_send(s.bank_got.at[pl.ds(0, ND - 1)], s.bank_s.at[0], s.bank_r.at[0])
    front_send().wait_send()
    for i in range(1, NP):
        proj_send(i).wait_send()
        back_send(i).wait_send()

    @pl.loop(0, G)
    def _(g):
        for idx in range(12):
            take_send(ar_ref(idx).at[pl.ds(0, ND - 1), group(g)], s.ar_s.at[idx, g], s.ar_r.at[idx, g])
        for idx in range(8):
            take_send(s.h1.at[0, pl.ds(0, NP - 1), group(g)], s.ag_s.at[idx, g], s.ag_r.at[idx, g])
        for idx in range(1, 4):
            take_send(s.put.at[idx, pl.ds(0, NP - 1), group(g)], s.rs_s.at[idx, g], s.rs_r.at[idx, g])

        @pl.when(me_p == 0)
        def _():
            take_send(s.put.at[0, pl.ds(0, NP - 1), group(g)], s.rs_s.at[0, g], s.rs_r.at[0, g])

    out_copy.wait()
    in_copy.wait()
    p_copy.wait()
    w_copy.wait()


def on_device(mesh, block_input, proj_weight, spatial_weight, norm_gain, norm_shift, output_grad, image_ids):
    bank = 8
    c = Sizes(mesh, block_input, proj_weight, spatial_weight, bank)
    extra = ((0, 0), (0, c.pad - c.rows), (0, 0))
    u = jnp.pad(block_input, extra)
    go = jnp.pad(output_grad, extra)
    sw = spatial_weight.reshape(TAPS, c.mid, spatial_weight.shape[2])
    ids = jnp.broadcast_to(image_ids.reshape(-1, 1), (image_ids.size, LANES))
    items = scratch_list(c)
    names = [n for n, _ in items]
    anyspec = pl.BlockSpec(memory_space=pl.ANY)
    vspec = pl.BlockSpec(memory_space=pltpu.VMEM)
    if c.deep:
        gp_shape, gw_shape = (c.ch, c.mid), (TAPS * c.mid, 2 * LANES)
    else:
        gp_shape, gw_shape = (c.pipes, c.cs, c.mid), (2, TAPS * c.mid, LANES)
    each = (2 * c.mid + c.ch) // LANES // c.pipes
    outs = pl.pallas_call(
        functools.partial(body, c, names),
        out_shape=(
            jax.ShapeDtypeStruct((c.micro, c.pad, c.cs), BF16),
            jax.ShapeDtypeStruct((c.micro, c.pad, c.cs), BF16),
            jax.ShapeDtypeStruct(gp_shape, BF16),
            jax.ShapeDtypeStruct(gw_shape, BF16),
            jax.ShapeDtypeStruct((each, 4, LANES), F32),
            jax.ShapeDtypeStruct((bank, c.cs), F32),
        ),
        in_specs=[anyspec] * 4 + [vspec] * 3,
        out_specs=(anyspec, anyspec, anyspec, anyspec, vspec, vspec),
        scratch_shapes=[v for _, v in items],
        compiler_params=pltpu.CompilerParams(collective_id=0, has_side_effects=True, vmem_limit_bytes=60 << 20),
    )(u, go, proj_weight[0], sw, norm_gain, norm_shift, ids)
    bo, ig, gp, gw, ns, mb = outs
    if not c.deep:
        gp = lax.psum(gp.astype(F32), "dp")
        gw = lax.psum(gw.astype(F32), "dp")
        gp = lax.all_to_all(gp, "pipe", 0, 0, tiled=True).reshape(c.ch, c.mid)
        gw = lax.all_gather(gw, "pipe")
        me = lax.axis_index("pipe")
        y, x = me // 2, me % 2
        near = lax.dynamic_index_in_dim(gw, me, 0, keepdims=False)
        far = lax.dynamic_index_in_dim(gw, 2 * (1 - y) + x, 0, keepdims=False)
        gw = jnp.concatenate(
            [lax.dynamic_index_in_dim(near, y, 0, keepdims=False), lax.dynamic_index_in_dim(far, y, 0, keepdims=False)],
            axis=1,
        )
    ns = jnp.transpose(ns.reshape(each, 2, 2, LANES), (2, 1, 0, 3)).reshape(2, 2, each * LANES)
    return (
        bo[:, : c.rows],
        ig[:, : c.rows],
        gp.astype(F32)[None],
        gw.astype(F32)[None],
        ns[0],
        ns[1],
        mb,
    )


def solution(mesh):
    return jax.shard_map(
        functools.partial(on_device, mesh),
        mesh=mesh,
        in_specs=(
            P(None, "dp", None),
            P("pipe", None, None),
            P("pipe", None, None),
            P(),
            P(),
            P(None, "dp", None),
            P(None, "dp"),
        ),
        out_specs=(
            P(None, "dp", "pipe"),
            P(None, "dp", "pipe"),
            P("pipe", None, None),
            P("pipe", None, None),
            P(None, "pipe"),
            P(None, "pipe"),
            P("dp", "pipe"),
        ),
        check_vma=False,
    )
```

time: 1750 us -> 332 us (0.19); the launches traced: 1730 us -> 330 us
  waiting for transfers between devices: 429 us -> 0 us
  blocking collectives: 409 us -> 0 us
  local copies, waits for them, and re-layouts: 416 us -> 11.4 us
  Pallas kernels: 0 us -> 311 us
  other arithmetic: 166 us -> 6.97 us
  starting transfers between devices: 147 us -> 0 us
  matrix products: 137 us -> 0 us
    psum x28 -> x0, blocking collectives: 409 us -> none  [the longest x14 210 us: norm_stats(): lax.psum((jnp.sum(values, axis=0), jnp.sum(values * values, axis=0)), 'dp')]
    pallas_call x0 -> x1, Pallas kernels: none -> 311 us  [on_device(): pl.pallas_call(functools.partial(body, c, names), out_shape=(jax.ShapeDty...]
    psum x1 -> x0, waiting for transfers between devices: 187 us -> none  [on_device(): summed_grads = lax.psum((pending_reduce, pending_spatial), 'dp')]
    ppermute x24 -> x0, waiting for transfers between devices: 159 us -> none  [passed_along(): return lax.ppermute(x, axis, pairs)]
    ppermute x24 -> x0, starting transfers between devices: 147 us -> none  [passed_along(): return lax.ppermute(x, axis, pairs)]
    dot_general x57 -> x0, matrix products: 137 us -> none  [the longest x14 39.9 us: contract_cols(): lax.dot_general(left, right, (((1,), (1,)), ((), ())), preferred_element_...]
    cond x347 -> x0, local copies, waits for them, and re-layouts: 109 us -> none
    slice x131 -> x2, local copies, waits for them, and re-layouts: 93.5 us -> 0.06 us  [the longest x1 0.03 us: on_device(): bo[:, :c.rows]]
  transfers between devices with their start and end apart: 30 -> 0, of which waited for: 21 -> 0; matrix products, arithmetic and copies ran while one was open for 30% -> 0% of each run, Pallas kernels for 0% -> 0%
where the time goes in v1:
time: 332 us; the launch traced here: 330 us
  Pallas kernels  311 us (94%)
  local copies, waits for them, and re-layouts  11.4 us (3%)
  other arithmetic  6.97 us (2%)
    pallas_call x1, Pallas kernels, on_device(): pl.pallas_call(functools.partial(body, c, names), out_shape=(jax.ShapeDty...  311 us

profile of v1, /device:TPU:0, one launch (start us, length us, event | category | flops | bytes accessed | tf_op | source)
XLA Modules:
  0.0 330.0 jit_solution(5619024050887383259)
XLA Ops:
  0.6 2.3 copy.21
  2.9 0.0 copy-start.1
  3.0 1.4 pad.7.refs_0_
  4.4 0.6 copy-done.1
  5.0 0.9 copy.22
  5.9 0.0 copy-start.5
  5.9 1.4 pad.8.refs_1_
  7.3 0.0 copy-done.5
  7.3 0.1 copy.23
  7.4 0.1 broadcast_in_dim.19
  7.5 0.7 broadcast_in_dim.20.refs_6_
  8.2 310.9 %shard_map.126 = (bf16[4,112,512]{2,1,0:T(8,128)(2,1)}, bf16[4,112,512]{2,1,0:T(8,128)(2,1)}, bf16[2048,512]{1,0:T(8,128)(2,1)}, bf16[4608,256]{1,0:T(8,128)(2,1...) custom-call(bf16[4,112,2048]{2,1,0:T(8,128)(2,1)} %pad.7.refs_0_, bf16[4,112,2048]{2,1,0:T(8,128)(2,1)} %pad.8.refs_1_, ...), custom_call_target="tpu_custom_call" | custom-call | tf_op jit(solution)/shard_map/pallas_call | solution.py:796
  319.1 0.7 copy.32
  319.8 0.6 copy_bitcast_fusion.1
  320.5 0.0 copy-start
  320.5 4.4 %bitcast_convert_fusion = f32[1,4608,256]{2,1,0:T(8,128)} fusion(bf16[4608,256]{1,0:T(8,128)(2,1)} %get-tuple-element.16), kind=kLoop, calls=%fused_computation | loop fusion | flops 1179648 | bytes 7077888 | tf_op jit(solution)/shard_map/broadcast_in_dim | solution.py:830
  324.8 0.0 copy-done
  324.8 0.0 copy-start.3
  324.8 0.0 copy-start.2
  324.8 2.6 bitcast_convert_fusion.1
  327.4 0.0 copy-start.4
  327.4 0.0 copy-done.3
  327.5 1.0 copy.25
  328.4 0.0 copy-done.2
  328.5 1.0 copy.26
  329.4 0.0 copy-done.4
  329.4 0.6 copy.34
  (3 shorter events, 0.1 us)
Async XLA Ops:
  2.9 2.1 copy-start.1
  5.9 1.4 copy-start.5
  320.5 4.4 %copy-start = (bf16[2048,512]{1,0:T(8,128)(2,1)S(1)}, bf16[2048,512]{1,0:T(8,128)(2,1)}, u32[]{:S(2)}) copy-start(bf16[2048,512]{1,0:T(8,128)(2,1)} %get-tuple-element.15) | copy-start | bytes 6291460
  324.8 2.6 copy-start.3
  324.8 3.6 %copy-start.2 = (bf16[4,112,512]{2,1,0:T(8,128)(2,1)S(1)}, bf16[4,112,512]{2,1,0:T(8,128)(2,1)}, u32[]{:S(2)}) copy-start(bf16[4,112,512]{2,1,0:T(8,128)(2,1)} %get-tuple-element.14) | copy-start | bytes 1376260
  327.4 2.0 copy-start.4

commit v2 on v1

v2 whole, which is shorter than its diff:
```python
import functools
import math
import types

import jax
import jax.numpy as jnp
from jax import lax
from jax.experimental import pallas as pl
from jax.experimental.pallas import tpu as pltpu
from jax.sharding import PartitionSpec as P

SIDE = 7
TAPS = 9
EPS = 1e-05
LANES = 128
GROUPS = 4
W_PIECES = 3
P_PIECES = 2
POINTS = (
    (0,),
    (0,),
    (1, 2, 3),
    (0, 1, 2, 3),
    (0,),
    (4, 0, 1),
    (5, 4, 0, 1, 2),
    (5, 1, 2, 3),
    (6, 7, 8, 4, 0, 1, 2, 3),
    (5, 6, 7, 8, 4, 2, 3),
    (9, 10, 5, 4, 1, 3),
    (9, 10, 6, 5, 4, 2),
)
LAST = (5, 6, 4, 3, 7, 9, 8, 10)
MESH = pl.DeviceIdType.MESH
F32 = jnp.float32
BF16 = jnp.bfloat16


def gelu_pair(v):
    c0 = math.sqrt(2.0 / math.pi)
    c1 = 0.044715
    sq = v * v
    t = jnp.tanh(c0 * v * (1.0 + c1 * sq))
    half = 0.5 + 0.5 * t
    slope = half + (0.5 * c0) * v * (1.0 - t * t) * (1.0 + (3.0 * c1) * sq)
    return v * half, slope


def dot(a, b):
    return jnp.dot(a, b, preferred_element_type=F32)


def dot_nt(a, b):
    return lax.dot_general(a, b, (((1,), (1,)), ((), ())), preferred_element_type=F32)


def dot_tn(a, b):
    return lax.dot_general(a, b, (((0,), (0,)), ((), ())), preferred_element_type=F32)


class Sizes:
    def __init__(self, mesh, block_input, proj, spatial, bank_rows):
        self.pipes = mesh.shape["pipe"]
        self.dps = mesh.shape["dp"]
        self.micro = block_input.shape[0]
        self.rows = block_input.shape[1]
        self.pad = -(-self.rows // 16) * 16
        self.ch = block_input.shape[2]
        self.mid = proj.shape[2]
        self.images = self.rows // (SIDE * SIDE)
        self.cs = self.ch // self.pipes
        self.msd = self.mid // self.pipes
        self.groups = GROUPS
        self.gm = self.micro // self.groups
        self.zs = self.dps // 2
        self.total = self.rows * self.dps
        self.bank = bank_rows
        self.deep = self.zs == 4
        self.jobs = {}
        taps = TAPS // W_PIECES
        for k in (1, 0):
            self.jobs[len(self.jobs)] = ("q", k, self.cs // 2, 0, 1 - k)
            for i in range(W_PIECES):
                self.jobs[len(self.jobs)] = ("w", k, taps * self.mid // 2, i * taps * self.mid, (1 - k) * W_PIECES + i)
            if k == 1:
                self.jobs[len(self.jobs)] = ("p", k, self.cs // 2, 0, 2)
        for i in range(P_PIECES):
            self.jobs[len(self.jobs)] = ("0", 0, self.ch // P_PIECES // 2, i * self.ch // P_PIECES, i)


def scratch_list(c):
    full = (c.micro, c.pad)
    seg = (c.pipes, c.micro, c.pad, LANES)
    items = [
        ("u_all", pltpu.VMEM(full + (c.ch,), BF16)),
        ("u_seg", pltpu.VMEM((2,) + full + (c.cs,), BF16)),
        ("g_seg", pltpu.VMEM(full + (c.cs,), BF16)),
        ("p_own", pltpu.VMEM((c.ch, c.mid), BF16)),
        ("pq", pltpu.VMEM((c.pipes, c.cs, c.mid), BF16)),
        ("wf", pltpu.VMEM((2, TAPS, c.mid, LANES), BF16)),
        ("wb", pltpu.VMEM((2, 4, TAPS, LANES, LANES), BF16)),
        ("sw", pltpu.VMEM((2, TAPS, c.mid, LANES), BF16)),
        ("mask", pltpu.VMEM((TAPS, c.pad, LANES), F32)),
        ("z1", pltpu.VMEM((2,) + full + (LANES,), F32)),
        ("d1", pltpu.VMEM((2,) + full + (LANES,), F32)),
        ("z2", pltpu.VMEM((2,) + full + (LANES,), F32)),
        ("d2", pltpu.VMEM((2,) + full + (LANES,), F32)),
        ("z3", pltpu.VMEM((2,) + full + (c.cs,), F32)),
        ("d3", pltpu.VMEM((2,) + full + (c.cs,), F32)),
        ("e3", pltpu.VMEM(full + (c.cs,), F32)),
        ("t1", pltpu.VMEM(full + (LANES,), F32)),
        ("gr1", pltpu.VMEM((2, c.micro, 1, LANES), F32)),
        ("gr2", pltpu.VMEM((2, c.micro, 1, LANES), F32)),
        ("gr3", pltpu.VMEM((2, c.micro, 1, c.cs), F32)),
        ("h1", pltpu.VMEM((2,) + seg, BF16)),
        ("h2", pltpu.VMEM((2,) + seg, BF16)),
        ("da3", pltpu.VMEM((2,) + full + (c.cs,), BF16)),
        ("da2", pltpu.VMEM((2,) + seg, BF16)),
        ("da1", pltpu.VMEM((2,) + seg, BF16)),
        ("first", pltpu.VMEM(full + (LANES,), BF16)),
        ("put", pltpu.VMEM((4,) + seg, BF16)),
        ("got", pltpu.VMEM((4,) + seg, BF16)),
        ("out_seg", pltpu.VMEM(full + (c.cs,), BF16)),
        ("in_seg", pltpu.VMEM(full + (c.cs,), BF16)),
        ("ar_small", pltpu.VMEM((8, c.dps, c.micro, 2, LANES), F32)),
        ("ar_wide", pltpu.VMEM((4, c.dps, c.micro, 2, c.cs), F32)),
        ("pool", pltpu.VMEM((c.micro * c.images, 1, c.cs), F32)),
        ("bank_put", pltpu.VMEM((c.dps, c.bank, c.cs), F32)),
        ("bank_got", pltpu.VMEM((c.dps, c.bank, c.cs), F32)),
        ("norm_sum", pltpu.VMEM((c.pipes, 6, 8, LANES), F32)),
        ("gp", pltpu.VMEM((c.pipes, c.cs, c.mid), BF16)),
        ("g0", pltpu.VMEM((c.ch, LANES), BF16)),
        ("gw", pltpu.VMEM((2, TAPS * c.mid, LANES), BF16)),
        ("ar_s", pltpu.SemaphoreType.DMA((12, c.groups))),
        ("ar_r", pltpu.SemaphoreType.DMA((12, c.groups))),
        ("ag_s", pltpu.SemaphoreType.DMA((8, c.groups))),
        ("ag_r", pltpu.SemaphoreType.DMA((8, c.groups))),
        ("rs_s", pltpu.SemaphoreType.DMA((4, c.groups))),
        ("rs_r", pltpu.SemaphoreType.DMA((4, c.groups))),
        ("w_s", pltpu.SemaphoreType.DMA((3, c.pipes))),
        ("pass_s", pltpu.SemaphoreType.DMA((3, c.pipes))),
        ("pq_r", pltpu.SemaphoreType.DMA((c.pipes,))),
        ("pq_q", pltpu.SemaphoreType.DMA((c.pipes,))),
        ("wf_r", pltpu.SemaphoreType.DMA((2,))),
        ("wf_q", pltpu.SemaphoreType.DMA((2,))),
        ("wb_r", pltpu.SemaphoreType.DMA((2, 2))),
        ("wb_q", pltpu.SemaphoreType.DMA((2, 2))),
        ("bank_s", pltpu.SemaphoreType.DMA((1,))),
        ("bank_r", pltpu.SemaphoreType.DMA((1,))),
        ("ns_s", pltpu.SemaphoreType.DMA((1,))),
        ("ns_r", pltpu.SemaphoreType.DMA((1,))),
        ("in_r", pltpu.SemaphoreType.DMA((6,))),
        ("out_r", pltpu.SemaphoreType.DMA((4 + c.pipes,))),
    ]
    if c.deep:
        for name, width in (("p", c.mid), ("w", LANES), ("0", LANES)):
            of = [job for job in c.jobs.values() if job[0] in {"p": "pq"}.get(name, name)]
            lead, n = len(of), of[0][2]
            items += [(key + name, pltpu.VMEM((lead, n // (1 + (key == "jd")), width), BF16)) for key in ("ja", "jb", "jc", "jd", "je")]
        count = len(c.jobs)
        items += [
            ("p_out", pltpu.VMEM((c.ch, c.mid), BF16)),
            ("p0_out", pltpu.VMEM((c.pipes, c.ch, LANES), BF16)),
            ("w_out", pltpu.VMEM((2, TAPS * c.mid, LANES), BF16)),
            ("gs", pltpu.SemaphoreType.DMA((count, 7))),
            ("gr", pltpu.SemaphoreType.DMA((count, 6))),
            ("own_s", pltpu.SemaphoreType.DMA((count,))),
            ("fin_s", pltpu.SemaphoreType.DMA((count,))),
            ("fin_r", pltpu.SemaphoreType.DMA((count,))),
        ]
    return items


def body(c, names, *refs):
    (u_hbm, go_hbm, pw_hbm, sw_hbm, gain_ref, shift_ref, ids_ref) = refs[:7]
    (bo_out, ig_out, gp_out, gw_out, ns_out, mb_out) = refs[7:13]
    s = types.SimpleNamespace(**dict(zip(names, refs[13:])))
    me_p = lax.axis_index("pipe")
    me_d = lax.axis_index("dp")
    me_x = lax.rem(me_p, 2)
    me_y = lax.div(me_p, 2)
    NP, ND, M, GM, G, R = c.pipes, c.dps, c.micro, c.gm, c.groups, c.pad
    flat = GM * R
    count = float(c.total)

    def shard(k, p):
        half = lax.div(p, 2)
        return 2 * lax.rem(p, 2) + (half if k == 0 else 1 - half)

    def pipe_peer(i):
        return lax.rem(me_p + i, NP)

    def dp_peer(i):
        return lax.rem(me_d + i, ND)

    def remote(src, dst, ss, rs, p, d):
        return pltpu.make_async_remote_copy(
            src_ref=src, dst_ref=dst, send_sem=ss, recv_sem=rs, device_id=(p, d), device_id_type=MESH
        )

    def take_recv(view, ss, rs):
        remote(view, view, ss, rs, me_p, me_d).wait_recv()

    def take_send(view, ss, rs):
        remote(view, view, ss, rs, me_p, me_d).wait_send()

    def group(g):
        return pl.ds(g * GM, GM)

    owed, due = {}, {}

    lane0 = pl.multiple_of(me_p * c.cs, LANES)
    seg_cols = pl.ds(lane0, c.cs)
    load_u = pltpu.make_async_copy(u_hbm.at[:, :, seg_cols], s.u_seg.at[0], s.in_r.at[0])
    load_g = pltpu.make_async_copy(go_hbm.at[:, :, seg_cols], s.g_seg, s.in_r.at[1])
    load_all = pltpu.make_async_copy(u_hbm, s.u_all, s.in_r.at[2])
    load_p = pltpu.make_async_copy(pw_hbm, s.p_own, s.in_r.at[3])
    load_w = [
        pltpu.make_async_copy(sw_hbm.at[:, :, pl.ds(h * LANES, LANES)], s.sw.at[h], s.in_r.at[4 + h]) for h in range(2)
    ]
    load_all.start()

    @pl.when(me_p == 0)
    def _():
        load_p.start()

    for load in load_w:
        load.start()
    load_u.start()
    load_g.start()

    barrier = pltpu.get_barrier_semaphore()
    for i in range(1, NP):
        pl.semaphore_signal(barrier, inc=1, device_id=(pipe_peer(i), me_d), device_id_type=MESH)

    @pl.loop(1, ND)
    def _(i):
        pl.semaphore_signal(barrier, inc=1, device_id=(me_p, dp_peer(i)), device_id_type=MESH)

    row = lax.broadcasted_iota(jnp.int32, (R, LANES), 0)
    image = jnp.zeros_like(row)
    for n in range(1, c.images):
        image = image + (row >= n * SIDE * SIDE).astype(jnp.int32)
    pixel = row - image * (SIDE * SIDE)
    up = jnp.zeros_like(row)
    for n in range(1, SIDE):
        up = up + (pixel >= n * SIDE).astype(jnp.int32)
    across = pixel - up * SIDE
    for t in range(TAPS):
        i, j = t // 3 - 1, t % 3 - 1
        ok = (up + i >= 0) & (up + i < SIDE) & (across + j >= 0) & (across + j < SIDE) & (row < c.rows)
        s.mask[t] = ok.astype(F32)
    s.norm_sum[...] = jnp.zeros_like(s.norm_sum)

    pl.semaphore_wait(barrier, NP - 1 + ND - 1)

    me_c = lax.rem(me_d, 2)
    me_z = lax.div(me_d, 2)
    sib = me_d + 1 - 2 * me_c

    def rows_of(p):
        return pl.ds(pl.multiple_of(p * c.cs, 16), c.cs)

    def half_of(n, which):
        return pl.ds(pl.multiple_of(which * (n // 2), 16), n // 2)

    def proj_half(i, core):
        return s.pq.at[i, half_of(c.cs, core)]

    def proj_send(i):
        p = pipe_peer(i)
        src = pw_hbm.at[pl.ds(pl.multiple_of(p * c.cs + me_c * (c.cs // 2), 16), c.cs // 2)]
        return remote(src, proj_half(me_p, me_c), s.w_s.at[0, i], s.pq_r.at[me_p], p, me_d)

    def proj_pass(i):
        view = proj_half(i, me_c)
        return remote(view, view, s.pass_s.at[0, i], s.pq_q.at[i], me_p, sib)

    def pass_proj(i):
        @pl.when(me_p != i)
        def _():
            take_recv(proj_half(i, me_c), s.pass_s.at[0, i], s.pq_r.at[i])
            proj_pass(i).start()

    def need_proj(i):
        @pl.when(me_p != i)
        def _():
            take_recv(proj_half(i, 1 - me_c), s.pass_s.at[0, i], s.pq_q.at[i])

        @pl.when(me_p == i)
        def _():
            pltpu.make_async_copy(s.pq.at[i], s.pq.at[i], s.pq_r.at[i]).wait()

    def end_proj(i):
        @pl.when(me_p != i)
        def _():
            proj_pass(i).wait_send()

    def front_half(k, core):
        return s.wf.at[k, :, half_of(c.mid, core)]

    def front_send():
        return remote(
            s.sw.at[1, :, half_of(c.mid, me_c)],
            front_half(me_y, me_c),
            s.w_s.at[1, 0],
            s.wf_r.at[me_y],
            lax.rem(me_p + 2, NP),
            me_d,
        )

    def front_pass(k):
        view = front_half(k, me_c)
        return remote(view, view, s.pass_s.at[1, k], s.wf_q.at[k], me_p, sib)

    def pass_front(k):
        @pl.when(me_y != k)
        def _():
            take_recv(front_half(k, me_c), s.pass_s.at[1, k], s.wf_r.at[k])
            front_pass(k).start()

    def need_front(k):
        @pl.when(me_y != k)
        def _():
            take_recv(front_half(k, 1 - me_c), s.pass_s.at[1, k], s.wf_q.at[k])

        @pl.when(me_y == k)
        def _():
            pltpu.make_async_copy(s.wf.at[k], s.wf.at[k], s.wf_r.at[k]).wait()

    def end_front(k):
        @pl.when(me_y != k)
        def _():
            front_pass(k).wait_send()

    def back_rows(p):
        sh = 2 * lax.rem(p, 2) + lax.rem(lax.div(p, 2) + me_y, 2)
        return pl.ds(pl.multiple_of(sh * LANES, LANES), LANES)

    def back_send(i):
        p = pipe_peer(i)
        return remote(
            s.sw.at[me_c, :, back_rows(p)],
            s.wb.at[me_y, 2 * me_x + me_c],
            s.w_s.at[2, i],
            s.wb_r.at[me_y, me_x],
            p,
            me_d,
        )

    def back_pass(k, e):
        view = s.wb.at[k, 2 * e + me_c]
        return remote(view, view, s.pass_s.at[2, 2 * k + e], s.wb_q.at[k, e], me_p, sib)

    def pass_back(k):
        for e in range(2):

            @pl.when(me_p != 2 * k + e)
            def _():
                take_recv(s.wb.at[k, 2 * e + me_c], s.pass_s.at[2, 2 * k + e], s.wb_r.at[k, e])
                back_pass(k, e).start()

    def need_back(k):
        for e in range(2):

            @pl.when(me_p != 2 * k + e)
            def _():
                take_recv(s.wb.at[k, 2 * e + 1 - me_c], s.pass_s.at[2, 2 * k + e], s.wb_q.at[k, e])

            @pl.when(me_p == 2 * k + e)
            def _():
                view = s.wb.at[k, pl.ds(2 * e, 2)]
                pltpu.make_async_copy(view, view, s.wb_r.at[k, e]).wait()

    def end_back(k):
        for e in range(2):

            @pl.when(me_p != 2 * k + e)
            def _():
                back_pass(k, e).wait_send()

    for load in load_w:
        load.wait()
    front_send().start()
    pltpu.make_async_copy(pw_hbm.at[rows_of(me_p)], s.pq.at[me_p], s.pq_r.at[me_p]).start()
    pltpu.make_async_copy(s.sw.at[0], s.wf.at[me_y], s.wf_r.at[me_y]).start()
    pltpu.make_async_copy(
        s.sw.at[:, :, back_rows(me_p)], s.wb.at[me_y, pl.ds(2 * me_x, 2)], s.wb_r.at[me_y, me_x]
    ).start()

    def note(kind, idx, view, ss, rs):
        owed[kind, idx] = lambda g: take_send(view(g), ss.at[idx, g], rs.at[idx, g])
        due[kind, idx] = lambda g: take_recv(view(g), ss.at[idx, g], rs.at[idx, g])

    def grab(kind, idx, g):
        due.pop((kind, idx))(g)

    def ar_ref(idx):
        return s.ar_small.at[idx] if idx < 8 else s.ar_wide.at[idx - 8]

    def ar_send(idx, g, first, second):
        buf = ar_ref(idx)
        buf[me_d, group(g), 0:1, :] = first
        buf[me_d, group(g), 1:2, :] = second

        @pl.loop(1, ND)
        def _(i):
            view = buf.at[me_d, group(g)]
            remote(view, view, s.ar_s.at[idx, g], s.ar_r.at[idx, g], me_p, dp_peer(i)).start()

        note("ar", idx, lambda g: ar_ref(idx).at[pl.ds(0, ND - 1), group(g)], s.ar_s, s.ar_r)

    def ar_take(idx, g):
        buf = ar_ref(idx)
        grab("ar", idx, g)
        tot = buf[0, group(g)]
        for d in range(1, ND):
            tot = tot + buf[d, group(g)]
        return tot[:, 0:1, :], tot[:, 1:2, :]

    def ag_send(idx, g, buf, slot):
        view = buf.at[slot, group(g)]
        for i in range(1, NP):
            remote(view, view, s.ag_s.at[idx, g], s.ag_r.at[idx, g], pipe_peer(i), me_d).start()
        note("ag", idx, lambda g: s.h1.at[0, pl.ds(0, NP - 1), group(g)], s.ag_s, s.ag_r)

    def ag_take(idx, g, buf):
        grab("ag", idx, g)
        return jnp.concatenate([buf[j, group(g)].reshape(flat, LANES) for j in range(NP)], axis=1)

    def rs_send(idx, g, k, partial):
        for j in range(NP):
            s.put[idx, j, group(g)] = partial[:, j * LANES : (j + 1) * LANES].reshape(GM, R, LANES).astype(BF16)
        for i in range(1, NP):
            p = pipe_peer(i)
            remote(
                s.put.at[idx, shard(k, p), group(g)],
                s.got.at[idx, me_p, group(g)],
                s.rs_s.at[idx, g],
                s.rs_r.at[idx, g],
                p,
                me_d,
            ).start()
        note("rs", idx, lambda g: s.got.at[idx, pl.ds(0, NP - 1), group(g)], s.rs_s, s.rs_r)

    def rs_take(idx, g, k):
        grab("rs", idx, g)
        tot = s.put[idx, shard(k, me_p), group(g)].astype(F32)
        for i in range(1, NP):
            tot = tot + s.got[idx, pipe_peer(i), group(g)].astype(F32)
        return tot

    def shard_cols(base, k):
        return pl.ds(pl.multiple_of(base + shard(k, me_p) * LANES, LANES), LANES)

    def norm_cols(which, k):
        if which == 1:
            return shard_cols(0, k)
        if which == 2:
            return shard_cols(c.mid, k)
        return pl.ds(pl.multiple_of(2 * c.mid + me_p * c.cs, LANES), c.cs)

    def real_rows(width):
        return lax.broadcasted_iota(jnp.int32, (GM, R, width), 1) < c.rows

    ZD = {1: (s.z1, s.d1, s.gr1), 2: (s.z2, s.d2, s.gr2), 3: (s.z3, s.d3, s.gr3)}
    FWD = {(0, 1): 0, (0, 2): 1, (1, 1): 2, (1, 2): 3, (0, 3): 8, (1, 3): 9}
    BWD = {(1, 2): 4, (1, 1): 5, (0, 2): 6, (0, 1): 7, (1, 3): 10, (0, 3): 11}

    def stats_out(k, which, g, a):
        ZD[which][0][k, group(g)] = a
        ar_send(FWD[(k, which)], g, jnp.sum(a, axis=1, keepdims=True), jnp.sum(a * a, axis=1, keepdims=True))

    def normed(k, which, g):
        z_ref, _, gr_ref = ZD[which]
        one, two = ar_take(FWD[(k, which)], g)
        mean = one / count
        inv = lax.rsqrt(two / count - mean * mean + EPS)
        z = (z_ref[k, group(g)] - mean) * inv
        z_ref[k, group(g)] = z
        gain = gain_ref[k : k + 1, norm_cols(which, k)][None]
        gr_ref[k, group(g)] = gain * inv
        return z * gain + shift_ref[k : k + 1, norm_cols(which, k)][None]

    def hidden_out(k, which, g, idx, buf):
        act, slope = gelu_pair(normed(k, which, g))
        ZD[which][1][k, group(g)] = slope
        mine = shard(k, me_p)
        buf[k, mine, group(g)] = jnp.where(real_rows(LANES), act, 0.0).astype(BF16)
        ag_send(idx, g, buf.at[k], mine)

    def back_out(k, which, g, up):
        ar_send(
            BWD[(k, which)],
            g,
            jnp.sum(up, axis=1, keepdims=True),
            jnp.sum(up * ZD[which][0][k, group(g)], axis=1, keepdims=True),
        )

    def back_in(k, which, g, up):
        z_ref, _, gr_ref = ZD[which]
        one, two = ar_take(BWD[(k, which)], g)
        chunk0 = {1: 0, 2: 1, 3: 2}[which]
        for n in range(one.shape[-1] // LANES):
            lanes = slice(n * LANES, (n + 1) * LANES)
            s.norm_sum[me_p, chunk0 + n, 2 * k : 2 * k + 1, :] += jnp.sum(two[:, :, lanes], axis=0)
            s.norm_sum[me_p, chunk0 + n, 2 * k + 1 : 2 * k + 2, :] += jnp.sum(one[:, :, lanes], axis=0)
        grad = gr_ref[k, group(g)] * (up - one / count - z_ref[k, group(g)] * (two / count))
        return jnp.where(real_rows(grad.shape[-1]), grad, 0.0).astype(BF16)

    def shifted(v, by):
        by = by % flat
        return v if by == 0 else pltpu.roll(v, by, 0)

    def tap_shift(t):
        return SIDE * (t // 3 - 1) + (t % 3 - 1)

    def masked(v, t):
        return v.reshape(GM, R, LANES) * s.mask[t][None]

    def conv(k, h):
        acc = None
        for t0 in range(0, TAPS, 2):
            taps = [t for t in (t0, t0 + 1) if t < TAPS]
            w = s.wf[k, taps[0]] if len(taps) == 1 else jnp.concatenate([s.wf[k, t] for t in taps], axis=1)
            y = dot(h, w)
            for n, t in enumerate(taps):
                part = masked(shifted(y[:, n * LANES : (n + 1) * LANES], -tap_shift(t)), t)
                acc = part if acc is None else acc + part
        return acc

    def conv_back(k, d):
        acc = None
        for t0 in range(0, TAPS, 2):
            taps = [t for t in (t0, t0 + 1) if t < TAPS]
            w = [jnp.concatenate([s.wb[k, o, t] for o in range(4)], axis=1) for t in taps]
            w = w[0] if len(taps) == 1 else jnp.concatenate(w, axis=0)
            y = dot_nt(d, w)
            for n, t in enumerate(taps):
                part = masked(y[:, n * LANES : (n + 1) * LANES], t).reshape(flat, LANES)
                part = shifted(part, tap_shift(t))
                acc = part if acc is None else acc + part
        return acc.reshape(GM, R, LANES)

    tail, ends = [], []

    def work():
        load_all.wait()

        @pl.when(me_p == 0)
        def _():
            load_p.wait()

            @pl.loop(0, G)
            def _(g):
                a = dot(s.u_all[group(g)].reshape(flat, c.ch), s.p_own[...])
                for j in range(NP):
                    s.put[0, j, group(g)] = a[:, j * LANES : (j + 1) * LANES].reshape(GM, R, LANES).astype(BF16)
                s.first[group(g)] = s.put[0, 0, group(g)]
                for p in range(1, NP):
                    remote(
                        s.put.at[0, shard(0, jnp.int32(p)), group(g)], s.first.at[group(g)], s.rs_s.at[0, g], s.rs_r.at[0, g], p, me_d
                    ).start()

        for i in range(1, NP):
            proj_send(i).start()
            tail.append(proj_send(i).wait_send)

        for k in range(2):

            @pl.loop(0, G)
            def _(g):
                if k == 0:

                    @pl.when(me_p != 0)
                    def _():
                        take_recv(s.first.at[group(g)], s.rs_s.at[0, g], s.rs_r.at[0, g])

                    a = s.first[group(g)].astype(F32)
                else:
                    a = rs_take(1, g, 1)
                stats_out(k, 1, g, a)
            if k == 0:
                pass_front(0)

            @pl.loop(0, G)
            def _(g):
                hidden_out(k, 1, g, 2 * k, s.h1)

            if k == 1:
                pass_proj(3)
            need_front(k)

            @pl.loop(0, G)
            def _(g):
                stats_out(k, 2, g, conv(k, ag_take(2 * k, g, s.h1.at[k])))
            if k == 0:
                pass_proj(1)

            @pl.loop(0, G)
            def _(g):
                hidden_out(k, 2, g, 2 * k + 1, s.h2)
            if k == 1:
                for i in range(1, NP):
                    back_send(i).start()
                    tail.append(back_send(i).wait_send)

            need_proj(2 * k + 1)
            if k == 0:
                load_u.wait()
                pass_proj(2)

            @pl.loop(0, G)
            def _(g):
                a = dot_nt(ag_take(2 * k + 1, g, s.h2.at[k]), s.pq[2 * k + 1])
                stats_out(k, 3, g, a.reshape(GM, R, c.cs))

            if k == 0:
                need_proj(2)

                @pl.loop(0, G)
                def _(g):
                    v = normed(0, 3, g) + s.u_seg[0, group(g)].astype(F32)
                    act, slope = gelu_pair(v)
                    s.d3[0, group(g)] = slope
                    o = jnp.where(real_rows(c.cs), act, 0.0).astype(BF16)
                    s.u_seg[1, group(g)] = o
                    rs_send(1, g, 1, dot(o.reshape(flat, c.cs), s.pq[2]))
                pass_front(1)

        load_g.wait()

        @pl.loop(0, G)
        def _(g):
            v = normed(1, 3, g) + s.u_seg[1, group(g)].astype(F32)
            act, slope = gelu_pair(v)
            o = jnp.where(real_rows(c.cs), act, 0.0).astype(BF16)
            s.out_seg[group(g)] = o
            e = s.g_seg[group(g)].astype(F32) * slope
            s.e3[group(g)] = e
            back_out(1, 3, g, e)
            o32 = o.astype(F32)
            place = lax.broadcasted_iota(jnp.int32, (GM, R, c.cs), 1)
            for n in range(c.images):
                here = (place >= n * SIDE * SIDE) & (place < (n + 1) * SIDE * SIDE)
                mean = jnp.sum(jnp.where(here, o32, 0.0), axis=1, keepdims=True) / float(SIDE * SIDE)
                for m in range(GM):
                    s.pool[(g * GM + m) * c.images + n] = mean[m]

        out_copy = pltpu.make_async_copy(s.out_seg, bo_out, s.out_r.at[0])
        out_copy.start()
        tail.append(out_copy.wait)

        banks = ND * c.bank
        which = lax.broadcasted_iota(jnp.int32, (banks, c.cs), 0)
        term = jnp.zeros((banks, c.cs), F32)
        for n in range(M * c.images):
            ids = jnp.concatenate([ids_ref[n : n + 1, :]] * (c.cs // LANES), axis=1)
            term = term + jnp.where(which == ids, s.pool[n], 0.0)
        s.bank_put[...] = term.reshape(ND, c.bank, c.cs)

        @pl.loop(1, ND)
        def _(i):
            d = dp_peer(i)
            remote(s.bank_put.at[d], s.bank_got.at[me_d], s.bank_s.at[0], s.bank_r.at[0], me_p, d).start()

        tail.append(lambda: take_send(s.bank_got.at[pl.ds(0, ND - 1)], s.bank_s.at[0], s.bank_r.at[0]))

        s.bank_got[me_d] = s.bank_put[me_d]

        def all_rows(ref):
            return ref[...].reshape(M * R, ref.shape[-1])

        def all_seg(ref):
            return jnp.concatenate([ref[j].reshape(M * R, LANES) for j in range(NP)], axis=1)

        def grad_q(k):
            h = all_seg(s.h2.at[k])
            s.gp[2 * k + 1] = dot_tn(all_rows(s.da3.at[k]), h).astype(BF16)

        def grad_p0():
            d = s.da1[0, shard(0, me_p)].reshape(M * R, LANES)
            s.g0[...] = dot_tn(all_rows(s.u_all), d).astype(BF16)

        def grad_p(k):
            d = all_seg(s.da1.at[k])
            s.gp[2 * k] = dot_tn(all_rows(s.u_seg.at[k]), d).astype(BF16)

        def grad_w(k):
            h = all_seg(s.h1.at[k])
            d = s.da2[k, shard(k, me_p)].astype(F32)
            for t0 in range(0, TAPS, 2):
                taps = [t for t in (t0, t0 + 1) if t < TAPS]
                cols = []
                for t in taps:
                    part = (d * s.mask[t][None]).reshape(M * R, LANES)
                    by = tap_shift(t) % (M * R)
                    cols.append((part if by == 0 else pltpu.roll(part, by, 0)).astype(BF16))
                v = dot_tn(h, cols[0] if len(cols) == 1 else jnp.concatenate(cols, axis=1))
                for n, t in enumerate(taps):
                    s.gw[k, t * c.mid : (t + 1) * c.mid, :] = v[:, n * LANES : (n + 1) * LANES].astype(BF16)

        def part(base, n):
            return pl.ds(pl.multiple_of(base, 16), n)

        inner = (me_z == 1) | (me_z == 2)
        z_side = lax.div(me_z, 2)
        outer_dev = 2 * (3 * z_side) + me_c
        inner_dev = 2 * (1 + z_side) + me_c
        across_dev = 2 * (2 - z_side) + me_c

        def job_own(job):
            kind, k, n, base, slot = c.jobs[job]
            ref = s.g0 if kind == "0" else s.gw.at[k] if kind == "w" else s.gp.at[2 * k + (kind == "q")]
            return ref, base

        def job_ref(name, job):
            kind, k, n, base, slot = c.jobs[job]
            return getattr(s, name + ("p" if kind in "pq" else kind)).at[slot]

        def job_core(job):
            own, base = job_own(job)
            n = c.jobs[job][2]
            view = own.at[part(base + (1 - me_c) * n, n)]
            remote(view, job_ref("ja", job), s.gs.at[job, 0], s.gr.at[job, 0], me_p, sib).start()

        def job_in(job):
            own, base = job_own(job)
            n = c.jobs[job][2]
            got, tot = job_ref("ja", job), job_ref("jb", job)
            take_recv(got, s.gs.at[job, 0], s.gr.at[job, 0])
            tot[...] = (got[...].astype(F32) + own[part(base + me_c * n, n), :].astype(F32)).astype(BF16)

            @pl.when(jnp.logical_not(inner))
            def _():
                remote(tot, job_ref("jc", job), s.gs.at[job, 1], s.gr.at[job, 1], me_p, inner_dev).start()

        def job_halve(job):
            n = c.jobs[job][2]
            got, tot, half = job_ref("jc", job), job_ref("jb", job), job_ref("jd", job)

            @pl.when(inner)
            def _():
                take_recv(got, s.gs.at[job, 1], s.gr.at[job, 1])
                tot[...] = (got[...].astype(F32) + tot[...].astype(F32)).astype(BF16)
                view = tot.at[part((1 - z_side) * (n // 2), n // 2)]
                remote(view, half, s.gs.at[job, 2], s.gr.at[job, 2], me_p, across_dev).start()

        def job_sum(job):
            n = c.jobs[job][2]
            tot, half, fin = job_ref("jb", job), job_ref("jd", job), job_ref("je", job)
            mine = part(z_side * (n // 2), n // 2)

            @pl.when(inner)
            def _():
                take_recv(half, s.gs.at[job, 2], s.gr.at[job, 2])
                fin[mine, :] = (half[...].astype(F32) + tot[mine, :].astype(F32)).astype(BF16)
                view = fin.at[mine]
                remote(view, view, s.gs.at[job, 3], s.gr.at[job, 3], me_p, across_dev).start()
                remote(view, view, s.gs.at[job, 4], s.gr.at[job, 3], me_p, outer_dev).start()

        def job_out(job):
            n = c.jobs[job][2]
            fin = job_ref("je", job)
            view = fin.at[part((1 - z_side) * (n // 2), n // 2)]

            @pl.when(inner)
            def _():
                take_recv(view, s.gs.at[job, 3], s.gr.at[job, 3])
                remote(view, view, s.gs.at[job, 5], s.gr.at[job, 4], me_p, outer_dev).start()

        def job_place(job, p, core):
            kind, k, n, base, slot = c.jobs[job]
            if kind == "0":
                return s.p0_out.at[shard(0, p), part(base + core * n, n)]
            if kind == "w":
                return s.w_out.at[lax.div(p, 2) if k == 0 else 1 - lax.div(p, 2), part(base + core * n, n)]
            return s.p_out.at[part(p * 2 * n + core * n, n)]

        def job_home(job, p):
            kind, k = c.jobs[job][:2]
            return 2 * k + lax.rem(p, 2) if kind == "w" else jnp.int32(2 * k + (kind == "q"))

        def job_holds(job):
            kind, k = c.jobs[job][:2]
            return me_y == k if kind == "w" else me_p == 2 * k + (kind == "q")

        def job_plane(job):
            n = c.jobs[job][2]
            fin = job_ref("je", job)

            @pl.when(jnp.logical_not(inner))
            def _():
                for step in (3, 4):
                    take_recv(fin.at[part(0, n // 2)], s.gs.at[job, step], s.gr.at[job, step])

            home = job_home(job, me_p)

            @pl.when(me_p != home)
            def _():
                remote(fin, job_place(job, me_p, me_c), s.gs.at[job, 6], s.gr.at[job, 5], home, me_d).start()

            @pl.when(me_p == home)
            def _():
                pltpu.make_async_copy(fin, job_place(job, me_p, me_c), s.own_s.at[job]).start()

        def job_many(job, count):
            kind, k, n, base, slot = c.jobs[job]
            if kind == "0":
                return s.p0_out.at[pl.ds(0, count), pl.ds(0, n)]
            return s.w_out.at[pl.ds(0, count), pl.ds(0, n)] if kind == "w" else s.p_out.at[pl.ds(0, n * count)]

        def job_share(job):
            fin = job_ref("je", job)
            from_pipes = [0, 2] if c.jobs[job][0] == "w" else [0, 1, 2, 3]

            @pl.when(job_holds(job))
            def _():
                pltpu.make_async_copy(fin, job_place(job, me_p, me_c), s.own_s.at[job]).wait()
                take_recv(job_many(job, len(from_pipes) - 1), s.gs.at[job, 6], s.gr.at[job, 5])
                for i in from_pipes:
                    view = job_place(job, pipe_peer(i), me_c)
                    remote(view, view, s.fin_s.at[job], s.fin_r.at[job], me_p, sib).start()

        def job_end(job):
            got, half, fin = job_ref("ja", job), job_ref("jd", job), job_ref("je", job)
            take_send(got, s.gs.at[job, 0], s.gr.at[job, 0])

            @pl.when(inner)
            def _():
                for step in (2, 3, 4, 5):
                    take_send(half, s.gs.at[job, step], s.gr.at[job, 2])

            @pl.when(jnp.logical_not(inner))
            def _():
                take_send(got, s.gs.at[job, 1], s.gr.at[job, 1])

            @pl.when(me_p != job_home(job, me_p))
            def _():
                take_send(fin, s.gs.at[job, 6], s.gr.at[job, 5])

            @pl.when(job_holds(job))
            def _():
                view = job_many(job, 2 if c.jobs[job][0] == "w" else NP)
                take_recv(view, s.fin_s.at[job], s.fin_r.at[job])
                take_send(view, s.fin_s.at[job], s.fin_r.at[job])

        steps = (job_core, job_in, job_halve, job_sum, job_out, job_plane, job_share)
        next_step = dict.fromkeys(c.jobs, 0)

        def advance(*jobs):
            if c.deep:
                for job in jobs:
                    if next_step[job] < len(steps):
                        steps[next_step[job]](job)
                        next_step[job] += 1

        def point(k, n):
            advance(*POINTS[(1 - k) * 6 + n])

        for k in (1, 0):
            side = 2 * (1 - k)

            @pl.loop(0, G)
            def _(g):
                grad = back_in(k, 3, g, s.e3[group(g)])
                s.da3[k, group(g)] = grad
                rs_send(2 + (1 - k), g, k, dot(grad.reshape(flat, c.cs), s.pq[2 * k + 1]))
            if k == 1:
                pass_back(1)
            else:
                pass_back(0)

            grad_q(k)
            if k == 1:
                pass_proj(0)
            point(k, 0)

            @pl.loop(0, G)
            def _(g):
                up = rs_take(2 + (1 - k), g, k) * s.d2[k, group(g)]
                s.t1[group(g)] = up
                back_out(k, 2, g, up)
            point(k, 1)

            @pl.loop(0, G)
            def _(g):
                mine = shard(k, me_p)
                s.da2[k, mine, group(g)] = back_in(k, 2, g, s.t1[group(g)])
                ag_send(4 + side, g, s.da2.at[k], mine)

            need_back(k)
            grad_w(k)
            point(k, 2)

            @pl.loop(0, G)
            def _(g):
                up = conv_back(k, ag_take(4 + side, g, s.da2.at[k])) * s.d1[k, group(g)]
                s.t1[group(g)] = up
                back_out(k, 1, g, up)
            point(k, 3)

            @pl.loop(0, G)
            def _(g):
                mine = shard(k, me_p)
                s.da1[k, mine, group(g)] = back_in(k, 1, g, s.t1[group(g)])
                ag_send(5 + side, g, s.da1.at[k], mine)
            if k == 0:
                grad_p0()
            point(k, 4)

            if k == 0:
                need_proj(0)
            @pl.loop(0, G)
            def _(g):
                d = dot_nt(ag_take(5 + side, g, s.da1.at[k]), s.pq[2 * k])
                d = d.reshape(GM, R, c.cs) + s.e3[group(g)]
                if k == 1:
                    e = d * s.d3[0, group(g)]
                    s.e3[group(g)] = e
                    back_out(0, 3, g, e)
                else:
                    s.in_seg[group(g)] = d.astype(BF16)

            if k == 1 or not c.deep:
                grad_p(k)
            point(k, 5)

        in_copy = pltpu.make_async_copy(s.in_seg, ig_out, s.out_r.at[1])
        in_copy.start()
        tail.append(in_copy.wait)
        view = s.norm_sum.at[me_p]
        for i in range(1, NP):
            remote(view, view, s.ns_s.at[0], s.ns_r.at[0], pipe_peer(i), me_d).start()
        tail.append(lambda: take_send(s.norm_sum.at[pl.ds(0, NP - 1)], s.ns_s.at[0], s.ns_r.at[0]))

        if c.deep:
            while min(next_step.values()) < len(steps):
                advance(*LAST)
            ends.extend(functools.partial(job_end, job) for job in c.jobs)

        take_recv(s.bank_got.at[pl.ds(0, ND - 1)], s.bank_s.at[0], s.bank_r.at[0])
        tot = s.bank_got[0]
        for d in range(1, ND):
            tot = tot + s.bank_got[d]
        mb_out[...] = tot
        take_recv(s.norm_sum.at[pl.ds(0, NP - 1)], s.ns_s.at[0], s.ns_r.at[0])
        per = c.mid // LANES
        wide = c.cs // LANES
        each = (2 * per + c.ch // LANES) // NP
        for k in range(2):
            for n in range(each):
                q = me_p * each + n
                in_one = q < per
                in_two = (q >= per) & (q < 2 * per)
                sh = jnp.where(in_one, q, q - per)
                half = lax.rem(sh + k, 2)
                small = 2 * half + lax.div(sh, 2)
                far = q - 2 * per
                p = jnp.where(q < 2 * per, small, lax.div(far, wide))
                chunk = jnp.where(in_one, 0, jnp.where(in_two, 1, 2 + lax.rem(far, wide)))
                ns_out[n, 2 * k : 2 * k + 2, :] = s.norm_sum[p, chunk, 2 * k : 2 * k + 2, :]

    work()

    for wait in ends:
        wait()
    if c.deep:
        copies = [
            pltpu.make_async_copy(s.w_out.at[h], gw_out.at[:, pl.ds(h * LANES, LANES)], s.out_r.at[2 + h]) for h in range(2)
        ]
        wide = [
            pltpu.make_async_copy(s.p0_out.at[j], gp_out.at[:, pl.ds(j * LANES, LANES)], s.out_r.at[4 + j])
            for j in range(NP)
        ]
        tall = pltpu.make_async_copy(s.p_out, gp_out, s.out_r.at[4])
        for copy in copies:
            copy.start()
        for act in ("start", "wait"):

            @pl.when(me_p == 0)
            def _():
                for copy in wide:
                    getattr(copy, act)()

            @pl.when(me_p != 0)
            def _():
                getattr(tall, act)()

    else:
        copies = [
            pltpu.make_async_copy(s.gp, gp_out, s.out_r.at[2]),
            pltpu.make_async_copy(s.gw, gw_out, s.out_r.at[3]),
        ]
        for copy in copies:
            copy.start()
    front_send().wait_send()
    for i in range(NP):
        end_proj(i)
    for k in range(2):
        end_front(k)
        end_back(k)

    @pl.loop(0, G)
    def _(g):
        for wait in [*due.values(), *owed.values()]:
            wait(g)

        @pl.when(me_p == 0)
        def _():
            take_send(s.put.at[0, pl.ds(0, NP - 1), group(g)], s.rs_s.at[0, g], s.rs_r.at[0, g])

    for wait in tail:
        wait()
    for copy in copies:
        copy.wait()


def on_device(mesh, block_input, proj_weight, spatial_weight, norm_gain, norm_shift, output_grad, image_ids):
    bank = 8
    c = Sizes(mesh, block_input, proj_weight, spatial_weight, bank)
    extra = ((0, 0), (0, c.pad - c.rows), (0, 0))
    u = jnp.pad(block_input, extra)
    go = jnp.pad(output_grad, extra)
    sw = spatial_weight.reshape(TAPS, c.mid, spatial_weight.shape[2])
    ids = jnp.broadcast_to(image_ids.reshape(-1, 1), (image_ids.size, LANES))
    items = scratch_list(c)
    names = [n for n, _ in items]
    anyspec = pl.BlockSpec(memory_space=pl.ANY)
    vspec = pl.BlockSpec(memory_space=pltpu.VMEM)
    if c.deep:
        gp_shape, gw_shape = (c.ch, c.mid), (TAPS * c.mid, 2 * LANES)
    else:
        gp_shape, gw_shape = (c.pipes, c.cs, c.mid), (2, TAPS * c.mid, LANES)
    each = (2 * c.mid + c.ch) // LANES // c.pipes
    outs = pl.pallas_call(
        functools.partial(body, c, names),
        out_shape=(
            jax.ShapeDtypeStruct((c.micro, c.pad, c.cs), BF16),
            jax.ShapeDtypeStruct((c.micro, c.pad, c.cs), BF16),
            jax.ShapeDtypeStruct(gp_shape, BF16),
            jax.ShapeDtypeStruct(gw_shape, BF16),
            jax.ShapeDtypeStruct((each, 4, LANES), F32),
            jax.ShapeDtypeStruct((bank, c.cs), F32),
        ),
        in_specs=[anyspec] * 4 + [vspec] * 3,
        out_specs=(anyspec, anyspec, anyspec, anyspec, vspec, vspec),
        scratch_shapes=[v for _, v in items],
        compiler_params=pltpu.CompilerParams(collective_id=0, has_side_effects=True, vmem_limit_bytes=60 << 20),
    )(u, go, proj_weight[0], sw, norm_gain, norm_shift, ids)
    bo, ig, gp, gw, ns, mb = outs
    if not c.deep:
        gp = lax.psum(gp.astype(F32), "dp")
        gw = lax.psum(gw.astype(F32), "dp")
        gp = lax.all_to_all(gp, "pipe", 0, 0, tiled=True).reshape(c.ch, c.mid)
        gw = lax.all_gather(gw, "pipe")
        me = lax.axis_index("pipe")
        y, x = me // 2, me % 2
        near = lax.dynamic_index_in_dim(gw, me, 0, keepdims=False)
        far = lax.dynamic_index_in_dim(gw, 2 * (1 - y) + x, 0, keepdims=False)
        gw = jnp.concatenate(
            [lax.dynamic_index_in_dim(near, y, 0, keepdims=False), lax.dynamic_index_in_dim(far, y, 0, keepdims=False)],
            axis=1,
        )
    ns = jnp.transpose(ns.reshape(each, 2, 2, LANES), (2, 1, 0, 3)).reshape(2, 2, each * LANES)
    return (
        bo[:, : c.rows],
        ig[:, : c.rows],
        gp.astype(F32)[None],
        gw.astype(F32)[None],
        ns[0],
        ns[1],
        mb,
    )


def solution(mesh):
    return jax.shard_map(
        functools.partial(on_device, mesh),
        mesh=mesh,
        in_specs=(
            P(None, "dp", None),
            P("pipe", None, None),
            P("pipe", None, None),
            P(),
            P(),
            P(None, "dp", None),
            P(None, "dp"),
        ),
        out_specs=(
            P(None, "dp", "pipe"),
            P(None, "dp", "pipe"),
            P("pipe", None, None),
            P("pipe", None, None),
            P(None, "pipe"),
            P(None, "pipe"),
            P("dp", "pipe"),
        ),
        check_vma=False,
    )
```

time: 332 us -> 221 us (0.67)
  Pallas kernels: 311 us -> 201 us
    pallas_call x1, Pallas kernels: 311 us -> 201 us  [on_device(): pl.pallas_call(functools.partial(body, c, names), out_shape=(jax.ShapeDty...]
where the time goes in v2:
time: 221 us; the launch traced here: 220 us
  Pallas kernels  201 us (91%)
  local copies, waits for them, and re-layouts  11.4 us (5%)
  other arithmetic  6.97 us (3%)
    pallas_call x1, Pallas kernels, on_device(): pl.pallas_call(functools.partial(body, c, names), out_shape=(jax.ShapeDty...  201 us
    unnamed x19, local copies, waits for them, and re-layouts  6.45 us

profile of v2, /device:TPU:0, one launch (start us, length us, event | category | flops | bytes accessed | tf_op | source)
XLA Modules:
  0.0 220.3 jit_solution(10561494990304972326)
XLA Ops:
  0.6 2.3 %copy.21 = bf16[4,98,2048]{2,1,0:T(8,128)(2,1)S(1)} copy(bf16[4,98,2048]{2,0,1:T(4,128)(2,1)} %param.7) | data formatting | bytes 3211264 | tf_op args[0]
  2.9 0.0 copy-start.1
  3.0 1.4 pad.7.refs_0_
  4.4 0.6 copy-done.1
  5.0 0.9 copy.22
  5.9 0.0 copy-start.5
  5.9 1.4 pad.8.refs_1_
  7.3 0.0 copy-done.5
  7.3 0.1 copy.23
  7.4 0.1 broadcast_in_dim.19
  7.5 0.7 broadcast_in_dim.20.refs_6_
  8.2 201.2 %shard_map.126 = (bf16[4,112,512]{2,1,0:T(8,128)(2,1)}, bf16[4,112,512]{2,1,0:T(8,128)(2,1)}, bf16[2048,512]{1,0:T(8,128)(2,1)}, bf16[4608,256]{1,0:T(8,128)(2,1...) custom-call(bf16[4,112,2048]{2,1,0:T(8,128)(2,1)} %pad.7.refs_0_, bf16[4,112,2048]{2,1,0:T(8,128)(2,1)} %pad.8.refs_1_, ...), custom_call_target="tpu_custom_call" | custom-call | tf_op jit(solution)/shard_map/pallas_call | solution.py:1036
  209.4 0.7 copy.32
  210.1 0.6 copy_bitcast_fusion.1
  210.7 0.0 copy-start
  210.7 4.4 %bitcast_convert_fusion = f32[1,4608,256]{2,1,0:T(8,128)} fusion(bf16[4608,256]{1,0:T(8,128)(2,1)} %get-tuple-element.16), kind=kLoop, calls=%fused_computation | loop fusion | flops 1179648 | bytes 7077888 | tf_op jit(solution)/shard_map/broadcast_in_dim | solution.py:1070
  215.1 0.0 copy-done
  215.1 0.0 copy-start.3
  215.1 0.0 copy-start.2
  215.1 2.6 %bitcast_convert_fusion.1 = f32[1,2048,512]{2,1,0:T(8,128)} fusion(bf16[2048,512]{1,0:T(8,128)(2,1)S(1)} %copy-done), kind=kLoop, calls=%fused_computation.1 | loop fusion | flops 1048576 | bytes 6291456 | tf_op jit(solution)/shard_map/broadcast_in_dim | solution.py:1069
  217.7 0.0 copy-start.4
  217.7 0.0 copy-done.3
  217.7 1.0 copy.25
  218.7 0.0 copy-done.2
  218.7 1.0 copy.26
  219.7 0.0 copy-done.4
  219.7 0.6 copy.34
  (3 shorter events, 0.1 us)
Async XLA Ops:
  2.9 2.1 copy-start.1
  5.9 1.4 copy-start.5
  210.7 4.4 %copy-start = (bf16[2048,512]{1,0:T(8,128)(2,1)S(1)}, bf16[2048,512]{1,0:T(8,128)(2,1)}, u32[]{:S(2)}) copy-start(bf16[2048,512]{1,0:T(8,128)(2,1)} %get-tuple-element.15) | copy-start | bytes 6291460
  215.1 2.6 %copy-start.3 = (bf16[4,112,512]{2,1,0:T(8,128)(2,1)S(1)}, bf16[4,112,512]{2,1,0:T(8,128)(2,1)}, u32[]{:S(2)}) copy-start(bf16[4,112,512]{2,1,0:T(8,128)(2,1)} %get-tuple-element.13) | copy-start | bytes 1376260
  215.1 3.6 %copy-start.2 = (bf16[4,112,512]{2,1,0:T(8,128)(2,1)S(1)}, bf16[4,112,512]{2,1,0:T(8,128)(2,1)}, u32[]{:S(2)}) copy-start(bf16[4,112,512]{2,1,0:T(8,128)(2,1)} %get-tuple-element.14) | copy-start | bytes 1376260
  217.7 2.0 copy-start.4

commit v3 on v2

--- a/solution.py
+++ b/solution.py
@@ -19,18 +19,18 @@
 POINTS = (
     (0,),
     (0,),
-    (1, 2, 3),
     (0, 1, 2, 3),
-    (0,),
-    (4, 0, 1),
-    (5, 4, 0, 1, 2),
-    (5, 1, 2, 3),
-    (6, 7, 8, 4, 0, 1, 2, 3),
-    (5, 6, 7, 8, 4, 2, 3),
-    (9, 10, 5, 4, 1, 3),
-    (9, 10, 6, 5, 4, 2),
+    (0, 1, 2),
+    (0, 1),
+    (1, 2, 3, 4),
+    (0, 1, 2, 3, 4, 5),
+    (2, 3, 4, 5),
+    (6, 7, 8, 1, 2, 3, 4, 5),
+    (6, 7, 8, 5, 4),
+    (9, 10, 6, 5, 3, 4),
+    (9, 10, 6, 7, 8, 5),
 )
-LAST = (5, 6, 4, 3, 7, 9, 8, 10)
+LAST = (0, 1, 2, 5, 6, 7, 8, 9, 10, 4, 3)
 MESH = pl.DeviceIdType.MESH
 F32 = jnp.float32
 BF16 = jnp.bfloat16
@@ -98,7 +98,6 @@
         ("p_own", pltpu.VMEM((c.ch, c.mid), BF16)),
         ("pq", pltpu.VMEM((c.pipes, c.cs, c.mid), BF16)),
         ("wf", pltpu.VMEM((2, TAPS, c.mid, LANES), BF16)),
-        ("wb", pltpu.VMEM((2, 4, TAPS, LANES, LANES), BF16)),
         ("sw", pltpu.VMEM((2, TAPS, c.mid, LANES), BF16)),
         ("mask", pltpu.VMEM((TAPS, c.pad, LANES), F32)),
         ("z1", pltpu.VMEM((2,) + full + (LANES,), F32)),
@@ -115,11 +114,11 @@
         ("h1", pltpu.VMEM((2,) + seg, BF16)),
         ("h2", pltpu.VMEM((2,) + seg, BF16)),
         ("da3", pltpu.VMEM((2,) + full + (c.cs,), BF16)),
-        ("da2", pltpu.VMEM((2,) + seg, BF16)),
+        ("dcol", pltpu.VMEM((2,) + full + (TAPS * LANES,), BF16)),
         ("da1", pltpu.VMEM((2,) + seg, BF16)),
         ("first", pltpu.VMEM(full + (LANES,), BF16)),
-        ("put", pltpu.VMEM((4,) + seg, BF16)),
-        ("got", pltpu.VMEM((4,) + seg, BF16)),
+        ("put", pltpu.VMEM((6,) + seg, BF16)),
+        ("got", pltpu.VMEM((6,) + seg, BF16)),
         ("out_seg", pltpu.VMEM(full + (c.cs,), BF16)),
         ("in_seg", pltpu.VMEM(full + (c.cs,), BF16)),
         ("ar_small", pltpu.VMEM((8, c.dps, c.micro, 2, LANES), F32)),
@@ -135,16 +134,13 @@
         ("ar_r", pltpu.SemaphoreType.DMA((12, c.groups))),
         ("ag_s", pltpu.SemaphoreType.DMA((8, c.groups))),
         ("ag_r", pltpu.SemaphoreType.DMA((8, c.groups))),
-        ("rs_s", pltpu.SemaphoreType.DMA((4, c.groups))),
-        ("rs_r", pltpu.SemaphoreType.DMA((4, c.groups))),
-        ("w_s", pltpu.SemaphoreType.DMA((3, c.pipes))),
-        ("pass_s", pltpu.SemaphoreType.DMA((3, c.pipes))),
-        ("pq_r", pltpu.SemaphoreType.DMA((c.pipes,))),
-        ("pq_q", pltpu.SemaphoreType.DMA((c.pipes,))),
-        ("wf_r", pltpu.SemaphoreType.DMA((2,))),
-        ("wf_q", pltpu.SemaphoreType.DMA((2,))),
-        ("wb_r", pltpu.SemaphoreType.DMA((2, 2))),
-        ("wb_q", pltpu.SemaphoreType.DMA((2, 2))),
+        ("rs_s", pltpu.SemaphoreType.DMA((6, c.groups))),
+        ("rs_r", pltpu.SemaphoreType.DMA((6, c.groups))),
+        ("w_s", pltpu.SemaphoreType.DMA((2, c.pipes))),
+        ("pass_s", pltpu.SemaphoreType.DMA((6, 3))),
+        ("w_r", pltpu.SemaphoreType.DMA((6,))),
+        ("w_z", pltpu.SemaphoreType.DMA((6,))),
+        ("w_q", pltpu.SemaphoreType.DMA((6,))),
         ("bank_s", pltpu.SemaphoreType.DMA((1,))),
         ("bank_r", pltpu.SemaphoreType.DMA((1,))),
         ("ns_s", pltpu.SemaphoreType.DMA((1,))),
@@ -258,135 +254,102 @@
     me_z = lax.div(me_d, 2)
     sib = me_d + 1 - 2 * me_c
 
-    def rows_of(p):
-        return pl.ds(pl.multiple_of(p * c.cs, 16), c.cs)
-
-    def half_of(n, which):
-        return pl.ds(pl.multiple_of(which * (n // 2), 16), n // 2)
-
-    def proj_half(i, core):
-        return s.pq.at[i, half_of(c.cs, core)]
+    def link_peer(i):
+        flip = me_p + 1 - 2 * me_x
+        return (None, flip, lax.rem(me_p + 2, NP), lax.rem(flip + 2, NP))[i]
+
+    def on_pipes(*pipes):
+        here = me_p == pipes[0]
+        for p in pipes[1:]:
+            here = here | (me_p == p)
+        return pl.when(here)
+
+    me_l = lax.rem(me_z, 2)
+    low = 2 * (me_z + 1 - 2 * me_l) + me_c
+
+    def quarter(part, core, z):
+        if part < 4:
+            return s.pq.at[part, pl.ds(pl.multiple_of((2 * core + z) * (c.cs // 4), 16), c.cs // 4)]
+        return s.wf.at[part - 4, :, pl.ds(pl.multiple_of((2 * core + z) * (c.mid // 4), 16), c.mid // 4)]
+
+    def whole_part(part, core):
+        if part < 4:
+            return s.pq.at[part] if core is None else s.pq.at[part, pl.ds(pl.multiple_of(core * (c.cs // 2), 16), c.cs // 2)]
+        rows = pl.ds(0, c.mid) if core is None else pl.ds(pl.multiple_of(core * (c.mid // 2), 16), c.mid // 2)
+        return s.wf.at[part - 4, :, rows]
+
+    def here_already(part):
+        return me_p == part if part < 4 else me_y == part - 4
 
     def proj_send(i):
-        p = pipe_peer(i)
-        src = pw_hbm.at[pl.ds(pl.multiple_of(p * c.cs + me_c * (c.cs // 2), 16), c.cs // 2)]
-        return remote(src, proj_half(me_p, me_c), s.w_s.at[0, i], s.pq_r.at[me_p], p, me_d)
-
-    def proj_pass(i):
-        view = proj_half(i, me_c)
-        return remote(view, view, s.pass_s.at[0, i], s.pq_q.at[i], me_p, sib)
-
-    def pass_proj(i):
-        @pl.when(me_p != i)
+        p = link_peer(i)
+        n = c.cs // 4
+        base = (2 * me_c + me_l) * n
+        src = pw_hbm.at[pl.ds(pl.multiple_of(p * c.cs + base, 16), n)]
+        dst = s.pq.at[me_p, pl.ds(pl.multiple_of(base, 16), n)]
+        return remote(src, dst, s.w_s.at[0, i], s.w_r.at[me_p], p, me_d)
+
+    def front_send():
+        rows = pl.ds(pl.multiple_of((2 * me_c + me_l) * (c.mid // 4), 16), c.mid // 4)
+        return remote(s.sw.at[1, :, rows], s.wf.at[me_y, :, rows], s.w_s.at[1, 0], s.w_r.at[4 + me_y], link_peer(2), me_d)
+
+    def pass_copies(part):
+        near, far = quarter(part, me_c, me_l), quarter(part, me_c, 1 - me_l)
+        return (
+            remote(near, near, s.pass_s.at[part, 0], s.w_z.at[part], me_p, low),
+            remote(near, near, s.pass_s.at[part, 1], s.w_q.at[part], me_p, sib),
+            remote(far, far, s.pass_s.at[part, 2], s.w_q.at[part], me_p, sib),
+        )
+
+    def pass_one(*parts):
+        for part in parts:
+
+            @pl.when(jnp.logical_not(here_already(part)))
+            def _():
+                take_recv(quarter(part, me_c, me_l), s.pass_s.at[part, 0], s.w_r.at[part])
+                for copy in pass_copies(part)[:2]:
+                    copy.start()
+
+    def pass_two(*parts):
+        for part in parts:
+
+            @pl.when(jnp.logical_not(here_already(part)))
+            def _():
+                take_recv(quarter(part, me_c, 1 - me_l), s.pass_s.at[part, 0], s.w_z.at[part])
+                pass_copies(part)[2].start()
+
+    def need(*parts):
+        for part in parts:
+
+            @pl.when(jnp.logical_not(here_already(part)))
+            def _():
+                take_recv(whole_part(part, 1 - me_c), s.pass_s.at[part, 0], s.w_q.at[part])
+
+            @pl.when(here_already(part))
+            def _():
+                pltpu.make_async_copy(whole_part(part, None), whole_part(part, None), s.w_r.at[part]).wait()
+
+    def end_part(part):
+        @pl.when(jnp.logical_not(here_already(part)))
         def _():
-            take_recv(proj_half(i, me_c), s.pass_s.at[0, i], s.pq_r.at[i])
-            proj_pass(i).start()
-
-    def need_proj(i):
-        @pl.when(me_p != i)
-        def _():
-            take_recv(proj_half(i, 1 - me_c), s.pass_s.at[0, i], s.pq_q.at[i])
-
-        @pl.when(me_p == i)
-        def _():
-            pltpu.make_async_copy(s.pq.at[i], s.pq.at[i], s.pq_r.at[i]).wait()
-
-    def end_proj(i):
-        @pl.when(me_p != i)
-        def _():
-            proj_pass(i).wait_send()
-
-    def front_half(k, core):
-        return s.wf.at[k, :, half_of(c.mid, core)]
-
-    def front_send():
-        return remote(
-            s.sw.at[1, :, half_of(c.mid, me_c)],
-            front_half(me_y, me_c),
-            s.w_s.at[1, 0],
-            s.wf_r.at[me_y],
-            lax.rem(me_p + 2, NP),
-            me_d,
-        )
-
-    def front_pass(k):
-        view = front_half(k, me_c)
-        return remote(view, view, s.pass_s.at[1, k], s.wf_q.at[k], me_p, sib)
-
-    def pass_front(k):
-        @pl.when(me_y != k)
-        def _():
-            take_recv(front_half(k, me_c), s.pass_s.at[1, k], s.wf_r.at[k])
-            front_pass(k).start()
-
-    def need_front(k):
-        @pl.when(me_y != k)
-        def _():
-            take_recv(front_half(k, 1 - me_c), s.pass_s.at[1, k], s.wf_q.at[k])
-
-        @pl.when(me_y == k)
-        def _():
-            pltpu.make_async_copy(s.wf.at[k], s.wf.at[k], s.wf_r.at[k]).wait()
-
-    def end_front(k):
-        @pl.when(me_y != k)
-        def _():
-            front_pass(k).wait_send()
-
-    def back_rows(p):
-        sh = 2 * lax.rem(p, 2) + lax.rem(lax.div(p, 2) + me_y, 2)
-        return pl.ds(pl.multiple_of(sh * LANES, LANES), LANES)
-
-    def back_send(i):
-        p = pipe_peer(i)
-        return remote(
-            s.sw.at[me_c, :, back_rows(p)],
-            s.wb.at[me_y, 2 * me_x + me_c],
-            s.w_s.at[2, i],
-            s.wb_r.at[me_y, me_x],
-            p,
-            me_d,
-        )
-
-    def back_pass(k, e):
-        view = s.wb.at[k, 2 * e + me_c]
-        return remote(view, view, s.pass_s.at[2, 2 * k + e], s.wb_q.at[k, e], me_p, sib)
-
-    def pass_back(k):
-        for e in range(2):
-
-            @pl.when(me_p != 2 * k + e)
-            def _():
-                take_recv(s.wb.at[k, 2 * e + me_c], s.pass_s.at[2, 2 * k + e], s.wb_r.at[k, e])
-                back_pass(k, e).start()
-
-    def need_back(k):
-        for e in range(2):
-
-            @pl.when(me_p != 2 * k + e)
-            def _():
-                take_recv(s.wb.at[k, 2 * e + 1 - me_c], s.pass_s.at[2, 2 * k + e], s.wb_q.at[k, e])
-
-            @pl.when(me_p == 2 * k + e)
-            def _():
-                view = s.wb.at[k, pl.ds(2 * e, 2)]
-                pltpu.make_async_copy(view, view, s.wb_r.at[k, e]).wait()
-
-    def end_back(k):
-        for e in range(2):
-
-            @pl.when(me_p != 2 * k + e)
-            def _():
-                back_pass(k, e).wait_send()
+            for copy in pass_copies(part):
+                copy.wait_send()
 
     for load in load_w:
         load.wait()
-    front_send().start()
-    pltpu.make_async_copy(pw_hbm.at[rows_of(me_p)], s.pq.at[me_p], s.pq_r.at[me_p]).start()
-    pltpu.make_async_copy(s.sw.at[0], s.wf.at[me_y], s.wf_r.at[me_y]).start()
-    pltpu.make_async_copy(
-        s.sw.at[:, :, back_rows(me_p)], s.wb.at[me_y, pl.ds(2 * me_x, 2)], s.wb_r.at[me_y, me_x]
-    ).start()
+
+    @on_pipes(1)
+    def _():
+        front_send().start()
+
+    @on_pipes(2)
+    def _():
+        for i in range(1, NP):
+            proj_send(i).start()
+
+    own_rows = pl.ds(pl.multiple_of(me_p * c.cs, 16), c.cs)
+    pltpu.make_async_copy(pw_hbm.at[own_rows], s.pq.at[me_p], s.w_r.at[me_p]).start()
+    pltpu.make_async_copy(s.sw.at[0], s.wf.at[me_y], s.w_r.at[4 + me_y]).start()
 
     def note(kind, idx, view, ss, rs):
         owed[kind, idx] = lambda g: take_send(view(g), ss.at[idx, g], rs.at[idx, g])
@@ -529,18 +492,13 @@
                 acc = part if acc is None else acc + part
         return acc
 
-    def conv_back(k, d):
-        acc = None
-        for t0 in range(0, TAPS, 2):
-            taps = [t for t in (t0, t0 + 1) if t < TAPS]
-            w = [jnp.concatenate([s.wb[k, o, t] for o in range(4)], axis=1) for t in taps]
-            w = w[0] if len(taps) == 1 else jnp.concatenate(w, axis=0)
-            y = dot_nt(d, w)
-            for n, t in enumerate(taps):
-                part = masked(y[:, n * LANES : (n + 1) * LANES], t).reshape(flat, LANES)
-                part = shifted(part, tap_shift(t))
-                acc = part if acc is None else acc + part
-        return acc.reshape(GM, R, LANES)
+    def conv_back(k, g, d):
+        flat_d = d.astype(F32)
+        for t in range(TAPS):
+            part = shifted((flat_d * s.mask[t][None]).reshape(flat, LANES), tap_shift(t))
+            s.dcol[k, group(g), :, t * LANES : (t + 1) * LANES] = part.astype(BF16).reshape(GM, R, LANES)
+        w = jnp.concatenate([s.wf[k, t] for t in range(TAPS)], axis=1)
+        return dot_nt(s.dcol[k, group(g)].reshape(flat, TAPS * LANES), w)
 
     tail, ends = [], []
 
@@ -562,9 +520,10 @@
                         s.put.at[0, shard(0, jnp.int32(p)), group(g)], s.first.at[group(g)], s.rs_s.at[0, g], s.rs_r.at[0, g], p, me_d
                     ).start()
 
-        for i in range(1, NP):
-            proj_send(i).start()
-            tail.append(proj_send(i).wait_send)
+        @on_pipes(0)
+        def _():
+            front_send().start()
+
 
         for k in range(2):
 
@@ -580,43 +539,61 @@
                 else:
                     a = rs_take(1, g, 1)
                 stats_out(k, 1, g, a)
-            if k == 0:
-                pass_front(0)
+            pass_one(4 if k == 0 else 3)
 
             @pl.loop(0, G)
             def _(g):
                 hidden_out(k, 1, g, 2 * k, s.h1)
-
-            if k == 1:
-                pass_proj(3)
-            need_front(k)
+            if k == 0:
+
+                @on_pipes(2, 3)
+                def _():
+                    front_send().start()
+
+                @on_pipes(1)
+                def _():
+                    for i in range(1, NP):
+                        proj_send(i).start()
+
+            else:
+                pass_two(3)
+
+
+            if k == 0:
+                pass_two(4)
+            need(4 + k)
 
             @pl.loop(0, G)
             def _(g):
                 stats_out(k, 2, g, conv(k, ag_take(2 * k, g, s.h1.at[k])))
             if k == 0:
-                pass_proj(1)
+                pass_one(1, 2)
 
             @pl.loop(0, G)
             def _(g):
                 hidden_out(k, 2, g, 2 * k + 1, s.h2)
-            if k == 1:
-                for i in range(1, NP):
-                    back_send(i).start()
-                    tail.append(back_send(i).wait_send)
-
-            need_proj(2 * k + 1)
+            if k == 0:
+                pass_two(1, 2)
+
+                @on_pipes(3)
+                def _():
+                    for i in range(1, NP):
+                        proj_send(i).start()
+
+
+            need(2 * k + 1)
             if k == 0:
                 load_u.wait()
-                pass_proj(2)
 
             @pl.loop(0, G)
             def _(g):
                 a = dot_nt(ag_take(2 * k + 1, g, s.h2.at[k]), s.pq[2 * k + 1])
                 stats_out(k, 3, g, a.reshape(GM, R, c.cs))
-
             if k == 0:
-                need_proj(2)
+                pass_one(5)
+
+            if k == 0:
+                need(2)
 
                 @pl.loop(0, G)
                 def _(g):
@@ -626,7 +603,7 @@
                     o = jnp.where(real_rows(c.cs), act, 0.0).astype(BF16)
                     s.u_seg[1, group(g)] = o
                     rs_send(1, g, 1, dot(o.reshape(flat, c.cs), s.pq[2]))
-                pass_front(1)
+                pass_two(5)
 
         load_g.wait()
 
@@ -688,15 +665,10 @@
 
         def grad_w(k):
             h = all_seg(s.h1.at[k])
-            d = s.da2[k, shard(k, me_p)].astype(F32)
             for t0 in range(0, TAPS, 2):
                 taps = [t for t in (t0, t0 + 1) if t < TAPS]
-                cols = []
-                for t in taps:
-                    part = (d * s.mask[t][None]).reshape(M * R, LANES)
-                    by = tap_shift(t) % (M * R)
-                    cols.append((part if by == 0 else pltpu.roll(part, by, 0)).astype(BF16))
-                v = dot_tn(h, cols[0] if len(cols) == 1 else jnp.concatenate(cols, axis=1))
+                d = s.dcol[k, :, :, t0 * LANES : (t0 + len(taps)) * LANES].reshape(M * R, len(taps) * LANES)
+                v = dot_tn(h, d)
                 for n, t in enumerate(taps):
                     s.gw[k, t * c.mid : (t + 1) * c.mid, :] = v[:, n * LANES : (n + 1) * LANES].astype(BF16)
 
@@ -708,6 +680,10 @@
         outer_dev = 2 * (3 * z_side) + me_c
         inner_dev = 2 * (1 + z_side) + me_c
         across_dev = 2 * (2 - z_side) + me_c
+        high_dev = 2 * lax.rem(me_z + 2, 4) + me_c
+
+        def halving(job):
+            return c.jobs[job][1] == 0
 
         def job_own(job):
             kind, k, n, base, slot = c.jobs[job]
@@ -730,6 +706,10 @@
             got, tot = job_ref("ja", job), job_ref("jb", job)
             take_recv(got, s.gs.at[job, 0], s.gr.at[job, 0])
             tot[...] = (got[...].astype(F32) + own[part(base + me_c * n, n), :].astype(F32)).astype(BF16)
+            if halving(job):
+                view = tot.at[part((1 - me_l) * (n // 2), n // 2)]
+                remote(view, job_ref("jc", job).at[0 : n // 2], s.gs.at[job, 1], s.gr.at[job, 1], me_p, low).start()
+                return
 
             @pl.when(jnp.logical_not(inner))
             def _():
@@ -738,6 +718,14 @@
         def job_halve(job):
             n = c.jobs[job][2]
             got, tot, half = job_ref("jc", job), job_ref("jb", job), job_ref("jd", job)
+            if halving(job):
+                got, half = got.at[0 : n // 2], half.at[0 : n // 4]
+                take_recv(got, s.gs.at[job, 1], s.gr.at[job, 1])
+                mine = part(me_l * (n // 2), n // 2)
+                tot[mine, :] = (got[...].astype(F32) + tot[mine, :].astype(F32)).astype(BF16)
+                view = tot.at[part(me_l * (n // 2) + (1 - z_side) * (n // 4), n // 4)]
+                remote(view, half, s.gs.at[job, 2], s.gr.at[job, 2], me_p, high_dev).start()
+                return
 
             @pl.when(inner)
             def _():
@@ -749,6 +737,13 @@
         def job_sum(job):
             n = c.jobs[job][2]
             tot, half, fin = job_ref("jb", job), job_ref("jd", job), job_ref("je", job)
+            if halving(job):
+                half = half.at[0 : n // 4]
+                take_recv(half, s.gs.at[job, 2], s.gr.at[job, 2])
+                mine = part(me_l * (n // 2) + z_side * (n // 4), n // 4)
+                fin[mine, :] = (half[...].astype(F32) + tot[mine, :].astype(F32)).astype(BF16)
+                remote(fin.at[mine], fin.at[mine], s.gs.at[job, 3], s.gr.at[job, 3], me_p, high_dev).start()
+                return
             mine = part(z_side * (n // 2), n // 2)
 
             @pl.when(inner)
@@ -762,6 +757,11 @@
         def job_out(job):
             n = c.jobs[job][2]
             fin = job_ref("je", job)
+            if halving(job):
+                take_recv(fin.at[0 : n // 4], s.gs.at[job, 3], s.gr.at[job, 3])
+                view = fin.at[part(me_l * (n // 2), n // 2)]
+                remote(view, view, s.gs.at[job, 4], s.gr.at[job, 4], me_p, low).start()
+                return
             view = fin.at[part((1 - z_side) * (n // 2), n // 2)]
 
             @pl.when(inner)
@@ -789,10 +789,14 @@
             n = c.jobs[job][2]
             fin = job_ref("je", job)
 
-            @pl.when(jnp.logical_not(inner))
-            def _():
-                for step in (3, 4):
-                    take_recv(fin.at[part(0, n // 2)], s.gs.at[job, step], s.gr.at[job, step])
+            if halving(job):
+                take_recv(fin.at[0 : n // 2], s.gs.at[job, 4], s.gr.at[job, 4])
+            else:
+
+                @pl.when(jnp.logical_not(inner))
+                def _():
+                    for step in (3, 4):
+                        take_recv(fin.at[0 : n // 2], s.gs.at[job, step], s.gr.at[job, step])
 
             home = job_home(job, me_p)
 
@@ -824,16 +828,21 @@
 
         def job_end(job):
             got, half, fin = job_ref("ja", job), job_ref("jd", job), job_ref("je", job)
+            n = c.jobs[job][2]
             take_send(got, s.gs.at[job, 0], s.gr.at[job, 0])
-
-            @pl.when(inner)
-            def _():
-                for step in (2, 3, 4, 5):
-                    take_send(half, s.gs.at[job, step], s.gr.at[job, 2])
-
-            @pl.when(jnp.logical_not(inner))
-            def _():
-                take_send(got, s.gs.at[job, 1], s.gr.at[job, 1])
+            if halving(job):
+                for step, rows in ((1, n // 2), (2, n // 4), (3, n // 4), (4, n // 2)):
+                    take_send(fin.at[0:rows], s.gs.at[job, step], s.gr.at[job, step])
+            else:
+
+                @pl.when(inner)
+                def _():
+                    for step in (2, 3, 4, 5):
+                        take_send(half, s.gs.at[job, step], s.gr.at[job, 2])
+
+                @pl.when(jnp.logical_not(inner))
+                def _():
+                    take_send(got, s.gs.at[job, 1], s.gr.at[job, 1])
 
             @pl.when(me_p != job_home(job, me_p))
             def _():
@@ -866,14 +875,15 @@
                 grad = back_in(k, 3, g, s.e3[group(g)])
                 s.da3[k, group(g)] = grad
                 rs_send(2 + (1 - k), g, k, dot(grad.reshape(flat, c.cs), s.pq[2 * k + 1]))
-            if k == 1:
-                pass_back(1)
-            else:
-                pass_back(0)
 
             grad_q(k)
             if k == 1:
-                pass_proj(0)
+
+                @on_pipes(0)
+                def _():
+                    for i in range(1, NP):
+                        proj_send(i).start()
+
             point(k, 0)
 
             @pl.loop(0, G)
@@ -881,21 +891,20 @@
                 up = rs_take(2 + (1 - k), g, k) * s.d2[k, group(g)]
                 s.t1[group(g)] = up
                 back_out(k, 2, g, up)
+            if k == 0:
+                pass_two(0)
             point(k, 1)
 
             @pl.loop(0, G)
             def _(g):
-                mine = shard(k, me_p)
-                s.da2[k, mine, group(g)] = back_in(k, 2, g, s.t1[group(g)])
-                ag_send(4 + side, g, s.da2.at[k], mine)
-
-            need_back(k)
+                rs_send(5 - k, g, k, conv_back(k, g, back_in(k, 2, g, s.t1[group(g)])))
+
             grad_w(k)
             point(k, 2)
 
             @pl.loop(0, G)
             def _(g):
-                up = conv_back(k, ag_take(4 + side, g, s.da2.at[k])) * s.d1[k, group(g)]
+                up = rs_take(5 - k, g, k) * s.d1[k, group(g)]
                 s.t1[group(g)] = up
                 back_out(k, 1, g, up)
             point(k, 3)
@@ -910,7 +919,7 @@
             point(k, 4)
 
             if k == 0:
-                need_proj(0)
+                need(0)
             @pl.loop(0, G)
             def _(g):
                 d = dot_nt(ag_take(5 + side, g, s.da1.at[k]), s.pq[2 * k])
@@ -924,6 +933,8 @@
 
             if k == 1 or not c.deep:
                 grad_p(k)
+            if k == 1:
+                pass_one(0)
             point(k, 5)
 
         in_copy = pltpu.make_async_copy(s.in_seg, ig_out, s.out_r.at[1])
@@ -935,8 +946,9 @@
         tail.append(lambda: take_send(s.norm_sum.at[pl.ds(0, NP - 1)], s.ns_s.at[0], s.ns_r.at[0]))
 
         if c.deep:
-            while min(next_step.values()) < len(steps):
-                advance(*LAST)
+            for stop in (len(steps) - 1, len(steps)):
+                while min(next_step.values()) < stop:
+                    advance(*[job for job in LAST if next_step[job] < stop])
             ends.extend(functools.partial(job_end, job) for job in c.jobs)
 
         take_recv(s.bank_got.at[pl.ds(0, ND - 1)], s.bank_s.at[0], s.bank_r.at[0])
@@ -995,11 +1007,10 @@
         for copy in copies:
             copy.start()
     front_send().wait_send()
-    for i in range(NP):
-        end_proj(i)
-    for k in range(2):
-        end_front(k)
-        end_back(k)
+    for i in range(1, NP):
+        proj_send(i).wait_send()
+    for n in range(6):
+        end_part(n)
 
     @pl.loop(0, G)
     def _(g):

time: 221 us -> 207 us (0.937)
  Pallas kernels: 201 us -> 188 us
    pallas_call x1, Pallas kernels: 201 us -> 188 us  [on_device(): pl.pallas_call(functools.partial(body, c, names), out_shape=(jax.ShapeDty...]
where the time goes in v3:
time: 207 us
  Pallas kernels  188 us (91%)
  local copies, waits for them, and re-layouts  11.4 us (6%)
  other arithmetic  6.97 us (3%)
    pallas_call x1, Pallas kernels, on_device(): pl.pallas_call(functools.partial(body, c, names), out_shape=(jax.ShapeDty...  188 us
    unnamed x19, local copies, waits for them, and re-layouts  6.45 us
    broadcast_in_dim x1, other arithmetic, on_device(): gw.astype(F32)[None]  4.37 us

profile of v3, /device:TPU:0, one launch (start us, length us, event | category | flops | bytes accessed | tf_op | source)
XLA Modules:
  0.0 206.8 jit_solution(5600678785560107082)
XLA Ops:
  0.6 2.3 %copy.21 = bf16[4,98,2048]{2,1,0:T(8,128)(2,1)S(1)} copy(bf16[4,98,2048]{2,0,1:T(4,128)(2,1)} %param.7) | data formatting | bytes 3211264 | tf_op args[0]
  2.9 0.0 copy-start.1
  3.0 1.4 pad.7.refs_0_
  4.4 0.6 copy-done.1
  5.0 0.9 copy.22
  5.9 0.0 copy-start.5
  5.9 1.4 pad.8.refs_1_
  7.3 0.0 copy-done.5
  7.3 0.1 copy.23
  7.4 0.1 broadcast_in_dim.19
  7.5 0.7 broadcast_in_dim.20.refs_6_
  8.2 187.7 %shard_map.126 = (bf16[4,112,512]{2,1,0:T(8,128)(2,1)}, bf16[4,112,512]{2,1,0:T(8,128)(2,1)}, bf16[2048,512]{1,0:T(8,128)(2,1)}, bf16[4608,256]{1,0:T(8,128)(2,1...) custom-call(bf16[4,112,2048]{2,1,0:T(8,128)(2,1)} %pad.7.refs_0_, bf16[4,112,2048]{2,1,0:T(8,128)(2,1)} %pad.8.refs_1_, ...), custom_call_target="tpu_custom_call" | custom-call | tf_op jit(solution)/shard_map/pallas_call | solution.py:1047
  195.9 0.7 copy.32
  196.6 0.6 copy_bitcast_fusion.1
  197.2 0.0 copy-start
  197.2 4.4 %bitcast_convert_fusion = f32[1,4608,256]{2,1,0:T(8,128)} fusion(bf16[4608,256]{1,0:T(8,128)(2,1)} %get-tuple-element.16), kind=kLoop, calls=%fused_computation | loop fusion | flops 1179648 | bytes 7077888 | tf_op jit(solution)/shard_map/broadcast_in_dim | solution.py:1081
  201.6 0.0 copy-done
  201.6 0.0 copy-start.3
  201.6 0.0 copy-start.2
  201.6 2.6 %bitcast_convert_fusion.1 = f32[1,2048,512]{2,1,0:T(8,128)} fusion(bf16[2048,512]{1,0:T(8,128)(2,1)S(1)} %copy-done), kind=kLoop, calls=%fused_computation.1 | loop fusion | flops 1048576 | bytes 6291456 | tf_op jit(solution)/shard_map/broadcast_in_dim | solution.py:1080
  204.2 0.0 copy-start.4
  204.2 0.0 copy-done.3
  204.2 1.0 copy.25
  205.2 0.0 copy-done.2
  205.2 1.0 copy.26
  206.2 0.0 copy-done.4
  206.2 0.6 copy.34
  (3 shorter events, 0.1 us)
Async XLA Ops:
  2.9 2.1 copy-start.1
  5.9 1.4 copy-start.5
  197.2 4.4 %copy-start = (bf16[2048,512]{1,0:T(8,128)(2,1)S(1)}, bf16[2048,512]{1,0:T(8,128)(2,1)}, u32[]{:S(2)}) copy-start(bf16[2048,512]{1,0:T(8,128)(2,1)} %get-tuple-element.15) | copy-start | bytes 6291460
  201.6 2.6 %copy-start.3 = (bf16[4,112,512]{2,1,0:T(8,128)(2,1)S(1)}, bf16[4,112,512]{2,1,0:T(8,128)(2,1)}, u32[]{:S(2)}) copy-start(bf16[4,112,512]{2,1,0:T(8,128)(2,1)} %get-tuple-element.13) | copy-start | bytes 1376260
  201.6 3.6 %copy-start.2 = (bf16[4,112,512]{2,1,0:T(8,128)(2,1)S(1)}, bf16[4,112,512]{2,1,0:T(8,128)(2,1)}, u32[]{:S(2)}) copy-start(bf16[4,112,512]{2,1,0:T(8,128)(2,1)} %get-tuple-element.14) | copy-start | bytes 1376260
  204.2 2.0 copy-start.4

commit v4 on v3

--- a/solution.py
+++ b/solution.py
@@ -27,10 +27,10 @@
     (2, 3, 4, 5),
     (6, 7, 8, 1, 2, 3, 4, 5),
     (6, 7, 8, 5, 4),
-    (9, 10, 6, 5, 3, 4),
-    (9, 10, 6, 7, 8, 5),
+    (9, 10, 6, 5),
+    (9, 10, 6, 7, 8, 5, 3, 4),
 )
-LAST = (0, 1, 2, 5, 6, 7, 8, 9, 10, 4, 3)
+LAST = (6, 7, 8, 9, 10, 5, 4, 3, 0, 1, 2)
 MESH = pl.DeviceIdType.MESH
 F32 = jnp.float32
 BF16 = jnp.bfloat16
@@ -338,9 +338,7 @@
     for load in load_w:
         load.wait()
 
-    @on_pipes(1)
-    def _():
-        front_send().start()
+    front_send().start()
 
     @on_pipes(2)
     def _():
@@ -520,10 +518,6 @@
                         s.put.at[0, shard(0, jnp.int32(p)), group(g)], s.first.at[group(g)], s.rs_s.at[0, g], s.rs_r.at[0, g], p, me_d
                     ).start()
 
-        @on_pipes(0)
-        def _():
-            front_send().start()
-
 
         for k in range(2):
 
@@ -539,16 +533,12 @@
                 else:
                     a = rs_take(1, g, 1)
                 stats_out(k, 1, g, a)
-            pass_one(4 if k == 0 else 3)
+            pass_one(*((4, 5) if k == 0 else (3,)))
 
             @pl.loop(0, G)
             def _(g):
                 hidden_out(k, 1, g, 2 * k, s.h1)
             if k == 0:
-
-                @on_pipes(2, 3)
-                def _():
-                    front_send().start()
 
                 @on_pipes(1)
                 def _():
@@ -560,7 +550,7 @@
 
 
             if k == 0:
-                pass_two(4)
+                pass_two(4, 5)
             need(4 + k)
 
             @pl.loop(0, G)
@@ -589,8 +579,6 @@
             def _(g):
                 a = dot_nt(ag_take(2 * k + 1, g, s.h2.at[k]), s.pq[2 * k + 1])
                 stats_out(k, 3, g, a.reshape(GM, R, c.cs))
-            if k == 0:
-                pass_one(5)
 
             if k == 0:
                 need(2)
@@ -603,7 +591,6 @@
                     o = jnp.where(real_rows(c.cs), act, 0.0).astype(BF16)
                     s.u_seg[1, group(g)] = o
                     rs_send(1, g, 1, dot(o.reshape(flat, c.cs), s.pq[2]))
-                pass_two(5)
 
         load_g.wait()
 
@@ -680,10 +667,6 @@
         outer_dev = 2 * (3 * z_side) + me_c
         inner_dev = 2 * (1 + z_side) + me_c
         across_dev = 2 * (2 - z_side) + me_c
-        high_dev = 2 * lax.rem(me_z + 2, 4) + me_c
-
-        def halving(job):
-            return c.jobs[job][1] == 0
 
         def job_own(job):
             kind, k, n, base, slot = c.jobs[job]
@@ -706,11 +689,6 @@
             got, tot = job_ref("ja", job), job_ref("jb", job)
             take_recv(got, s.gs.at[job, 0], s.gr.at[job, 0])
             tot[...] = (got[...].astype(F32) + own[part(base + me_c * n, n), :].astype(F32)).astype(BF16)
-            if halving(job):
-                view = tot.at[part((1 - me_l) * (n // 2), n // 2)]
-                remote(view, job_ref("jc", job).at[0 : n // 2], s.gs.at[job, 1], s.gr.at[job, 1], me_p, low).start()
-                return
-
             @pl.when(jnp.logical_not(inner))
             def _():
                 remote(tot, job_ref("jc", job), s.gs.at[job, 1], s.gr.at[job, 1], me_p, inner_dev).start()
@@ -718,14 +696,6 @@
         def job_halve(job):
             n = c.jobs[job][2]
             got, tot, half = job_ref("jc", job), job_ref("jb", job), job_ref("jd", job)
-            if halving(job):
-                got, half = got.at[0 : n // 2], half.at[0 : n // 4]
-                take_recv(got, s.gs.at[job, 1], s.gr.at[job, 1])
-                mine = part(me_l * (n // 2), n // 2)
-                tot[mine, :] = (got[...].astype(F32) + tot[mine, :].astype(F32)).astype(BF16)
-                view = tot.at[part(me_l * (n // 2) + (1 - z_side) * (n // 4), n // 4)]
-                remote(view, half, s.gs.at[job, 2], s.gr.at[job, 2], me_p, high_dev).start()
-                return
 
             @pl.when(inner)
             def _():
@@ -737,13 +707,6 @@
         def job_sum(job):
             n = c.jobs[job][2]
             tot, half, fin = job_ref("jb", job), job_ref("jd", job), job_ref("je", job)
-            if halving(job):
-                half = half.at[0 : n // 4]
-                take_recv(half, s.gs.at[job, 2], s.gr.at[job, 2])
-                mine = part(me_l * (n // 2) + z_side * (n // 4), n // 4)
-                fin[mine, :] = (half[...].astype(F32) + tot[mine, :].astype(F32)).astype(BF16)
-                remote(fin.at[mine], fin.at[mine], s.gs.at[job, 3], s.gr.at[job, 3], me_p, high_dev).start()
-                return
             mine = part(z_side * (n // 2), n // 2)
 
             @pl.when(inner)
@@ -757,11 +720,6 @@
         def job_out(job):
             n = c.jobs[job][2]
             fin = job_ref("je", job)
-            if halving(job):
-                take_recv(fin.at[0 : n // 4], s.gs.at[job, 3], s.gr.at[job, 3])
-                view = fin.at[part(me_l * (n // 2), n // 2)]
-                remote(view, view, s.gs.at[job, 4], s.gr.at[job, 4], me_p, low).start()
-                return
             view = fin.at[part((1 - z_side) * (n // 2), n // 2)]
 
             @pl.when(inner)
@@ -789,14 +747,10 @@
             n = c.jobs[job][2]
             fin = job_ref("je", job)
 
-            if halving(job):
-                take_recv(fin.at[0 : n // 2], s.gs.at[job, 4], s.gr.at[job, 4])
-            else:
-
-                @pl.when(jnp.logical_not(inner))
-                def _():
-                    for step in (3, 4):
-                        take_recv(fin.at[0 : n // 2], s.gs.at[job, step], s.gr.at[job, step])
+            @pl.when(jnp.logical_not(inner))
+            def _():
+                for step in (3, 4):
+                    take_recv(fin.at[0 : n // 2], s.gs.at[job, step], s.gr.at[job, step])
 
             home = job_home(job, me_p)
 
@@ -828,21 +782,16 @@
 
         def job_end(job):
             got, half, fin = job_ref("ja", job), job_ref("jd", job), job_ref("je", job)
-            n = c.jobs[job][2]
             take_send(got, s.gs.at[job, 0], s.gr.at[job, 0])
-            if halving(job):
-                for step, rows in ((1, n // 2), (2, n // 4), (3, n // 4), (4, n // 2)):
-                    take_send(fin.at[0:rows], s.gs.at[job, step], s.gr.at[job, step])
-            else:
-
-                @pl.when(inner)
-                def _():
-                    for step in (2, 3, 4, 5):
-                        take_send(half, s.gs.at[job, step], s.gr.at[job, 2])
-
-                @pl.when(jnp.logical_not(inner))
-                def _():
-                    take_send(got, s.gs.at[job, 1], s.gr.at[job, 1])
+
+            @pl.when(inner)
+            def _():
+                for step in (2, 3, 4, 5):
+                    take_send(half, s.gs.at[job, step], s.gr.at[job, 2])
+
+            @pl.when(jnp.logical_not(inner))
+            def _():
+                take_send(got, s.gs.at[job, 1], s.gr.at[job, 1])
 
             @pl.when(me_p != job_home(job, me_p))
             def _():

time: 207 us -> 194 us (0.937)
  Pallas kernels: 188 us -> 175 us
    pallas_call x1, Pallas kernels: 188 us -> 175 us  [on_device(): pl.pallas_call(functools.partial(body, c, names), out_shape=(jax.ShapeDty...]
where the time goes in v4:
time: 194 us
  Pallas kernels  175 us (90%)
  local copies, waits for them, and re-layouts  11.4 us (6%)
  other arithmetic  6.97 us (4%)
    pallas_call x1, Pallas kernels, on_device(): pl.pallas_call(functools.partial(body, c, names), out_shape=(jax.ShapeDty...  175 us
    unnamed x19, local copies, waits for them, and re-layouts  6.45 us
    broadcast_in_dim x1, other arithmetic, on_device(): gw.astype(F32)[None]  4.37 us

profile of v4, /device:TPU:0, one launch (start us, length us, event | category | flops | bytes accessed | tf_op | source)
XLA Modules:
  0.0 194.1 jit_solution(12461785367485012636)
XLA Ops:
  0.6 2.3 %copy.21 = bf16[4,98,2048]{2,1,0:T(8,128)(2,1)S(1)} copy(bf16[4,98,2048]{2,0,1:T(4,128)(2,1)} %param.7) | data formatting | bytes 3211264 | tf_op args[0]
  2.9 0.0 copy-start.1
  3.0 1.4 pad.7.refs_0_
  4.4 0.6 copy-done.1
  5.0 0.9 copy.22
  5.9 0.0 copy-start.5
  5.9 1.4 pad.8.refs_1_
  7.3 0.0 copy-done.5
  7.3 0.1 copy.23
  7.4 0.1 broadcast_in_dim.19
  7.5 0.7 broadcast_in_dim.20.refs_6_
  8.2 175.0 %shard_map.126 = (bf16[4,112,512]{2,1,0:T(8,128)(2,1)}, bf16[4,112,512]{2,1,0:T(8,128)(2,1)}, bf16[2048,512]{1,0:T(8,128)(2,1)}, bf16[4608,256]{1,0:T(8,128)(2,1...) custom-call(bf16[4,112,2048]{2,1,0:T(8,128)(2,1)} %pad.7.refs_0_, bf16[4,112,2048]{2,1,0:T(8,128)(2,1)} %pad.8.refs_1_, ...), custom_call_target="tpu_custom_call" | custom-call | tf_op jit(solution)/shard_map/pallas_call | solution.py:996
  183.2 0.7 copy.32
  183.9 0.6 copy_bitcast_fusion.1
  184.5 0.0 copy-start
  184.5 4.4 %bitcast_convert_fusion = f32[1,4608,256]{2,1,0:T(8,128)} fusion(bf16[4608,256]{1,0:T(8,128)(2,1)} %get-tuple-element.16), kind=kLoop, calls=%fused_computation | loop fusion | flops 1179648 | bytes 7077888 | tf_op jit(solution)/shard_map/broadcast_in_dim | solution.py:1030
  188.9 0.0 copy-done
  188.9 0.0 copy-start.3
  188.9 0.0 copy-start.2
  188.9 2.6 %bitcast_convert_fusion.1 = f32[1,2048,512]{2,1,0:T(8,128)} fusion(bf16[2048,512]{1,0:T(8,128)(2,1)S(1)} %copy-done), kind=kLoop, calls=%fused_computation.1 | loop fusion | flops 1048576 | bytes 6291456 | tf_op jit(solution)/shard_map/broadcast_in_dim | solution.py:1029
  191.5 0.0 copy-start.4
  191.5 0.0 copy-done.3
  191.6 1.0 copy.25
  192.5 0.0 copy-done.2
  192.5 1.0 copy.26
  193.5 0.0 copy-done.4
  193.5 0.6 copy.34
  (3 shorter events, 0.1 us)
Async XLA Ops:
  2.9 2.1 %copy-start.1 = (bf16[4,98,2048]{2,0,1:T(4,128)(2,1)S(1)}, bf16[4,98,2048]{2,0,1:T(4,128)(2,1)}, u32[]{:S(2)}) copy-start(bf16[4,98,2048]{2,0,1:T(4,128)(2,1)} %param.12) | copy-start | bytes 4816900
  5.9 1.4 copy-start.5
  184.5 4.4 %copy-start = (bf16[2048,512]{1,0:T(8,128)(2,1)S(1)}, bf16[2048,512]{1,0:T(8,128)(2,1)}, u32[]{:S(2)}) copy-start(bf16[2048,512]{1,0:T(8,128)(2,1)} %get-tuple-element.15) | copy-start | bytes 6291460
  188.9 2.6 %copy-start.3 = (bf16[4,112,512]{2,1,0:T(8,128)(2,1)S(1)}, bf16[4,112,512]{2,1,0:T(8,128)(2,1)}, u32[]{:S(2)}) copy-start(bf16[4,112,512]{2,1,0:T(8,128)(2,1)} %get-tuple-element.13) | copy-start | bytes 1376260
  188.9 3.6 %copy-start.2 = (bf16[4,112,512]{2,1,0:T(8,128)(2,1)S(1)}, bf16[4,112,512]{2,1,0:T(8,128)(2,1)}, u32[]{:S(2)}) copy-start(bf16[4,112,512]{2,1,0:T(8,128)(2,1)} %get-tuple-element.14) | copy-start | bytes 1376260
  191.5 2.0 %copy-start.4 = (f32[8,512]{1,0:T(8,128)S(1)}, f32[8,512]{1,0:T(8,128)}, u32[]{:S(2)}) copy-start(f32[8,512]{1,0:T(8,128)} %get-tuple-element.50) | copy-start | bytes 49156

commit v5 on v4

--- a/solution.py
+++ b/solution.py
@@ -161,6 +161,7 @@
             ("gs", pltpu.SemaphoreType.DMA((count, 7))),
             ("gr", pltpu.SemaphoreType.DMA((count, 6))),
             ("own_s", pltpu.SemaphoreType.DMA((count,))),
+            ("store", pltpu.SemaphoreType.DMA((count, c.pipes))),
             ("fin_s", pltpu.SemaphoreType.DMA((count,))),
             ("fin_r", pltpu.SemaphoreType.DMA((count,))),
         ]
@@ -208,7 +209,7 @@
     lane0 = pl.multiple_of(me_p * c.cs, LANES)
     seg_cols = pl.ds(lane0, c.cs)
     load_u = pltpu.make_async_copy(u_hbm.at[:, :, seg_cols], s.u_seg.at[0], s.in_r.at[0])
-    load_g = pltpu.make_async_copy(go_hbm.at[:, :, seg_cols], s.g_seg, s.in_r.at[1])
+    load_g = pltpu.make_async_copy(go_hbm, s.g_seg, s.in_r.at[1])
     load_all = pltpu.make_async_copy(u_hbm, s.u_all, s.in_r.at[2])
     load_p = pltpu.make_async_copy(pw_hbm, s.p_own, s.in_r.at[3])
     load_w = [
@@ -498,7 +499,7 @@
         w = jnp.concatenate([s.wf[k, t] for t in range(TAPS)], axis=1)
         return dot_nt(s.dcol[k, group(g)].reshape(flat, TAPS * LANES), w)
 
-    tail, ends = [], []
+    tail = []
 
     def work():
         load_all.wait()
@@ -803,6 +804,21 @@
                 take_recv(view, s.fin_s.at[job], s.fin_r.at[job])
                 take_send(view, s.fin_s.at[job], s.fin_r.at[job])
 
+        def job_store(job, act):
+            kind, k, n, base, slot = c.jobs[job]
+            rows = pl.ds(base, 2 * n)
+            if kind == "0":
+                parts = [(s.p0_out.at[j, rows], gp_out.at[rows, pl.ds(j * LANES, LANES)]) for j in range(NP)]
+            elif kind == "w":
+                parts = [(s.w_out.at[h, rows], gw_out.at[rows, pl.ds(h * LANES, LANES)]) for h in range(2)]
+            else:
+                parts = [(s.p_out, gp_out)]
+
+            @pl.when(job_holds(job))
+            def _():
+                for i, (src, dst) in enumerate(parts):
+                    getattr(pltpu.make_async_copy(src, dst, s.store.at[job, i]), act)()
+
         steps = (job_core, job_in, job_halve, job_sum, job_out, job_plane, job_share)
         next_step = dict.fromkeys(c.jobs, 0)
 
@@ -869,6 +885,7 @@
 
             if k == 0:
                 need(0)
+
             @pl.loop(0, G)
             def _(g):
                 d = dot_nt(ag_take(5 + side, g, s.da1.at[k]), s.pq[2 * k])
@@ -894,11 +911,8 @@
             remote(view, view, s.ns_s.at[0], s.ns_r.at[0], pipe_peer(i), me_d).start()
         tail.append(lambda: take_send(s.norm_sum.at[pl.ds(0, NP - 1)], s.ns_s.at[0], s.ns_r.at[0]))
 
-        if c.deep:
-            for stop in (len(steps) - 1, len(steps)):
-                while min(next_step.values()) < stop:
-                    advance(*[job for job in LAST if next_step[job] < stop])
-            ends.extend(functools.partial(job_end, job) for job in c.jobs)
+        while c.deep and min(next_step.values()) < len(steps) - 1:
+            advance(*[job for job in LAST if next_step[job] < len(steps) - 1])
 
         take_recv(s.bank_got.at[pl.ds(0, ND - 1)], s.bank_s.at[0], s.bank_r.at[0])
         tot = s.bank_got[0]
@@ -922,58 +936,44 @@
                 chunk = jnp.where(in_one, 0, jnp.where(in_two, 1, 2 + lax.rem(far, wide)))
                 ns_out[n, 2 * k : 2 * k + 2, :] = s.norm_sum[p, chunk, 2 * k : 2 * k + 2, :]
 
+        def drain():
+            front_send().wait_send()
+            for i in range(1, NP):
+                proj_send(i).wait_send()
+            for n in range(6):
+                end_part(n)
+
+            @pl.loop(0, G)
+            def _(g):
+                for wait in [*due.values(), *owed.values()]:
+                    wait(g)
+
+                @pl.when(me_p == 0)
+                def _():
+                    take_send(s.put.at[0, pl.ds(0, NP - 1), group(g)], s.rs_s.at[0, g], s.rs_r.at[0, g])
+            for wait in tail:
+                wait()
+
+        drain()
+        advance(*c.jobs)
+        if c.deep:
+            for job in c.jobs:
+                job_end(job)
+                job_store(job, "start")
+            for job in c.jobs:
+                job_store(job, "wait")
+
     work()
 
-    for wait in ends:
-        wait()
-    if c.deep:
-        copies = [
-            pltpu.make_async_copy(s.w_out.at[h], gw_out.at[:, pl.ds(h * LANES, LANES)], s.out_r.at[2 + h]) for h in range(2)
-        ]
-        wide = [
-            pltpu.make_async_copy(s.p0_out.at[j], gp_out.at[:, pl.ds(j * LANES, LANES)], s.out_r.at[4 + j])
-            for j in range(NP)
-        ]
-        tall = pltpu.make_async_copy(s.p_out, gp_out, s.out_r.at[4])
-        for copy in copies:
-            copy.start()
-        for act in ("start", "wait"):
-
-            @pl.when(me_p == 0)
-            def _():
-                for copy in wide:
-                    getattr(copy, act)()
-
-            @pl.when(me_p != 0)
-            def _():
-                getattr(tall, act)()
-
-    else:
+    if not c.deep:
         copies = [
             pltpu.make_async_copy(s.gp, gp_out, s.out_r.at[2]),
             pltpu.make_async_copy(s.gw, gw_out, s.out_r.at[3]),
         ]
         for copy in copies:
             copy.start()
-    front_send().wait_send()
-    for i in range(1, NP):
-        proj_send(i).wait_send()
-    for n in range(6):
-        end_part(n)
-
-    @pl.loop(0, G)
-    def _(g):
-        for wait in [*due.values(), *owed.values()]:
-            wait(g)
-
-        @pl.when(me_p == 0)
-        def _():
-            take_send(s.put.at[0, pl.ds(0, NP - 1), group(g)], s.rs_s.at[0, g], s.rs_r.at[0, g])
-
-    for wait in tail:
-        wait()
-    for copy in copies:
-        copy.wait()
+        for copy in copies:
+            copy.wait()
 
 
 def on_device(mesh, block_input, proj_weight, spatial_weight, norm_gain, norm_shift, output_grad, image_ids):
@@ -981,7 +981,8 @@
     c = Sizes(mesh, block_input, proj_weight, spatial_weight, bank)
     extra = ((0, 0), (0, c.pad - c.rows), (0, 0))
     u = jnp.pad(block_input, extra)
-    go = jnp.pad(output_grad, extra)
+    go = lax.dynamic_slice_in_dim(output_grad, lax.axis_index("pipe") * c.cs, c.cs, axis=2)
+    go = jnp.pad(go, extra)
     sw = spatial_weight.reshape(TAPS, c.mid, spatial_weight.shape[2])
     ids = jnp.broadcast_to(image_ids.reshape(-1, 1), (image_ids.size, LANES))
     items = scratch_list(c)

time: 194 us -> 191 us (0.985)
    unnamed x19 -> x21, local copies, waits for them, and re-layouts: 6.45 us -> 5 us
where the time goes in v5:
time: 191 us
  Pallas kernels  174 us (91%)
  local copies, waits for them, and re-layouts  9.54 us (5%)
  other arithmetic  6.97 us (4%)
    pallas_call x1, Pallas kernels, on_device(): pl.pallas_call(functools.partial(body, c, names), out_shape=(jax.ShapeDty...  174 us
    unnamed x21, local copies, waits for them, and re-layouts  5 us
    broadcast_in_dim x1, other arithmetic, on_device(): gw.astype(F32)[None]  4.37 us

profile of v5, /device:TPU:0, one launch (start us, length us, event | category | flops | bytes accessed | tf_op | source)
XLA Modules:
  0.0 190.9 jit_solution(9880339288994715694)
XLA Ops:
  0.6 0.0 copy-start
  0.6 0.0 copy-start.2
  0.7 1.4 copy-done
  2.1 0.2 constant_dynamic-slice_fusion
  2.2 0.1 copy.27
  2.3 0.8 pad.9.refs_1_
  3.1 0.0 copy-done.2
  3.1 0.9 copy.21
  4.0 0.0 copy-start.6
  4.0 1.4 pad.8.refs_0_
  5.5 0.0 copy-done.6
  5.5 0.1 copy.23
  5.6 0.1 broadcast_in_dim.19
  5.6 0.7 broadcast_in_dim.20.refs_6_
  6.3 173.7 %shard_map.126 = (bf16[4,112,512]{2,1,0:T(8,128)(2,1)}, bf16[4,112,512]{2,1,0:T(8,128)(2,1)}, bf16[2048,512]{1,0:T(8,128)(2,1)}, bf16[4608,256]{1,0:T(8,128)(2,1...) custom-call(bf16[4,112,2048]{2,1,0:T(8,128)(2,1)} %pad.8.refs_0_, bf16[4,112,512]{2,1,0:T(8,128)(2,1)} %pad.9.refs_1_, ...), custom_call_target="tpu_custom_call" | custom-call | tf_op jit(solution)/shard_map/pallas_call | solution.py:997
  180.0 0.7 copy.33
  180.7 0.6 copy_bitcast_fusion.1
  181.3 0.0 copy-start.1
  181.3 4.4 %bitcast_convert_fusion = f32[1,4608,256]{2,1,0:T(8,128)} fusion(bf16[4608,256]{1,0:T(8,128)(2,1)} %get-tuple-element.16), kind=kLoop, calls=%fused_computation | loop fusion | flops 1179648 | bytes 7077888 | tf_op jit(solution)/shard_map/broadcast_in_dim | solution.py:1031
  185.7 0.0 copy-done.1
  185.7 0.0 copy-start.4
  185.7 0.0 copy-start.3
  185.7 2.6 %bitcast_convert_fusion.1 = f32[1,2048,512]{2,1,0:T(8,128)} fusion(bf16[2048,512]{1,0:T(8,128)(2,1)S(1)} %copy-done.1), kind=kLoop, calls=%fused_computation.1 | loop fusion | flops 1048576 | bytes 6291456 | tf_op jit(solution)/shard_map/broadcast_in_dim | solution.py:1030
  188.3 0.0 copy-start.5
  188.3 0.0 copy-done.4
  188.3 1.0 copy.25
  189.3 0.0 copy-done.3
  189.3 1.0 copy.26
  190.3 0.0 copy-done.5
  190.3 0.6 copy.35
  (3 shorter events, 0.1 us)
Async XLA Ops:
  0.6 1.4 copy-start
  0.6 2.5 %copy-start.2 = (bf16[4,98,2048]{2,0,1:T(4,128)(2,1)S(1)}, bf16[4,98,2048]{2,0,1:T(4,128)(2,1)}, u32[]{:S(2)}) copy-start(bf16[4,98,2048]{2,0,1:T(4,128)(2,1)} %param.7) | copy-start | bytes 4816900
  4.0 1.4 copy-start.6
  181.3 4.4 %copy-start.1 = (bf16[2048,512]{1,0:T(8,128)(2,1)S(1)}, bf16[2048,512]{1,0:T(8,128)(2,1)}, u32[]{:S(2)}) copy-start(bf16[2048,512]{1,0:T(8,128)(2,1)} %get-tuple-element.15) | copy-start | bytes 6291460
  185.7 2.6 %copy-start.4 = (bf16[4,112,512]{2,1,0:T(8,128)(2,1)S(1)}, bf16[4,112,512]{2,1,0:T(8,128)(2,1)}, u32[]{:S(2)}) copy-start(bf16[4,112,512]{2,1,0:T(8,128)(2,1)} %get-tuple-element.13) | copy-start | bytes 1376260
  185.7 3.6 %copy-start.3 = (bf16[4,112,512]{2,1,0:T(8,128)(2,1)S(1)}, bf16[4,112,512]{2,1,0:T(8,128)(2,1)}, u32[]{:S(2)}) copy-start(bf16[4,112,512]{2,1,0:T(8,128)(2,1)} %get-tuple-element.14) | copy-start | bytes 1376260
  188.3 2.0 %copy-start.5 = (f32[8,512]{1,0:T(8,128)S(1)}, f32[8,512]{1,0:T(8,128)}, u32[]{:S(2)}) copy-start(f32[8,512]{1,0:T(8,128)} %get-tuple-element.50) | copy-start | bytes 49156

commit v6 on v5

--- a/solution.py
+++ b/solution.py
@@ -368,7 +368,7 @@
         @pl.loop(1, ND)
         def _(i):
             view = buf.at[me_d, group(g)]
-            remote(view, view, s.ar_s.at[idx, g], s.ar_r.at[idx, g], me_p, dp_peer(i)).start()
+            remote(view, view, s.ar_s.at[idx, g], s.ar_r.at[idx, g], me_p, me_d ^ (ND - i)).start()
 
         note("ar", idx, lambda g: ar_ref(idx).at[pl.ds(0, ND - 1), group(g)], s.ar_s, s.ar_r)
 
@@ -382,8 +382,8 @@
 
     def ag_send(idx, g, buf, slot):
         view = buf.at[slot, group(g)]
-        for i in range(1, NP):
-            remote(view, view, s.ag_s.at[idx, g], s.ag_r.at[idx, g], pipe_peer(i), me_d).start()
+        for i in (3, 1, 2):
+            remote(view, view, s.ag_s.at[idx, g], s.ag_r.at[idx, g], link_peer(i), me_d).start()
         note("ag", idx, lambda g: s.h1.at[0, pl.ds(0, NP - 1), group(g)], s.ag_s, s.ag_r)
 
     def ag_take(idx, g, buf):
@@ -393,8 +393,8 @@
     def rs_send(idx, g, k, partial):
         for j in range(NP):
             s.put[idx, j, group(g)] = partial[:, j * LANES : (j + 1) * LANES].reshape(GM, R, LANES).astype(BF16)
-        for i in range(1, NP):
-            p = pipe_peer(i)
+        for i in (3, 1, 2):
+            p = link_peer(i)
             remote(
                 s.put.at[idx, shard(k, p), group(g)],
                 s.got.at[idx, me_p, group(g)],
@@ -857,7 +857,7 @@
                 s.t1[group(g)] = up
                 back_out(k, 2, g, up)
             if k == 0:
-                pass_two(0)
+                pass_one(0)
             point(k, 1)
 
             @pl.loop(0, G)
@@ -872,6 +872,8 @@
                 up = rs_take(5 - k, g, k) * s.d1[k, group(g)]
                 s.t1[group(g)] = up
                 back_out(k, 1, g, up)
+            if k == 0:
+                pass_two(0)
             point(k, 3)
 
             @pl.loop(0, G)
@@ -899,8 +901,6 @@
 
             if k == 1 or not c.deep:
                 grad_p(k)
-            if k == 1:
-                pass_one(0)
             point(k, 5)
 
         in_copy = pltpu.make_async_copy(s.in_seg, ig_out, s.out_r.at[1])

time: 191 us -> 190 us (level)
  no operation moved by 1% of the time
where the time goes in v6:
time: 190 us
  Pallas kernels  173 us (91%)
  local copies, waits for them, and re-layouts  9.54 us (5%)
  other arithmetic  6.97 us (4%)
    pallas_call x1, Pallas kernels, on_device(): pl.pallas_call(functools.partial(body, c, names), out_shape=(jax.ShapeDty...  173 us
    unnamed x21, local copies, waits for them, and re-layouts  5 us
    broadcast_in_dim x1, other arithmetic, on_device(): gw.astype(F32)[None]  4.37 us

profile of v6, /device:TPU:0, one launch (start us, length us, event | category | flops | bytes accessed | tf_op | source)
XLA Modules:
  0.0 189.9 jit_solution(8495678192756832798)
XLA Ops:
  0.6 0.0 copy-start
  0.6 0.0 copy-start.2
  0.7 1.4 copy-done
  2.1 0.2 constant_dynamic-slice_fusion
  2.2 0.1 copy.27
  2.3 0.8 pad.9.refs_1_
  3.1 0.0 copy-done.2
  3.1 0.9 copy.21
  4.0 0.0 copy-start.6
  4.0 1.4 pad.8.refs_0_
  5.5 0.0 copy-done.6
  5.5 0.1 copy.23
  5.6 0.1 broadcast_in_dim.19
  5.6 0.7 broadcast_in_dim.20.refs_6_
  6.3 172.7 %shard_map.126 = (bf16[4,112,512]{2,1,0:T(8,128)(2,1)}, bf16[4,112,512]{2,1,0:T(8,128)(2,1)}, bf16[2048,512]{1,0:T(8,128)(2,1)}, bf16[4608,256]{1,0:T(8,128)(2,1...) custom-call(bf16[4,112,2048]{2,1,0:T(8,128)(2,1)} %pad.8.refs_0_, bf16[4,112,512]{2,1,0:T(8,128)(2,1)} %pad.9.refs_1_, ...), custom_call_target="tpu_custom_call" | custom-call | tf_op jit(solution)/shard_map/pallas_call | solution.py:997
  179.0 0.7 copy.33
  179.7 0.6 copy_bitcast_fusion.1
  180.3 0.0 copy-start.1
  180.3 4.4 %bitcast_convert_fusion = f32[1,4608,256]{2,1,0:T(8,128)} fusion(bf16[4608,256]{1,0:T(8,128)(2,1)} %get-tuple-element.16), kind=kLoop, calls=%fused_computation | loop fusion | flops 1179648 | bytes 7077888 | tf_op jit(solution)/shard_map/broadcast_in_dim | solution.py:1031
  184.7 0.0 copy-done.1
  184.7 0.0 copy-start.4
  184.7 0.0 copy-start.3
  184.7 2.6 %bitcast_convert_fusion.1 = f32[1,2048,512]{2,1,0:T(8,128)} fusion(bf16[2048,512]{1,0:T(8,128)(2,1)S(1)} %copy-done.1), kind=kLoop, calls=%fused_computation.1 | loop fusion | flops 1048576 | bytes 6291456 | tf_op jit(solution)/shard_map/broadcast_in_dim | solution.py:1030
  187.3 0.0 copy-start.5
  187.3 0.0 copy-done.4
  187.4 1.0 copy.25
  188.3 0.0 copy-done.3
  188.4 1.0 copy.26
  189.3 0.0 copy-done.5
  189.3 0.6 copy.35
  (3 shorter events, 0.1 us)
Async XLA Ops:
  0.6 1.4 copy-start
  0.6 2.5 %copy-start.2 = (bf16[4,98,2048]{2,0,1:T(4,128)(2,1)S(1)}, bf16[4,98,2048]{2,0,1:T(4,128)(2,1)}, u32[]{:S(2)}) copy-start(bf16[4,98,2048]{2,0,1:T(4,128)(2,1)} %param.7) | copy-start | bytes 4816900
  4.0 1.4 copy-start.6
  180.3 4.4 %copy-start.1 = (bf16[2048,512]{1,0:T(8,128)(2,1)S(1)}, bf16[2048,512]{1,0:T(8,128)(2,1)}, u32[]{:S(2)}) copy-start(bf16[2048,512]{1,0:T(8,128)(2,1)} %get-tuple-element.15) | copy-start | bytes 6291460
  184.7 2.6 %copy-start.4 = (bf16[4,112,512]{2,1,0:T(8,128)(2,1)S(1)}, bf16[4,112,512]{2,1,0:T(8,128)(2,1)}, u32[]{:S(2)}) copy-start(bf16[4,112,512]{2,1,0:T(8,128)(2,1)} %get-tuple-element.13) | copy-start | bytes 1376260
  184.7 3.6 %copy-start.3 = (bf16[4,112,512]{2,1,0:T(8,128)(2,1)S(1)}, bf16[4,112,512]{2,1,0:T(8,128)(2,1)}, u32[]{:S(2)}) copy-start(bf16[4,112,512]{2,1,0:T(8,128)(2,1)} %get-tuple-element.14) | copy-start | bytes 1376260
  187.3 2.0 %copy-start.5 = (f32[8,512]{1,0:T(8,128)S(1)}, f32[8,512]{1,0:T(8,128)}, u32[]{:S(2)}) copy-start(f32[8,512]{1,0:T(8,128)} %get-tuple-element.50) | copy-start | bytes 49156

commit v7 on v6

--- a/solution.py
+++ b/solution.py
@@ -215,14 +215,14 @@
     load_w = [
         pltpu.make_async_copy(sw_hbm.at[:, :, pl.ds(h * LANES, LANES)], s.sw.at[h], s.in_r.at[4 + h]) for h in range(2)
     ]
+    for load in reversed(load_w):
+        load.start()
     load_all.start()
 
     @pl.when(me_p == 0)
     def _():
         load_p.start()
 
-    for load in load_w:
-        load.start()
     load_u.start()
     load_g.start()
 

time: 190 us -> 193 us (1.016)
  Pallas kernels: 173 us -> 175 us
    pallas_call x1, Pallas kernels: 173 us -> 175 us  [on_device(): pl.pallas_call(functools.partial(body, c, names), out_shape=(jax.ShapeDty...]
where the time goes in v7:
time: 193 us; the launch traced here: 192 us
  Pallas kernels  175 us (91%)
  local copies, waits for them, and re-layouts  9.54 us (5%)
  other arithmetic  6.97 us (4%)
    pallas_call x1, Pallas kernels, on_device(): pl.pallas_call(functools.partial(body, c, names), out_shape=(jax.ShapeDty...  175 us
    unnamed x21, local copies, waits for them, and re-layouts  5 us
    broadcast_in_dim x1, other arithmetic, on_device(): gw.astype(F32)[None]  4.37 us

profile of v7, /device:TPU:0, one launch (start us, length us, event | category | flops | bytes accessed | tf_op | source)
XLA Modules:
  0.0 192.4 jit_solution(1587081561646811952)
XLA Ops:
  0.6 0.0 copy-start
  0.6 0.0 copy-start.2
  0.7 1.4 copy-done
  2.1 0.2 constant_dynamic-slice_fusion
  2.2 0.1 copy.27
  2.3 0.8 pad.9.refs_1_
  3.1 0.0 copy-done.2
  3.1 0.9 copy.21
  4.0 0.0 copy-start.6
  4.0 1.4 pad.8.refs_0_
  5.5 0.0 copy-done.6
  5.5 0.1 copy.23
  5.6 0.1 broadcast_in_dim.19
  5.6 0.7 broadcast_in_dim.20.refs_6_
  6.3 175.1 %shard_map.126 = (bf16[4,112,512]{2,1,0:T(8,128)(2,1)}, bf16[4,112,512]{2,1,0:T(8,128)(2,1)}, bf16[2048,512]{1,0:T(8,128)(2,1)}, bf16[4608,256]{1,0:T(8,128)(2,1...) custom-call(bf16[4,112,2048]{2,1,0:T(8,128)(2,1)} %pad.8.refs_0_, bf16[4,112,512]{2,1,0:T(8,128)(2,1)} %pad.9.refs_1_, ...), custom_call_target="tpu_custom_call" | custom-call | tf_op jit(solution)/shard_map/pallas_call | solution.py:997
  181.5 0.7 copy.33
  182.2 0.6 copy_bitcast_fusion.1
  182.8 0.0 copy-start.1
  182.8 4.4 %bitcast_convert_fusion = f32[1,4608,256]{2,1,0:T(8,128)} fusion(bf16[4608,256]{1,0:T(8,128)(2,1)} %get-tuple-element.16), kind=kLoop, calls=%fused_computation | loop fusion | flops 1179648 | bytes 7077888 | tf_op jit(solution)/shard_map/broadcast_in_dim | solution.py:1031
  187.2 0.0 copy-done.1
  187.2 0.0 copy-start.4
  187.2 0.0 copy-start.3
  187.2 2.6 %bitcast_convert_fusion.1 = f32[1,2048,512]{2,1,0:T(8,128)} fusion(bf16[2048,512]{1,0:T(8,128)(2,1)S(1)} %copy-done.1), kind=kLoop, calls=%fused_computation.1 | loop fusion | flops 1048576 | bytes 6291456 | tf_op jit(solution)/shard_map/broadcast_in_dim | solution.py:1030
  189.8 0.0 copy-start.5
  189.8 0.0 copy-done.4
  189.8 1.0 copy.25
  190.8 0.0 copy-done.3
  190.8 1.0 copy.26
  191.7 0.0 copy-done.5
  191.8 0.6 copy.35
  (3 shorter events, 0.1 us)
Async XLA Ops:
  0.6 1.4 copy-start
  0.6 2.5 %copy-start.2 = (bf16[4,98,2048]{2,0,1:T(4,128)(2,1)S(1)}, bf16[4,98,2048]{2,0,1:T(4,128)(2,1)}, u32[]{:S(2)}) copy-start(bf16[4,98,2048]{2,0,1:T(4,128)(2,1)} %param.7) | copy-start | bytes 4816900
  4.0 1.4 copy-start.6
  182.8 4.4 %copy-start.1 = (bf16[2048,512]{1,0:T(8,128)(2,1)S(1)}, bf16[2048,512]{1,0:T(8,128)(2,1)}, u32[]{:S(2)}) copy-start(bf16[2048,512]{1,0:T(8,128)(2,1)} %get-tuple-element.15) | copy-start | bytes 6291460
  187.2 2.6 %copy-start.4 = (bf16[4,112,512]{2,1,0:T(8,128)(2,1)S(1)}, bf16[4,112,512]{2,1,0:T(8,128)(2,1)}, u32[]{:S(2)}) copy-start(bf16[4,112,512]{2,1,0:T(8,128)(2,1)} %get-tuple-element.13) | copy-start | bytes 1376260
  187.2 3.6 %copy-start.3 = (bf16[4,112,512]{2,1,0:T(8,128)(2,1)S(1)}, bf16[4,112,512]{2,1,0:T(8,128)(2,1)}, u32[]{:S(2)}) copy-start(bf16[4,112,512]{2,1,0:T(8,128)(2,1)} %get-tuple-element.14) | copy-start | bytes 1376260
  189.8 2.0 %copy-start.5 = (f32[8,512]{1,0:T(8,128)S(1)}, f32[8,512]{1,0:T(8,128)}, u32[]{:S(2)}) copy-start(f32[8,512]{1,0:T(8,128)} %get-tuple-element.50) | copy-start | bytes 49156
